TPU v7x, 512 devices: a whole 4x8x8 slice. The times are simulated.
512 devices in a mesh: tm: 16 (over x, z_lo), clus: 32 (over z_hi, y, core).
Axes of the slice: x: 4, y: 8, z: 8 (z_hi: 2, z_lo: 4; z = z_hi * 4 + z_lo), core: 2. Of those that a mesh axis runs over, the one named last changes fastest.
Arguments:
- currents: bfloat16 [1024, 1024, 128], P('clus', 'tm'), may hold values from -6 to 6
- excitation: bfloat16 [1024, 1024, 128], P('clus', 'tm'), may hold values from -6 to 6
- neighbours: int32 [1024, 30], P('clus'), may hold values from -1 to 1023, as said below
- lag_profile: bfloat16 [30, 64], replicated, may hold values from -0.125 to 0.125
- couplings: bfloat16 [30, 128, 128], replicated, may hold values from -0.5 to 0.5
- block_inverses: bfloat16 [1024, 128, 128], P('clus'), may hold values from -0.5 to 0.5
- charge_map: bfloat16 [128, 128], replicated, may hold values from -0.015625 to 0.015625
- potential: bfloat16 [128, 128], replicated, may hold values from -0.5 to 0.5
Outputs:
- updated: bfloat16 [1024, 1024, 128], P('clus', 'tm')
- residual: float32 [1024, 1024, 128], P('clus', 'tm')
Inputs may be any that keep to these rules, and one draw needn't show every extreme that they name: `neighbours`: row j lists distinct panel clusters from j // 32 * 32 - 32 to j // 32 * 32 + 2 * 32 - 1, modulo 1024; entries -1 pad the end of a row, and every row has a cluster in its first slot.
All inputs are finite; a program needn't handle non-finite values.
Results may differ from a plain program's by a relative error of at most 0.0051.
Values may be sent and summed in bfloat16 or wider, within the bound.
No kernel may reach another device: no remote copies, remote signals or barrier semaphores. Data moves between devices by JAX's collectives and lax.ppermute only.
A program may use at most 64 MiB of HBM per device.

v0:
```python
import math

import jax
import jax.numpy as jnp
from jax import lax
from jax.sharding import PartitionSpec as P


def from_behind(x, axis, by):
    peers = lax.axis_size(axis)
    pairs = [(i, i + by) for i in range(peers) if 0 <= i + by < peers]
    return lax.ppermute(x, axis, pairs)


def with_halo(x, sides, width):
    for axis, dim in sides:
        peers, length = (lax.axis_size(axis), x.shape[dim])
        up = [(i, (i + 1) % peers) for i in range(peers)]
        down = [(j, i) for i, j in up]
        last = lax.slice_in_dim(x, length - width, length, axis=dim)
        first = lax.slice_in_dim(x, 0, width, axis=dim)
        before = lax.ppermute(last, axis, up)
        after = lax.ppermute(first, axis, down)
        x = jnp.concatenate([before, x, after], axis=dim)
    return x


def entering(value, axis, join, neutral):
    count, mine = (lax.axis_size(axis), lax.axis_index(axis))
    pieces = lax.all_gather(value, axis)
    so_far = jnp.full_like(value, 0) + jnp.asarray(neutral, value.dtype)

    def lap(position, so_far):
        longer = join(so_far, pieces[position])
        return jnp.where(position < mine, longer, so_far)

    return lax.fori_loop(0, count - 1, lap, so_far)


def add_terms(earlier, later):
    return earlier + later


def on_device(
    currents, excitation, neighbours, lag_profile, couplings, block_inverses, charge_map, potential
):
    per_dev, steps_block, unknowns = currents.shape
    slot_count, lag_count = lag_profile.shape
    window = steps_block + lag_count
    cluster_total = per_dev * lax.axis_size("clus")
    previous = from_behind(currents, "tm", 1)
    joined = jnp.concatenate([previous, currents], axis=1)
    extended = with_halo(joined, (("clus", 0),), per_dev)
    first_local = (lax.axis_index("clus") - 1) * per_dev
    present = neighbours >= 0
    local_ids = jnp.where(present, (neighbours - first_local) % cluster_total, 0)
    present_f = present.astype(jnp.float32)
    lag_index = jnp.arange(steps_block)[:, None] + lag_count - jnp.arange(window)[None, :]
    lag_onehot = (lag_index[:, :, None] == jnp.arange(lag_count)[None, None, :]).astype(
        jnp.bfloat16
    )
    toeplitz = jnp.einsum(
        "kl,tsl->kts", lag_profile, lag_onehot, preferred_element_type=jnp.float32
    ).astype(jnp.bfloat16)
    per_group = math.gcd(slot_count, 6)
    group_count = slot_count // per_group
    slot_ids = local_ids.T.reshape(group_count, per_group, per_dev)
    slot_mask = present_f.T.reshape(group_count, per_group, per_dev)
    slot_toep = toeplitz.reshape(group_count, per_group, steps_block, window)
    slot_coup = couplings.reshape(group_count, per_group, unknowns, unknowns)

    def add_group(accum, pieces):
        group_ids, group_mask, group_toep, group_coup = pieces
        gathered = jnp.take(extended, group_ids, axis=0)
        filtered = jnp.einsum(
            "kts,kcsb->kctb", group_toep, gathered, preferred_element_type=jnp.float32
        )
        filtered = (filtered * group_mask[:, :, None, None]).astype(jnp.bfloat16)
        return (
            accum
            + jnp.einsum("kctb,kbd->ctd", filtered, group_coup, preferred_element_type=jnp.float32),
            None,
        )

    start_field = jnp.zeros((per_dev, steps_block, unknowns), jnp.float32)
    near_field, _ = lax.scan(add_group, start_field, (slot_ids, slot_mask, slot_toep, slot_coup))
    increments = jnp.dot(
        currents.reshape(-1, unknowns), charge_map, preferred_element_type=jnp.float32
    )
    increments = increments.reshape(per_dev, steps_block, -1)
    totals = jnp.sum(increments, axis=1)
    before = entering(totals, "tm", add_terms, jnp.zeros_like(totals))
    lower_ones = (jnp.arange(steps_block)[:, None] >= jnp.arange(steps_block)[None, :]).astype(
        jnp.float32
    )
    running = jnp.einsum("ts,csm->ctm", lower_ones, increments, precision=lax.Precision.HIGHEST)
    charge = (before[:, None, :] + running).astype(jnp.bfloat16)
    charge_field = jnp.dot(
        charge.reshape(per_dev * steps_block, -1), potential, preferred_element_type=jnp.float32
    )
    charge_field = charge_field.reshape(per_dev, steps_block, unknowns)
    residual = excitation.astype(jnp.float32) - near_field - charge_field
    correction = jnp.einsum(
        "ctb,cbd->ctd",
        residual.astype(jnp.bfloat16),
        block_inverses,
        preferred_element_type=jnp.float32,
    )
    updated = (currents.astype(jnp.float32) + correction).astype(jnp.bfloat16)
    return (updated, residual)


def solution(mesh):
    in_specs = (
        P("clus", "tm", None),
        P("clus", "tm", None),
        P("clus", None),
        P(),
        P(),
        P("clus", None, None),
        P(),
        P(),
    )
    out_specs = (P("clus", "tm", None), P("clus", "tm", None))
    return jax.shard_map(
        on_device, mesh=mesh, in_specs=in_specs, out_specs=out_specs, check_vma=False
    )
```

profile of v0, /device:TPU:57, one launch (start us, length us, event | category | flops | bytes accessed | tf_op | source)
XLA Modules:
  0.0 184.2 jit_solution(9128017647233922127)
XLA Ops:
  0.7 4.2 %collective-permute-start = (bf16[32,64,128]{2,1,0:T(8,128)(2,1)}, bf16[32,64,128]{2,1,0:T(8,128)(2,1)S(1)}, u32[]{:S(2)}, u32[]{:S(2)}) collective-permute-start(bf16[32,64,128]{2,1,0:T(8,128)(2,1)} %param.12), channel_id=1, source_target_pairs={{0,32},{32,64},{64,96},{96,128},{128,160},{160,192},{192,224},{224... | collective-permute-start | bytes 1572872 | tf_op jit(solution)/shard_map/ppermute | solution.py:12
  4.8 1.3 fusion.46
  6.2 42.6 %all-gather = f32[512,128]{1,0:T(8,128)S(1)} all-gather(f32[32,128]{1,0:T(8,128)S(1)} %get-tuple-element.195), channel_id=2, replica_groups=mesh['tm'=16,'clus'=32] {'tm'}, dimensions={0}, use_global_device_ids=true | all-gather | bytes 278528 | tf_op jit(solution)/shard_map/all_gather | solution.py:30
  50.3 1.9 %constant_dynamic-update-slice_fusion = bf16[32,128,128]{2,1,0:T(8,128)(2,1)} fusion(bf16[32,128,128]{2,1,0:T(8,128)(2,1)} %constant_dynamic-update-slice_fusion.1, bf16[32,64,128]{2,1,0:T(8,128)(2,1)} %param.12), kind=kLoop, calls=%fused_computation.50 | loop fusion | bytes 1048576 | tf_op jit(solution)/shard_map/concatenate | solution.py:52
  52.3 14.6 %collective-permute-start.1 = (bf16[32,128,128]{2,1,0:T(8,128)(2,1)}, bf16[32,128,128]{2,1,0:T(8,128)(2,1)S(1)}, u32[]{:S(2)}, u32[]{:S(2)}) collective-permute-start(bf16[32,128,128]{2,1,0:T(8,128)(2,1)} %constant_dynamic-update-slice_fusion), channel_id=1, source_target_pairs={{0,1},{1,2},{2,3},{3,4},{4,5},{5,6},{6,7},{7,8},{8,9},{9,10},{10,1... | collective-permute-start | bytes 3145736 | tf_op jit(solution)/shard_map/ppermute | solution.py:22
  66.9 1.9 %collective-permute-start.2 = (bf16[32,128,128]{2,1,0:T(8,128)(2,1)}, bf16[32,128,128]{2,1,0:T(8,128)(2,1)}, u32[]{:S(2)}, u32[]{:S(2)}) collective-permute-start(bf16[32,128,128]{2,1,0:T(8,128)(2,1)} %constant_dynamic-update-slice_fusion), channel_id=1, source_target_pairs={{1,0},{2,1},{3,2},{4,3},{5,4},{6,5},{7,6},{8,7},{9,8},{10,9},{11,1... | collective-permute-start | bytes 3145736 | tf_op jit(solution)/shard_map/ppermute | solution.py:23
  69.6 1.2 fusion.32
  70.8 1.0 copy.13
  73.6 14.0 %collective-permute-done.1 = bf16[32,128,128]{2,1,0:T(8,128)(2,1)S(1)} collective-permute-done((bf16[32,128,128]{2,1,0:T(8,128)(2,1)}, bf16[32,128,128]{2,1,0:T(8,128)(2,1)S(1)}, u32[]{:S(2)}, u32[]{:S(2)}) %collective-permute-start.1) | collective-permute-done | bytes 1048608 | tf_op jit(solution)/shard_map/ppermute | solution.py:22
  87.6 10.6 %collective-permute-done.2 = bf16[32,128,128]{2,1,0:T(8,128)(2,1)} collective-permute-done((bf16[32,128,128]{2,1,0:T(8,128)(2,1)}, bf16[32,128,128]{2,1,0:T(8,128)(2,1)}, u32[]{:S(2)}, u32[]{:S(2)}) %collective-permute-start.2) | collective-permute-done | bytes 1048608 | tf_op jit(solution)/shard_map/ppermute | solution.py:23
  98.2 3.1 %pad_maximum_fusion = bf16[96,128,128]{2,1,0:T(8,128)(2,1)} fusion(bf16[32,128,128]{2,1,0:T(8,128)(2,1)} %collective-permute-done.2, bf16[32,128,128]{2,1,0:T(8,128)(2,1)} %constant_dynamic-update-slice_fusion, bf16[32,128,128]{2,1,0:T(8,128)(2,1)S(1)} %collective-permute-done.1), kind=kLoop, calls=%fused_computation.21 | loop fusion | flops 3145728 | bytes 6291456 | tf_op jit(solution)/shard_map/concatenate | solution.py:24
  101.3 80.1 %while.25 = (s32[]{:T(128)}, f32[32,64,128]{2,1,0:T(8,128)}, s32[5,6,32]{2,1,0:T(8,128)S(1)}, bf16[96,128,128]{2,1,0:T(8,128)(2,1)}, bf16[5,6,64,128]{3,2,1,0:T(...) while((s32[]{:T(128)}, f32[32,64,128]{2,1,0:T(8,128)}, ...), condition=%wide.region_1.2_spmd.clone, body=%wide.region_0.1_spmd.clone.sunk | while | flops 812124864 | bytes 21281268 | solution.py:86
  101.4 10.0 %gather_fusion = bf16[192,128,128]{2,1,0:T(8,128)(2,1)} fusion(bf16[96,128,128]{2,1,0:T(8,128)(2,1)} %get-tuple-element.304, s32[1024]{0:T(1024)S(1)} %pad_clamp_fusion.2), kind=kCustom, calls=%fused_computation.clone.clone.1 | custom fusion | bytes 12583680 | tf_op jit(solution)/shard_map/while/body/eval_jaxpr/jit(_take)/gather | solution.py:74
  111.5 5.7 %fusion.60 = f32[32,64,128]{2,1,0:T(8,128)} fusion(f32[6,32]{0,1:T(8,128)S(1)} %bitcast.83, f32[32,64,128]{2,1,0:T(8,128)} %get-tuple-element.293, pred[]{:T(512)S(6)} %compare.7, bf16[5,6,128,128]{3,2,1,0:T(8,128)(2,1)} %get-tuple-element.307, s32[]{:T(128)} %get-tuple-element.292, bf16[5,6,64,128]{3,2,1,0:T(8,128)(2,1)} %get-tuple-element.305, ...), kind=kOutput, calls=%fused_computation.9.clone.1 | convolution fusion | flops 812122112 | bytes 8685505 | tf_op jit(solution)/shard_map/while/body/eval_jaxpr/kctb,kbd->ctd/dot_general | solution.py:81
  117.4 10.0 %gather_fusion = bf16[192,128,128]{2,1,0:T(8,128)(2,1)} fusion(bf16[96,128,128]{2,1,0:T(8,128)(2,1)} %get-tuple-element.304, s32[1024]{0:T(1024)S(1)} %pad_clamp_fusion.2), kind=kCustom, calls=%fused_computation.clone.clone.1 | custom fusion | bytes 12583680 | tf_op jit(solution)/shard_map/while/body/eval_jaxpr/jit(_take)/gather | solution.py:74
  127.4 5.9 %fusion.60 = f32[32,64,128]{2,1,0:T(8,128)} fusion(f32[6,32]{0,1:T(8,128)S(1)} %bitcast.83, f32[32,64,128]{2,1,0:T(8,128)} %get-tuple-element.293, pred[]{:T(512)S(6)} %compare.7, bf16[5,6,128,128]{3,2,1,0:T(8,128)(2,1)} %get-tuple-element.307, s32[]{:T(128)} %get-tuple-element.292, bf16[5,6,64,128]{3,2,1,0:T(8,128)(2,1)} %get-tuple-element.305, ...), kind=kOutput, calls=%fused_computation.9.clone.1 | convolution fusion | flops 812122112 | bytes 8685505 | tf_op jit(solution)/shard_map/while/body/eval_jaxpr/kctb,kbd->ctd/dot_general | solution.py:81
  133.4 10.0 %gather_fusion = bf16[192,128,128]{2,1,0:T(8,128)(2,1)} fusion(bf16[96,128,128]{2,1,0:T(8,128)(2,1)} %get-tuple-element.304, s32[1024]{0:T(1024)S(1)} %pad_clamp_fusion.2), kind=kCustom, calls=%fused_computation.clone.clone.1 | custom fusion | bytes 12583680 | tf_op jit(solution)/shard_map/while/body/eval_jaxpr/jit(_take)/gather | solution.py:74
  143.5 5.9 %fusion.60 = f32[32,64,128]{2,1,0:T(8,128)} fusion(f32[6,32]{0,1:T(8,128)S(1)} %bitcast.83, f32[32,64,128]{2,1,0:T(8,128)} %get-tuple-element.293, pred[]{:T(512)S(6)} %compare.7, bf16[5,6,128,128]{3,2,1,0:T(8,128)(2,1)} %get-tuple-element.307, s32[]{:T(128)} %get-tuple-element.292, bf16[5,6,64,128]{3,2,1,0:T(8,128)(2,1)} %get-tuple-element.305, ...), kind=kOutput, calls=%fused_computation.9.clone.1 | convolution fusion | flops 812122112 | bytes 8685505 | tf_op jit(solution)/shard_map/while/body/eval_jaxpr/kctb,kbd->ctd/dot_general | solution.py:81
  149.5 10.0 %gather_fusion = bf16[192,128,128]{2,1,0:T(8,128)(2,1)} fusion(bf16[96,128,128]{2,1,0:T(8,128)(2,1)} %get-tuple-element.304, s32[1024]{0:T(1024)S(1)} %pad_clamp_fusion.2), kind=kCustom, calls=%fused_computation.clone.clone.1 | custom fusion | bytes 12583680 | tf_op jit(solution)/shard_map/while/body/eval_jaxpr/jit(_take)/gather | solution.py:74
  159.5 5.9 %fusion.60 = f32[32,64,128]{2,1,0:T(8,128)} fusion(f32[6,32]{0,1:T(8,128)S(1)} %bitcast.83, f32[32,64,128]{2,1,0:T(8,128)} %get-tuple-element.293, pred[]{:T(512)S(6)} %compare.7, bf16[5,6,128,128]{3,2,1,0:T(8,128)(2,1)} %get-tuple-element.307, s32[]{:T(128)} %get-tuple-element.292, bf16[5,6,64,128]{3,2,1,0:T(8,128)(2,1)} %get-tuple-element.305, ...), kind=kOutput, calls=%fused_computation.9.clone.1 | convolution fusion | flops 812122112 | bytes 8685505 | tf_op jit(solution)/shard_map/while/body/eval_jaxpr/kctb,kbd->ctd/dot_general | solution.py:81
  165.5 9.9 %gather_fusion = bf16[192,128,128]{2,1,0:T(8,128)(2,1)} fusion(bf16[96,128,128]{2,1,0:T(8,128)(2,1)} %get-tuple-element.304, s32[1024]{0:T(1024)S(1)} %pad_clamp_fusion.2), kind=kCustom, calls=%fused_computation.clone.clone.1 | custom fusion | bytes 12583680 | tf_op jit(solution)/shard_map/while/body/eval_jaxpr/jit(_take)/gather | solution.py:74
  175.5 5.9 %fusion.60 = f32[32,64,128]{2,1,0:T(8,128)} fusion(f32[6,32]{0,1:T(8,128)S(1)} %bitcast.83, f32[32,64,128]{2,1,0:T(8,128)} %get-tuple-element.293, pred[]{:T(512)S(6)} %compare.7, bf16[5,6,128,128]{3,2,1,0:T(8,128)(2,1)} %get-tuple-element.307, s32[]{:T(128)} %get-tuple-element.292, bf16[5,6,64,128]{3,2,1,0:T(8,128)(2,1)} %get-tuple-element.305, ...), kind=kOutput, calls=%fused_computation.9.clone.1 | convolution fusion | flops 812122112 | bytes 8685505 | tf_op jit(solution)/shard_map/while/body/eval_jaxpr/kctb,kbd->ctd/dot_general | solution.py:81
  181.4 1.5 subtract_subtract_fusion
  182.9 1.2 fusion.29
  (70 shorter events, 5.3 us)
Async XLA Ops:
  0.6 182.3 %copy-start = (bf16[32,128,128]{2,1,0:T(8,128)(2,1)S(1)}, bf16[32,128,128]{2,1,0:T(8,128)(2,1)}, u32[]{:S(2)}) copy-start(bf16[32,128,128]{2,1,0:T(8,128)(2,1)} %param.17) | copy-start | bytes 3145732
  0.6 72.7 %copy-start.4 = (bf16[128,128]{1,0:T(8,128)(2,1)S(1)}, bf16[128,128]{1,0:T(8,128)(2,1)}, u32[]{:S(2)}) copy-start(bf16[128,128]{1,0:T(8,128)(2,1)} %param.19) | copy-start | bytes 98308
  0.7 48.8 %collective-permute-start = (bf16[32,64,128]{2,1,0:T(8,128)(2,1)}, bf16[32,64,128]{2,1,0:T(8,128)(2,1)S(1)}, u32[]{:S(2)}, u32[]{:S(2)}) collective-permute-start(bf16[32,64,128]{2,1,0:T(8,128)(2,1)} %param.12), channel_id=1, source_target_pairs={{0,32},{32,64},{64,96},{96,128},{128,160},{160,192},{192,224},{224... | collective-permute-start | bytes 1572872 | tf_op jit(solution)/shard_map/ppermute | solution.py:12
  52.3 35.3 %collective-permute-start.1 = (bf16[32,128,128]{2,1,0:T(8,128)(2,1)}, bf16[32,128,128]{2,1,0:T(8,128)(2,1)S(1)}, u32[]{:S(2)}, u32[]{:S(2)}) collective-permute-start(bf16[32,128,128]{2,1,0:T(8,128)(2,1)} %constant_dynamic-update-slice_fusion), channel_id=1, source_target_pairs={{0,1},{1,2},{2,3},{3,4},{4,5},{5,6},{6,7},{7,8},{8,9},{9,10},{10,1... | collective-permute-start | bytes 3145736 | tf_op jit(solution)/shard_map/ppermute | solution.py:22
  66.9 31.4 %collective-permute-start.2 = (bf16[32,128,128]{2,1,0:T(8,128)(2,1)}, bf16[32,128,128]{2,1,0:T(8,128)(2,1)}, u32[]{:S(2)}, u32[]{:S(2)}) collective-permute-start(bf16[32,128,128]{2,1,0:T(8,128)(2,1)} %constant_dynamic-update-slice_fusion), channel_id=1, source_target_pairs={{1,0},{2,1},{3,2},{4,3},{5,4},{6,5},{7,6},{8,7},{9,8},{10,9},{11,1... | collective-permute-start | bytes 3145736 | tf_op jit(solution)/shard_map/ppermute | solution.py:23
  101.3 80.1 %copy-start.3 = (bf16[32,64,128]{2,1,0:T(8,128)(2,1)S(1)}, bf16[32,64,128]{2,1,0:T(8,128)(2,1)}, u32[]{:S(2)}) copy-start(bf16[32,64,128]{2,1,0:T(8,128)(2,1)} %param.13) | copy-start | bytes 1572868
  101.3 81.6 %copy-start.1 = (bf16[32,64,128]{2,1,0:T(8,128)(2,1)S(1)}, bf16[32,64,128]{2,1,0:T(8,128)(2,1)}, u32[]{:S(2)}) copy-start(bf16[32,64,128]{2,1,0:T(8,128)(2,1)} %param.12) | copy-start | bytes 1572868
  182.9 1.2 copy-start.2
where the time goes:
time: 185 us; the launch traced here: 184 us
  local copies, waits for them, and re-layouts  54.7 us (30%)
  blocking collectives  42.6 us (23%)
  matrix products  34.1 us (18%)
  waiting for transfers between devices  24.6 us (13%)
  starting transfers between devices  20.7 us (11%)
  other arithmetic  6.31 us (3%)
    gather x5, local copies, waits for them, and re-layouts, add_group(): gathered = jnp.take(extended, group_ids, axis=0)  49.8 us
    all_gather x1, blocking collectives, entering(): pieces = lax.all_gather(value, axis)  42.6 us
    dot_general x5, matrix products, add_group(): jnp.einsum('kctb,kbd->ctd', filtered, group_coup, preferred_element_type=...  29.4 us
    ppermute x1, starting transfers between devices, with_halo(): before = lax.ppermute(last, axis, up)  14.6 us
    ppermute x1, waiting for transfers between devices, with_halo(): before = lax.ppermute(last, axis, up)  14 us
    ppermute x1, waiting for transfers between devices, with_halo(): after = lax.ppermute(first, axis, down)  10.6 us
    ppermute x1, starting transfers between devices, from_behind(): return lax.ppermute(x, axis, pairs)  4.16 us
  transfers between devices with their start and end apart: 3, of which 2 were waited for; matrix products, arithmetic and copies ran while one was open for 3% of the time, Pallas kernels for 0%

commit v1 on v0

v1 whole, which is shorter than its diff:
```python
import jax
import jax.numpy as jnp
from jax import lax
from jax.experimental import pallas as pl
from jax.experimental.pallas import tpu as pltpu
from jax.sharding import PartitionSpec as P

F32, BF16 = jnp.float32, jnp.bfloat16
MIB = 1 << 20


def whole(space=pltpu.VMEM):
    return pl.BlockSpec(memory_space=space)


def dot(a, b):
    return jnp.dot(a, b, preferred_element_type=F32)


def charge_kernel(cur_ref, map_ref, running_ref, totals_ref):
    per_dev, steps, unknowns = cur_ref.shape
    row = lax.broadcasted_iota(jnp.int32, (steps, 2 * steps), 0)
    col = lax.broadcasted_iota(jnp.int32, (steps, 2 * steps), 1)
    lower = (row >= col % steps).astype(F32).astype(BF16)
    group = 8

    @pl.loop(0, per_dev // group)
    def _(g):
        first = g * group
        rows = cur_ref[pl.ds(first, group)].reshape(group * steps, unknowns)
        inc = dot(rows, map_ref[...])
        high = inc.astype(BF16)
        low = (inc - high.astype(F32)).astype(BF16)
        last = []
        for i in range(group):
            cut = slice(i * steps, (i + 1) * steps)
            run = dot(lower, jnp.concatenate([high[cut], low[cut]], axis=0))
            running_ref[first + i] = run
            last.append(run[steps - 1 : steps])
        totals_ref[pl.ds(first, group)] = jnp.concatenate(last, axis=0)


def near_kernel(
    ids_ref, edge_ref, lag_ref, coup_ref, own_ref, up_ref, down_ref, wrap_ref,
    head_ref, tail_ref, field, blocks, toep, terms, sems,
):
    per_dev, steps, unknowns = own_ref.shape
    slots = coup_ref.shape[0]
    group = 8

    own_copy = pltpu.make_async_copy(own_ref, field.at[pl.ds(per_dev, per_dev)], sems.at[0])
    own_copy.start()

    def fetch(ref, start, sem):
        return pltpu.make_async_copy(ref, field.at[pl.ds(start, per_dev)], sem)

    low_edge, high_edge = edge_ref[0] > 0, edge_ref[1] > 0

    @pl.when(low_edge)
    def _():
        fetch(wrap_ref, 0, sems.at[1]).start()

    @pl.when(jnp.logical_not(low_edge))
    def _():
        fetch(up_ref, 0, sems.at[1]).start()

    @pl.when(high_edge)
    def _():
        fetch(wrap_ref, 2 * per_dev, sems.at[2]).start()

    @pl.when(jnp.logical_not(high_edge))
    def _():
        fetch(down_ref, 2 * per_dev, sems.at[2]).start()

    field[3 * per_dev] = jnp.zeros((steps, unknowns), BF16)
    lane = lax.broadcasted_iota(jnp.int32, (2 * steps, 2 * steps), 1)
    for p in range(slots // 2):
        square = jnp.zeros((unknowns, unknowns), BF16)
        blocks[p, :unknowns, :unknowns] = coup_ref[2 * p]
        blocks[p, :unknowns, unknowns:] = square
        blocks[p, unknowns:, :unknowns] = square
        blocks[p, unknowns:, unknowns:] = coup_ref[2 * p + 1]
        even = jnp.broadcast_to(lag_ref[2 * p : 2 * p + 1, :], lane.shape)
        odd = jnp.broadcast_to(lag_ref[2 * p + 1 : 2 * p + 2, :], lane.shape)
        even = pltpu.roll(even, 0, 1, stride=1, stride_axis=0)
        odd = pltpu.roll(odd, steps, 1, stride=1, stride_axis=0)
        both = jnp.where(lane < steps, even, odd)
        toep[:, p * 2 * steps : (p + 1) * 2 * steps] = both.astype(BF16)
    own_copy.wait()
    fetch(up_ref, 0, sems.at[1]).wait()
    fetch(down_ref, 2 * per_dev, sems.at[2]).wait()

    @pl.loop(0, per_dev // group)
    def _(g):
        first = g * group
        for p in range(slots // 2):
            rows = [
                jnp.concatenate(
                    [
                        field[ids_ref[first + i, 2 * p]],
                        field[ids_ref[first + i, 2 * p + 1]],
                    ],
                    axis=1,
                )
                for i in range(group)
            ]
            z = dot(jnp.concatenate(rows, axis=0), blocks[p]).astype(BF16)
            for i in range(group):
                cut = slice(i * steps, (i + 1) * steps)
                lanes = slice((i % 2) * unknowns, (i % 2 + 1) * unknowns)
                for h in range(2):
                    at = (2 * p + h) * steps
                    terms[i // 2, at : at + steps, lanes] = z[cut, h * unknowns : (h + 1) * unknowns]
        for i in range(0, group, 2):
            out = dot(toep[...], terms[i // 2])
            for j in range(2):
                lanes = slice(j * unknowns, (j + 1) * unknowns)
                head_ref[first + i + j] = out[:steps, lanes]
                tail_ref[first + i + j] = out[steps:, lanes].astype(BF16)


def base_kernel(exc_ref, head_ref, running_ref, before_ref, pot_ref, base_ref):
    per_dev, steps, unknowns = exc_ref.shape
    group = 8

    @pl.loop(0, per_dev // group)
    def _(g):
        at = pl.ds(g * group, group)
        charge = (running_ref[at] + before_ref[at][:, None, :]).astype(BF16)
        field = dot(charge.reshape(group * steps, -1), pot_ref[...])
        field = field.reshape(group, steps, unknowns)
        base_ref[at] = exc_ref[at].astype(F32) - head_ref[at] - field


def final_kernel(cur_ref, base_ref, tail_ref, inv_ref, updated_ref, residual_ref):
    for i in range(cur_ref.shape[0]):
        residual = base_ref[i] - tail_ref[i].astype(F32)
        residual_ref[i] = residual
        correction = dot(residual.astype(BF16), inv_ref[i])
        updated_ref[i] = (cur_ref[i].astype(F32) + correction).astype(BF16)


def on_device(
    currents, excitation, neighbours, lag_profile, couplings, block_inverses, charge_map, potential
):
    per_dev, steps, unknowns = currents.shape
    slots, lags = lag_profile.shape
    blocks_tm, peers = lax.axis_size("tm"), lax.axis_size("clus")
    total = per_dev * peers
    half = peers // 2
    me = lax.axis_index("clus")

    def send(x, where):
        pairs = [
            (t * peers + c, u * peers + d)
            for t in range(blocks_tm)
            for c in range(peers)
            for u, d in [where(t, c)]
            if 0 <= u < blocks_tm and 0 <= d < peers
        ]
        return lax.ppermute(x, ("tm", "clus"), pairs)

    def edge(t, c):
        if c % half == half - 1:
            return t, (c + 1) % peers
        return t, ((c - 1) % peers if c % half == 0 else -1)

    wrapped = send(currents, edge)
    up = send(currents, lambda t, c: (t, c + 1 if c % half != half - 1 else -1))
    down = send(currents, lambda t, c: (t, c - 1 if c % half != 0 else -1))

    shape3 = (per_dev, steps, unknowns)
    params = lambda mib: pltpu.CompilerParams(vmem_limit_bytes=mib * MIB)
    running, totals = pl.pallas_call(
        charge_kernel,
        name="charge",
        out_shape=(
            jax.ShapeDtypeStruct(shape3, F32),
            jax.ShapeDtypeStruct((per_dev, unknowns), F32),
        ),
        in_specs=[whole()] * 2,
        out_specs=(whole(), whole()),
        compiler_params=params(32),
    )(currents, charge_map)

    def behind(x, by):
        return send(x, lambda t, c: (t + by, c))

    window = totals
    for j in (1, 2, 3):
        window = window + behind(totals, j)
    before = behind(window, 1)
    for j in (5, 9, 13):
        before = before + behind(window, j)

    first_local = (me - 1) * per_dev
    local_ids = jnp.where(neighbours >= 0, (neighbours - first_local) % total, 3 * per_dev)
    edges = jnp.stack([me % half == 0, me % half == half - 1]).astype(jnp.int32)
    lag_rows = jnp.pad(lag_profile.astype(F32), ((0, 0), (0, 2 * steps - lags)))
    lag_rows = jnp.roll(lag_rows[:, ::-1], 1, axis=1)
    head, tail = pl.pallas_call(
        near_kernel,
        name="near",
        out_shape=(
            jax.ShapeDtypeStruct(shape3, F32),
            jax.ShapeDtypeStruct(shape3, BF16),
        ),
        in_specs=[whole(pltpu.SMEM)] * 2 + [whole()] * 2 + [whole(pl.ANY)] * 4,
        out_specs=(whole(), whole()),
        scratch_shapes=[
            pltpu.VMEM((3 * per_dev + 1, steps, unknowns), BF16),
            pltpu.VMEM((slots // 2, 2 * unknowns, 2 * unknowns), BF16),
            pltpu.VMEM((2 * steps, slots * steps), BF16),
            pltpu.VMEM((4, slots * steps, 2 * unknowns), BF16),
            pltpu.SemaphoreType.DMA((3,)),
        ],
        compiler_params=params(40),
    )(local_ids, edges, lag_rows, couplings, currents, up, down, wrapped)

    tail_before = behind(tail, 1)
    base = pl.pallas_call(
        base_kernel,
        name="base",
        out_shape=jax.ShapeDtypeStruct(shape3, F32),
        in_specs=[whole()] * 5,
        out_specs=whole(),
        compiler_params=params(32),
    )(excitation, head, running, before, potential)
    return pl.pallas_call(
        final_kernel,
        name="final",
        out_shape=(
            jax.ShapeDtypeStruct(shape3, BF16),
            jax.ShapeDtypeStruct(shape3, F32),
        ),
        in_specs=[whole()] * 4,
        out_specs=(whole(), whole()),
        compiler_params=params(32),
    )(currents, base, tail_before, block_inverses)


def solution(mesh):
    in_specs = (
        P("clus", "tm", None),
        P("clus", "tm", None),
        P("clus", None),
        P(),
        P(),
        P("clus", None, None),
        P(),
        P(),
    )
    out_specs = (P("clus", "tm", None), P("clus", "tm", None))
    return jax.shard_map(
        on_device, mesh=mesh, in_specs=in_specs, out_specs=out_specs, check_vma=False
    )
```

time: 185 us -> 74.7 us (0.40)
  the two profiles are of different devices: /device:TPU:57 before, /device:TPU:2 now
where the time goes in v1:
time: 74.7 us; the launch traced here: 74.1 us
  starting transfers between devices  38.2 us (51%)
  waiting for transfers between devices  18.7 us (25%)
  Pallas kernels  11.9 us (16%)
  local copies, waits for them, and re-layouts  4.23 us (6%)
  between operations  0.86 us (1%)
    ppermute x11, starting transfers between devices, send(): return lax.ppermute(x, ('tm', 'clus'), pairs)  38.2 us
    ppermute x11, waiting for transfers between devices, send(): return lax.ppermute(x, ('tm', 'clus'), pairs)  18.7 us
    pallas_call x1, Pallas kernels, on_device(): pl.pallas_call(near_kernel, name='near', out_shape=(jax.ShapeDtypeStruct(...  8.44 us
    unnamed x16, local copies, waits for them, and re-layouts  4.08 us
  transfers between devices with their start and end apart: 11, of which 4 were waited for; matrix products, arithmetic and copies ran while one was open for 0% of the time, Pallas kernels for 3%

profile of v1, /device:TPU:2, one launch (start us, length us, event | category | flops | bytes accessed | tf_op | source)
XLA Modules:
  0.0 74.1 jit_solution(6846577386222286470)
XLA Ops:
  0.6 13.3 %collective-permute-start.2 = (bf16[32,64,128]{2,1,0:T(8,128)(2,1)}, bf16[32,64,128]{2,1,0:T(8,128)(2,1)S(1)}, u32[]{:S(2)}, u32[]{:S(2)}) collective-permute-start(bf16[32,64,128]{2,1,0:T(8,128)(2,1)} %cur_ref.3), channel_id=1, source_target_pairs={{0,31},{15,16},{16,15},{31,0},{32,63},{47,48},{48,47},{63,32},{64,... | collective-permute-start | bytes 1572872 | tf_op jit(solution)/shard_map/ppermute | solution.py:161
  13.9 1.3 %collective-permute-start.1 = (bf16[32,64,128]{2,1,0:T(8,128)(2,1)}, bf16[32,64,128]{2,1,0:T(8,128)(2,1)S(1)}, u32[]{:S(2)}, u32[]{:S(2)}) collective-permute-start(bf16[32,64,128]{2,1,0:T(8,128)(2,1)} %cur_ref.3), channel_id=1, source_target_pairs={{1,0},{2,1},{3,2},{4,3},{5,4},{6,5},{7,6},{8,7},{9,8},{10,9},{11,1... | collective-permute-start | bytes 1572872 | tf_op jit(solution)/shard_map/ppermute | solution.py:161
  15.2 3.1 %collective-permute-start = (bf16[32,64,128]{2,1,0:T(8,128)(2,1)}, bf16[32,64,128]{2,1,0:T(8,128)(2,1)S(1)}, u32[]{:S(2)}, u32[]{:S(2)}) collective-permute-start(bf16[32,64,128]{2,1,0:T(8,128)(2,1)} %cur_ref.3), channel_id=1, source_target_pairs={{0,1},{1,2},{2,3},{3,4},{4,5},{5,6},{6,7},{7,8},{8,9},{9,10},{10,1... | collective-permute-start | bytes 1572872 | tf_op jit(solution)/shard_map/ppermute | solution.py:161
  18.3 0.7 copy-done.6
  19.3 0.6 copy-done.7
  20.0 6.6 %collective-permute-done.2.wrap_ref = bf16[32,64,128]{2,1,0:T(8,128)(2,1)S(1)} collective-permute-done((bf16[32,64,128]{2,1,0:T(8,128)(2,1)}, bf16[32,64,128]{2,1,0:T(8,128)(2,1)S(1)}, u32[]{:S(2)}, u32[]{:S(2)}) %collective-permute-start.2) | collective-permute-done | bytes 524320 | tf_op jit(solution)/shard_map/ppermute | solution.py:161
  26.5 1.0 %copy-done = bf16[32,64,128]{2,1,0:T(8,128)(2,1)S(1)} copy-done((bf16[32,64,128]{2,1,0:T(8,128)(2,1)S(1)}, bf16[32,64,128]{2,1,0:T(8,128)(2,1)}, u32[]{:S(2)}) %copy-start) | copy-done | bytes 524312
  27.6 1.2 %copy-done.2 = bf16[30,128,128]{2,1,0:T(8,128)(2,1)S(1)} copy-done((bf16[30,128,128]{2,1,0:T(8,128)(2,1)S(1)}, bf16[30,128,128]{2,1,0:T(8,128)(2,1)}, u32[]{:S(2)}) %copy-start.2) | copy-done | bytes 983064
  28.8 8.4 %near.1 = (f32[32,64,128]{2,1,0:T(8,128)S(1)}, bf16[32,64,128]{2,1,0:T(8,128)(2,1)S(1)}) custom-call(s32[32,30]{1,0:T(8,128)S(1)} %fusion.1.ids_ref, s32[2]{0:T(128)S(1)} %add_convert_fusion.edge_ref, f32[30,128]{1,0:T(8,128)S(1)} %pad_maximum_fusion.lag_ref, bf16[30,128,128]{2,1,0:T(8,128)(2,1)S(1)} %copy-done.2, bf16[32,64,128]{2,1,0:T(8,128)(2,1)S(1)} %copy-done, ...), custom_call_target="tpu_custom_call" | custom-call | tf_op jit(solution)/shard_map/near/pallas_call | solution.py:201
  37.2 2.1 %collective-permute-start.10 = (bf16[32,64,128]{2,1,0:T(8,128)(2,1)S(1)}, bf16[32,64,128]{2,1,0:T(8,128)(2,1)S(1)}, u32[]{:S(2)}, u32[]{:S(2)}) collective-permute-start(bf16[32,64,128]{2,1,0:T(8,128)(2,1)S(1)} %get-tuple-element.9), channel_id=1, source_target_pairs={{0,32},{1,33},{2,34},{3,35},{4,36},{5,37},{6,38},{7,39},{8,40},{9,... | collective-permute-start | bytes 1572872 | tf_op jit(solution)/shard_map/ppermute | solution.py:161
  39.3 1.4 %charge.1 = (f32[32,64,128]{2,1,0:T(8,128)S(1)}, f32[32,128]{1,0:T(8,128)S(1)}) custom-call(bf16[32,64,128]{2,1,0:T(8,128)(2,1)S(1)} %copy-done, bf16[128,128]{1,0:T(8,128)(2,1)S(1)} %copy-done.5), custom_call_target="tpu_custom_call" | custom-call | tf_op jit(solution)/shard_map/charge/pallas_call | solution.py:174
  40.7 6.7 %collective-permute-start.5 = (f32[32,128]{1,0:T(8,128)S(1)}, f32[32,128]{1,0:T(8,128)S(1)}, u32[]{:S(2)}, u32[]{:S(2)}) collective-permute-start(f32[32,128]{1,0:T(8,128)S(1)} %get-tuple-element.8), channel_id=1, source_target_pairs={{0,96},{1,97},{2,98},{3,99},{4,100},{5,101},{6,102},{7,103},{8,104... | collective-permute-start | bytes 49160 | tf_op jit(solution)/shard_map/ppermute | solution.py:161
  47.4 2.9 %collective-permute-start.4 = (f32[32,128]{1,0:T(8,128)S(1)}, f32[32,128]{1,0:T(8,128)S(1)}, u32[]{:S(2)}, u32[]{:S(2)}) collective-permute-start(f32[32,128]{1,0:T(8,128)S(1)} %get-tuple-element.8), channel_id=1, source_target_pairs={{0,64},{1,65},{2,66},{3,67},{4,68},{5,69},{6,70},{7,71},{8,72},{9,... | collective-permute-start | bytes 49160 | tf_op jit(solution)/shard_map/ppermute | solution.py:161
  50.3 3.2 %collective-permute-start.3 = (f32[32,128]{1,0:T(8,128)S(1)}, f32[32,128]{1,0:T(8,128)S(1)}, u32[]{:S(2)}, u32[]{:S(2)}) collective-permute-start(f32[32,128]{1,0:T(8,128)S(1)} %get-tuple-element.8), channel_id=1, source_target_pairs={{0,32},{1,33},{2,34},{3,35},{4,36},{5,37},{6,38},{7,39},{8,40},{9,... | collective-permute-start | bytes 49160 | tf_op jit(solution)/shard_map/ppermute | solution.py:161
  53.5 1.6 %collective-permute-done.4 = f32[32,128]{1,0:T(8,128)S(1)} collective-permute-done((f32[32,128]{1,0:T(8,128)S(1)}, f32[32,128]{1,0:T(8,128)S(1)}, u32[]{:S(2)}, u32[]{:S(2)}) %collective-permute-start.4) | collective-permute-done | bytes 16416 | tf_op jit(solution)/shard_map/ppermute | solution.py:161
  55.2 3.5 %collective-permute-done.3 = f32[32,128]{1,0:T(8,128)S(1)} collective-permute-done((f32[32,128]{1,0:T(8,128)S(1)}, f32[32,128]{1,0:T(8,128)S(1)}, u32[]{:S(2)}, u32[]{:S(2)}) %collective-permute-start.3) | collective-permute-done | bytes 16416 | tf_op jit(solution)/shard_map/ppermute | solution.py:161
  58.7 0.7 collective-permute-start.9
  59.3 1.3 %collective-permute-start.8 = (f32[32,128]{1,0:T(8,128)S(1)}, f32[32,128]{1,0:T(8,128)S(1)}, u32[]{:S(2)}, u32[]{:S(2)}) collective-permute-start(f32[32,128]{1,0:T(8,128)S(1)} %add_add_fusion.1), channel_id=1, source_target_pairs={{0,288},{1,289},{2,290},{3,291},{4,292},{5,293},{6,294},{7,295},{8... | collective-permute-start | bytes 49160 | tf_op jit(solution)/shard_map/ppermute | solution.py:161
  60.6 1.3 %collective-permute-start.7 = (f32[32,128]{1,0:T(8,128)S(1)}, f32[32,128]{1,0:T(8,128)S(1)}, u32[]{:S(2)}, u32[]{:S(2)}) collective-permute-start(f32[32,128]{1,0:T(8,128)S(1)} %add_add_fusion.1), channel_id=1, source_target_pairs={{0,160},{1,161},{2,162},{3,163},{4,164},{5,165},{6,166},{7,167},{8... | collective-permute-start | bytes 49160 | tf_op jit(solution)/shard_map/ppermute | solution.py:161
  61.9 2.5 %collective-permute-start.6 = (f32[32,128]{1,0:T(8,128)S(1)}, f32[32,128]{1,0:T(8,128)S(1)}, u32[]{:S(2)}, u32[]{:S(2)}) collective-permute-start(f32[32,128]{1,0:T(8,128)S(1)} %add_add_fusion.1), channel_id=1, source_target_pairs={{0,32},{1,33},{2,34},{3,35},{4,36},{5,37},{6,38},{7,39},{8,40},{9,... | collective-permute-start | bytes 49160 | tf_op jit(solution)/shard_map/ppermute | solution.py:161
  64.5 7.0 %collective-permute-done.6 = f32[32,128]{1,0:T(8,128)S(1)} collective-permute-done((f32[32,128]{1,0:T(8,128)S(1)}, f32[32,128]{1,0:T(8,128)S(1)}, u32[]{:S(2)}, u32[]{:S(2)}) %collective-permute-start.6) | collective-permute-done | bytes 16416 | tf_op jit(solution)/shard_map/ppermute | solution.py:161
  71.5 0.7 base.1.base_ref
  72.2 0.5 copy-done.1
  72.7 1.4 %final.1 = (bf16[32,64,128]{2,1,0:T(8,128)(2,1)}, f32[32,64,128]{2,1,0:T(8,128)}) custom-call(bf16[32,64,128]{2,1,0:T(8,128)(2,1)S(1)} %copy-done, f32[32,64,128]{2,1,0:T(8,128)S(1)} %base.1.base_ref, bf16[32,64,128]{2,1,0:T(8,128)(2,1)S(1)} %collective-permute-done.10.tail_ref, bf16[32,128,128]{2,1,0:T(8,128)(2,1)S(1)} %copy-done.1), custom_call_target="tpu_custom_call" | custom-call | tf_op jit(solution)/shard_map/final/pallas_call | solution.py:229
  (27 shorter events, 0.4 us)
Async XLA Ops:
  0.6 25.9 %collective-permute-start.2 = (bf16[32,64,128]{2,1,0:T(8,128)(2,1)}, bf16[32,64,128]{2,1,0:T(8,128)(2,1)S(1)}, u32[]{:S(2)}, u32[]{:S(2)}) collective-permute-start(bf16[32,64,128]{2,1,0:T(8,128)(2,1)} %cur_ref.3), channel_id=1, source_target_pairs={{0,31},{15,16},{16,15},{31,0},{32,63},{47,48},{48,47},{63,32},{64,... | collective-permute-start | bytes 1572872 | tf_op jit(solution)/shard_map/ppermute | solution.py:161
  13.9 12.6 %collective-permute-start.1 = (bf16[32,64,128]{2,1,0:T(8,128)(2,1)}, bf16[32,64,128]{2,1,0:T(8,128)(2,1)S(1)}, u32[]{:S(2)}, u32[]{:S(2)}) collective-permute-start(bf16[32,64,128]{2,1,0:T(8,128)(2,1)} %cur_ref.3), channel_id=1, source_target_pairs={{1,0},{2,1},{3,2},{4,3},{5,4},{6,5},{7,6},{8,7},{9,8},{10,9},{11,1... | collective-permute-start | bytes 1572872 | tf_op jit(solution)/shard_map/ppermute | solution.py:161
  15.2 11.3 %collective-permute-start = (bf16[32,64,128]{2,1,0:T(8,128)(2,1)}, bf16[32,64,128]{2,1,0:T(8,128)(2,1)S(1)}, u32[]{:S(2)}, u32[]{:S(2)}) collective-permute-start(bf16[32,64,128]{2,1,0:T(8,128)(2,1)} %cur_ref.3), channel_id=1, source_target_pairs={{0,1},{1,2},{2,3},{3,4},{4,5},{5,6},{6,7},{7,8},{8,9},{9,10},{10,1... | collective-permute-start | bytes 1572872 | tf_op jit(solution)/shard_map/ppermute | solution.py:161
  18.3 0.7 copy-start.6
  19.2 0.7 copy-start.7
  19.9 19.4 %copy-start.5 = (bf16[128,128]{1,0:T(8,128)(2,1)S(1)}, bf16[128,128]{1,0:T(8,128)(2,1)}, u32[]{:S(2)}) copy-start(bf16[128,128]{1,0:T(8,128)(2,1)} %map_ref.1) | copy-start | bytes 98308
  26.5 1.0 %copy-start = (bf16[32,64,128]{2,1,0:T(8,128)(2,1)S(1)}, bf16[32,64,128]{2,1,0:T(8,128)(2,1)}, u32[]{:S(2)}) copy-start(bf16[32,64,128]{2,1,0:T(8,128)(2,1)} %cur_ref.3) | copy-start | bytes 1572868
  27.6 1.2 %copy-start.2 = (bf16[30,128,128]{2,1,0:T(8,128)(2,1)S(1)}, bf16[30,128,128]{2,1,0:T(8,128)(2,1)}, u32[]{:S(2)}) copy-start(bf16[30,128,128]{2,1,0:T(8,128)(2,1)} %coup_ref.1) | copy-start | bytes 2949124
  37.2 34.3 %copy-start.3 = (bf16[32,64,128]{2,1,0:T(8,128)(2,1)S(1)}, bf16[32,64,128]{2,1,0:T(8,128)(2,1)}, u32[]{:S(2)}) copy-start(bf16[32,64,128]{2,1,0:T(8,128)(2,1)} %exc_ref.1) | copy-start | bytes 1572868
  37.2 35.0 %collective-permute-start.10 = (bf16[32,64,128]{2,1,0:T(8,128)(2,1)S(1)}, bf16[32,64,128]{2,1,0:T(8,128)(2,1)S(1)}, u32[]{:S(2)}, u32[]{:S(2)}) collective-permute-start(bf16[32,64,128]{2,1,0:T(8,128)(2,1)S(1)} %get-tuple-element.9), channel_id=1, source_target_pairs={{0,32},{1,33},{2,34},{3,35},{4,36},{5,37},{6,38},{7,39},{8,40},{9,... | collective-permute-start | bytes 1572872 | tf_op jit(solution)/shard_map/ppermute | solution.py:161
  40.7 12.8 %collective-permute-start.5 = (f32[32,128]{1,0:T(8,128)S(1)}, f32[32,128]{1,0:T(8,128)S(1)}, u32[]{:S(2)}, u32[]{:S(2)}) collective-permute-start(f32[32,128]{1,0:T(8,128)S(1)} %get-tuple-element.8), channel_id=1, source_target_pairs={{0,96},{1,97},{2,98},{3,99},{4,100},{5,101},{6,102},{7,103},{8,104... | collective-permute-start | bytes 49160 | tf_op jit(solution)/shard_map/ppermute | solution.py:161
  47.4 7.8 %collective-permute-start.4 = (f32[32,128]{1,0:T(8,128)S(1)}, f32[32,128]{1,0:T(8,128)S(1)}, u32[]{:S(2)}, u32[]{:S(2)}) collective-permute-start(f32[32,128]{1,0:T(8,128)S(1)} %get-tuple-element.8), channel_id=1, source_target_pairs={{0,64},{1,65},{2,66},{3,67},{4,68},{5,69},{6,70},{7,71},{8,72},{9,... | collective-permute-start | bytes 49160 | tf_op jit(solution)/shard_map/ppermute | solution.py:161
  50.3 8.3 %collective-permute-start.3 = (f32[32,128]{1,0:T(8,128)S(1)}, f32[32,128]{1,0:T(8,128)S(1)}, u32[]{:S(2)}, u32[]{:S(2)}) collective-permute-start(f32[32,128]{1,0:T(8,128)S(1)} %get-tuple-element.8), channel_id=1, source_target_pairs={{0,32},{1,33},{2,34},{3,35},{4,36},{5,37},{6,38},{7,39},{8,40},{9,... | collective-permute-start | bytes 49160 | tf_op jit(solution)/shard_map/ppermute | solution.py:161
  58.7 12.9 %copy-start.4 = (bf16[128,128]{1,0:T(8,128)(2,1)S(1)}, bf16[128,128]{1,0:T(8,128)(2,1)}, u32[]{:S(2)}) copy-start(bf16[128,128]{1,0:T(8,128)(2,1)} %pot_ref.1) | copy-start | bytes 98308
  58.7 5.8 %collective-permute-start.9 = (f32[32,128]{1,0:T(8,128)S(1)}, f32[32,128]{1,0:T(8,128)S(1)}, u32[]{:S(2)}, u32[]{:S(2)}) collective-permute-start(f32[32,128]{1,0:T(8,128)S(1)} %add_add_fusion.1), channel_id=1, source_target_pairs={{0,416},{1,417},{2,418},{3,419},{4,420},{5,421},{6,422},{7,423},{8... | collective-permute-start | bytes 49160 | tf_op jit(solution)/shard_map/ppermute | solution.py:161
  59.3 5.1 %collective-permute-start.8 = (f32[32,128]{1,0:T(8,128)S(1)}, f32[32,128]{1,0:T(8,128)S(1)}, u32[]{:S(2)}, u32[]{:S(2)}) collective-permute-start(f32[32,128]{1,0:T(8,128)S(1)} %add_add_fusion.1), channel_id=1, source_target_pairs={{0,288},{1,289},{2,290},{3,291},{4,292},{5,293},{6,294},{7,295},{8... | collective-permute-start | bytes 49160 | tf_op jit(solution)/shard_map/ppermute | solution.py:161
  60.6 3.9 %collective-permute-start.7 = (f32[32,128]{1,0:T(8,128)S(1)}, f32[32,128]{1,0:T(8,128)S(1)}, u32[]{:S(2)}, u32[]{:S(2)}) collective-permute-start(f32[32,128]{1,0:T(8,128)S(1)} %add_add_fusion.1), channel_id=1, source_target_pairs={{0,160},{1,161},{2,162},{3,163},{4,164},{5,165},{6,166},{7,167},{8... | collective-permute-start | bytes 49160 | tf_op jit(solution)/shard_map/ppermute | solution.py:161
  61.9 9.6 %collective-permute-start.6 = (f32[32,128]{1,0:T(8,128)S(1)}, f32[32,128]{1,0:T(8,128)S(1)}, u32[]{:S(2)}, u32[]{:S(2)}) collective-permute-start(f32[32,128]{1,0:T(8,128)S(1)} %add_add_fusion.1), channel_id=1, source_target_pairs={{0,32},{1,33},{2,34},{3,35},{4,36},{5,37},{6,38},{7,39},{8,40},{9,... | collective-permute-start | bytes 49160 | tf_op jit(solution)/shard_map/ppermute | solution.py:161
  71.5 1.2 %copy-start.1 = (bf16[32,128,128]{2,1,0:T(8,128)(2,1)S(1)}, bf16[32,128,128]{2,1,0:T(8,128)(2,1)}, u32[]{:S(2)}) copy-start(bf16[32,128,128]{2,1,0:T(8,128)(2,1)} %inv_ref.1) | copy-start | bytes 3145732

commit v2 on v1

v2 whole, which is shorter than its diff:
```python
import jax
import jax.numpy as jnp
from jax import lax
from jax.experimental import pallas as pl
from jax.experimental.pallas import tpu as pltpu
from jax.sharding import PartitionSpec as P

F32, BF16 = jnp.float32, jnp.bfloat16
MIB = 1 << 20


def whole(space=pltpu.VMEM):
    return pl.BlockSpec(memory_space=space)


def dot(a, b):
    return jnp.dot(a, b, preferred_element_type=F32)


def prep_kernel(cur_ref, map_ref, coup_ref, running_ref, totals_ref):
    del coup_ref
    per_dev, steps, unknowns = cur_ref.shape
    row = lax.broadcasted_iota(jnp.int32, (steps, 2 * steps), 0)
    col = lax.broadcasted_iota(jnp.int32, (steps, 2 * steps), 1)
    lower = (row >= col % steps).astype(F32).astype(BF16)
    group = 8

    @pl.loop(0, per_dev // group)
    def _(g):
        first = g * group
        rows = cur_ref[pl.ds(first, group)].reshape(group * steps, unknowns)
        inc = dot(rows, map_ref[...])
        high = inc.astype(BF16)
        low = (inc - high.astype(F32)).astype(BF16)
        last = []
        for i in range(group):
            cut = slice(i * steps, (i + 1) * steps)
            run = dot(lower, jnp.concatenate([high[cut], low[cut]], axis=0))
            running_ref[first + i] = run
            last.append(run[steps - 1 : steps])
        totals_ref[pl.ds(first, group)] = jnp.concatenate(last, axis=0)


def near_kernel(
    ids_ref, lag_ref, own_ref, inner_ref, outer_ref, coup_ref,
    head_ref, tail_ref, field, toep_ref, terms,
):
    per_dev, steps, unknowns = own_ref.shape
    slots = coup_ref.shape[0]
    group = min(16, per_dev)
    for part, ref in enumerate((own_ref, inner_ref, outer_ref)):
        field[part * per_dev : (part + 1) * per_dev] = ref[...]
    field[3 * per_dev] = jnp.zeros((steps, unknowns), BF16)
    lane = lax.broadcasted_iota(jnp.int32, (2 * steps, 2 * steps), 1)
    for p in range(slots // 2):
        even = jnp.broadcast_to(lag_ref[2 * p : 2 * p + 1, :], lane.shape)
        odd = jnp.broadcast_to(lag_ref[2 * p + 1 : 2 * p + 2, :], lane.shape)
        even = pltpu.roll(even, 0, 1, stride=1, stride_axis=0)
        odd = pltpu.roll(odd, steps, 1, stride=1, stride_axis=0)
        both = jnp.where(lane < steps, even, odd)
        toep_ref[:, p * 2 * steps : (p + 1) * 2 * steps] = both.astype(BF16)

    @pl.loop(0, per_dev // group)
    def _(g):
        first = g * group
        for k in range(slots):
            rows = [field[ids_ref[first + i, k]] for i in range(group)]
            z = dot(jnp.concatenate(rows, axis=0), coup_ref[k]).astype(BF16)
            at = slice(k * steps, (k + 1) * steps)
            for i in range(group):
                lanes = slice((i % 2) * unknowns, (i % 2 + 1) * unknowns)
                terms[i // 2, at, lanes] = z[i * steps : (i + 1) * steps]
        for i in range(0, group, 2):
            out = dot(toep_ref[...], terms[i // 2])
            for j in range(2):
                lanes = slice(j * unknowns, (j + 1) * unknowns)
                head_ref[first + i + j] = out[:steps, lanes]
                tail_ref[first + i + j] = out[steps:, lanes].astype(BF16)


def base_kernel(exc_ref, head_ref, running_ref, sums_ref, totals_ref, pot_ref, base_ref):
    per_dev, steps, unknowns = exc_ref.shape
    group = 8

    @pl.loop(0, per_dev // group)
    def _(g):
        at = pl.ds(g * group, group)
        before = sums_ref[at] - totals_ref[at]
        charge = (running_ref[at] + before[:, None, :]).astype(BF16)
        field = dot(charge.reshape(group * steps, -1), pot_ref[...])
        field = field.reshape(group, steps, unknowns)
        base_ref[at] = exc_ref[at].astype(F32) - head_ref[at] - field


def final_kernel(cur_ref, base_ref, tail_ref, inv_ref, updated_ref, residual_ref):
    for i in range(cur_ref.shape[0]):
        residual = base_ref[i] - tail_ref[i].astype(F32)
        residual_ref[i] = residual
        correction = dot(residual.astype(BF16), inv_ref[i])
        updated_ref[i] = (cur_ref[i].astype(F32) + correction).astype(BF16)


def on_device(
    currents, excitation, neighbours, lag_profile, couplings, block_inverses, charge_map, potential
):
    per_dev, steps, unknowns = currents.shape
    slots, lags = lag_profile.shape
    blocks, peers = lax.axis_size("tm"), lax.axis_size("clus")
    me = lax.axis_index("clus")

    def send(x, where):
        pairs = [
            (t * peers + c, u * peers + d % peers)
            for t in range(blocks)
            for c in range(peers)
            for u, d in [where(t, c)]
            if 0 <= u < blocks
        ]
        return lax.ppermute(x, ("tm", "clus"), pairs)

    def behind(x, by):
        return send(x, lambda t, c: (t + by, c))

    outer = send(currents, lambda t, c: (t, c + 1 if c % 2 else c - 1))
    inner = send(currents, lambda t, c: (t, c ^ 1))

    shape3 = (per_dev, steps, unknowns)
    sds = jax.ShapeDtypeStruct
    params = lambda mib: pltpu.CompilerParams(vmem_limit_bytes=mib * MIB)
    lag_rows = jnp.pad(lag_profile.astype(F32), ((0, 0), (0, 2 * steps - lags)))
    lag_rows = jnp.roll(lag_rows[:, ::-1], 1, axis=1)
    running, totals = pl.pallas_call(
        prep_kernel,
        name="prep",
        out_shape=(
            sds(shape3, F32),
            sds((per_dev, unknowns), F32),
        ),
        in_specs=[whole()] * 3,
        out_specs=(whole(),) * 2,
        compiler_params=params(16),
    )(currents, charge_map, couplings)

    owner = neighbours // per_dev
    part = jnp.where(owner == me, 0, jnp.where(owner == me ^ 1, 1, 2))
    ids = jnp.where(neighbours >= 0, part * per_dev + neighbours % per_dev, 3 * per_dev)

    sums = totals + behind(totals, 1)
    sums = sums + behind(sums, 2)
    ids, sums = lax.optimization_barrier((ids, sums))
    head, tail = pl.pallas_call(
        near_kernel,
        name="near",
        out_shape=(sds(shape3, F32), sds(shape3, BF16)),
        in_specs=[whole(pltpu.SMEM)] + [whole()] * 5,
        out_specs=(whole(), whole()),
        scratch_shapes=[
            pltpu.VMEM((3 * per_dev + 1, steps, unknowns), BF16),
            pltpu.VMEM((2 * steps, slots * steps), BF16),
            pltpu.VMEM((8, slots * steps, 2 * unknowns), BF16),
        ],
        compiler_params=params(24),
        cost_estimate=pl.CostEstimate(
            flops=2 * per_dev * slots * steps * unknowns * (unknowns + 2 * steps),
            bytes_accessed=8 * MIB,
            transcendentals=0,
        ),
    )(ids, lag_rows, currents, inner, outer, couplings)

    tail_before = behind(tail, 1)
    sums, head = lax.optimization_barrier((sums, head))
    by = 4
    while by < blocks:
        sums = sums + behind(sums, by)
        by *= 2
    base = pl.pallas_call(
        base_kernel,
        name="base",
        out_shape=sds(shape3, F32),
        in_specs=[whole()] * 6,
        out_specs=whole(),
        compiler_params=params(16),
    )(excitation, head, running, sums, totals, potential)
    return pl.pallas_call(
        final_kernel,
        name="final",
        out_shape=(sds(shape3, BF16), sds(shape3, F32)),
        in_specs=[whole()] * 4,
        out_specs=(whole(), whole()),
        compiler_params=params(16),
    )(currents, base, tail_before, block_inverses)


def solution(mesh):
    in_specs = (
        P("clus", "tm", None),
        P("clus", "tm", None),
        P("clus", None),
        P(),
        P(),
        P("clus", None, None),
        P(),
        P(),
    )
    out_specs = (P("clus", "tm", None), P("clus", "tm", None))
    return jax.shard_map(
        on_device, mesh=mesh, in_specs=in_specs, out_specs=out_specs, check_vma=False
    )
```

time: 74.7 us -> 74.3 us (level)
  the two profiles are of different devices: /device:TPU:2 before, /device:TPU:6 now
where the time goes in v2:
time: 74.3 us; the launch traced here: 73.7 us
  waiting for transfers between devices  32.3 us (43%)
  starting transfers between devices  25.2 us (34%)
  Pallas kernels  11.5 us (15%)
  local copies, waits for them, and re-layouts  3.67 us (5%)
  between operations  0.82 us (1%)
    ppermute x7, waiting for transfers between devices, send(): return lax.ppermute(x, ('tm', 'clus'), pairs)  32.3 us
    ppermute x7, starting transfers between devices, send(): return lax.ppermute(x, ('tm', 'clus'), pairs)  25.2 us
    pallas_call x1, Pallas kernels, on_device(): pl.pallas_call(near_kernel, name='near', out_shape=(sds(shape3, F32), sds...  8.04 us
    unnamed x20, local copies, waits for them, and re-layouts  3.52 us
  transfers between devices with their start and end apart: 7, of which 4 were waited for; matrix products, arithmetic and copies ran while one was open for 0% of the time, Pallas kernels for 3%

profile of v2, /device:TPU:6, one launch (start us, length us, event | category | flops | bytes accessed | tf_op | source)
XLA Modules:
  0.0 73.7 jit_solution(12269839615496514526)
XLA Ops:
  0.6 13.3 %collective-permute-start.3 = (bf16[32,64,128]{2,1,0:T(8,128)(2,1)}, bf16[32,64,128]{2,1,0:T(8,128)(2,1)S(1)}, u32[]{:S(2)}, u32[]{:S(2)}) collective-permute-start(bf16[32,64,128]{2,1,0:T(8,128)(2,1)} %cur_ref.3), channel_id=1, source_target_pairs={{0,31},{1,2},{2,1},{3,4},{4,3},{5,6},{6,5},{7,8},{8,7},{9,10},{10,... | collective-permute-start | bytes 1572872 | tf_op jit(solution)/shard_map/ppermute | solution.py:119
  13.9 1.9 %collective-permute-start.2 = (bf16[32,64,128]{2,1,0:T(8,128)(2,1)}, bf16[32,64,128]{2,1,0:T(8,128)(2,1)}, u32[]{:S(2)}, u32[]{:S(2)}) collective-permute-start(bf16[32,64,128]{2,1,0:T(8,128)(2,1)} %cur_ref.3), channel_id=1, source_target_pairs={{0,1},{1,0},{2,3},{3,2},{4,5},{5,4},{6,7},{7,6},{8,9},{9,8},{10,11... | collective-permute-start | bytes 1572872 | tf_op jit(solution)/shard_map/ppermute | solution.py:119
  15.8 1.0 %copy-done = bf16[32,64,128]{2,1,0:T(8,128)(2,1)S(1)} copy-done((bf16[32,64,128]{2,1,0:T(8,128)(2,1)S(1)}, bf16[32,64,128]{2,1,0:T(8,128)(2,1)}, u32[]{:S(2)}) %copy-start) | copy-done | bytes 524312
  16.9 1.2 %copy-done.3 = bf16[30,128,128]{2,1,0:T(8,128)(2,1)S(1)} copy-done((bf16[30,128,128]{2,1,0:T(8,128)(2,1)S(1)}, bf16[30,128,128]{2,1,0:T(8,128)(2,1)}, u32[]{:S(2)}) %copy-start.3) | copy-done | bytes 983064
  18.1 0.8 %copy-done.7 = bf16[128,128]{1,0:T(8,128)(2,1)S(1)} copy-done((bf16[128,128]{1,0:T(8,128)(2,1)S(1)}, bf16[128,128]{1,0:T(8,128)(2,1)}, u32[]{:S(2)}) %copy-start.7) | copy-done | bytes 32792
  18.8 1.4 %prep.1 = (f32[32,64,128]{2,1,0:T(8,128)S(1)}, f32[32,128]{1,0:T(8,128)S(1)}) custom-call(bf16[32,64,128]{2,1,0:T(8,128)(2,1)S(1)} %copy-done, bf16[128,128]{1,0:T(8,128)(2,1)S(1)} %copy-done.7, bf16[30,128,128]{2,1,0:T(8,128)(2,1)S(1)} %copy-done.3), custom_call_target="tpu_custom_call" | custom-call | tf_op jit(solution)/shard_map/prep/pallas_call | solution.py:132
  20.2 0.0 copy-start.9
  20.3 3.5 %collective-permute-start = (f32[32,128]{1,0:T(8,128)S(1)}, f32[32,128]{1,0:T(8,128)S(1)}, u32[]{:S(2)}, u32[]{:S(2)}) collective-permute-start(f32[32,128]{1,0:T(8,128)S(1)} %get-tuple-element.10.totals_ref), channel_id=1, source_target_pairs={{0,32},{1,33},{2,34},{3,35},{4,36},{5,37},{6,38},{7,39},{8,40},{9,... | collective-permute-start | bytes 49160 | tf_op jit(solution)/shard_map/ppermute | solution.py:119
  23.9 0.1 pad_slice_fusion
  23.9 0.1 slice.15
  24.0 6.8 %collective-permute-done = f32[32,128]{1,0:T(8,128)S(1)} collective-permute-done((f32[32,128]{1,0:T(8,128)S(1)}, f32[32,128]{1,0:T(8,128)S(1)}, u32[]{:S(2)}, u32[]{:S(2)}) %collective-permute-start) | collective-permute-done | bytes 16416 | tf_op jit(solution)/shard_map/ppermute | solution.py:119
  30.9 1.9 %collective-permute-start.1 = (f32[32,128]{1,0:T(8,128)S(1)}, f32[32,128]{1,0:T(8,128)S(1)}, u32[]{:S(2)}, u32[]{:S(2)}) collective-permute-start(f32[32,128]{1,0:T(8,128)S(1)} %add.26), channel_id=1, source_target_pairs={{0,64},{1,65},{2,66},{3,67},{4,68},{5,69},{6,70},{7,71},{8,72},{9,... | collective-permute-start | bytes 49160 | tf_op jit(solution)/shard_map/ppermute | solution.py:119
  32.8 0.1 pad_maximum_fusion.lag_ref
  32.9 5.4 %collective-permute-done.1 = f32[32,128]{1,0:T(8,128)S(1)} collective-permute-done((f32[32,128]{1,0:T(8,128)S(1)}, f32[32,128]{1,0:T(8,128)S(1)}, u32[]{:S(2)}, u32[]{:S(2)}) %collective-permute-start.1) | collective-permute-done | bytes 16416 | tf_op jit(solution)/shard_map/ppermute | solution.py:119
  38.3 8.0 %near.1 = (f32[32,64,128]{2,1,0:T(8,128)S(1)}, bf16[32,64,128]{2,1,0:T(8,128)(2,1)S(1)}) custom-call(s32[32,30]{1,0:T(8,128)S(1)} %fusion.1.ids_ref, f32[30,128]{1,0:T(8,128)S(1)} %pad_maximum_fusion.lag_ref, bf16[32,64,128]{2,1,0:T(8,128)(2,1)S(1)} %copy-done.1, bf16[32,64,128]{2,1,0:T(8,128)(2,1)} %collective-permute-done.2.inner_ref, ...), custom_call_target="tpu_custom_call" | custom-call | flops 4026531840 | bytes 8388608 | tf_op jit(solution)/shard_map/near/pallas_call | solution.py:151
  46.4 1.9 %collective-permute-start.6 = (bf16[32,64,128]{2,1,0:T(8,128)(2,1)S(1)}, bf16[32,64,128]{2,1,0:T(8,128)(2,1)S(1)}, u32[]{:S(2)}, u32[]{:S(2)}) collective-permute-start(bf16[32,64,128]{2,1,0:T(8,128)(2,1)S(1)} %get-tuple-element.17), channel_id=1, source_target_pairs={{0,32},{1,33},{2,34},{3,35},{4,36},{5,37},{6,38},{7,39},{8,40},{9,... | collective-permute-start | bytes 1572872 | tf_op jit(solution)/shard_map/ppermute | solution.py:119
  48.3 1.3 %collective-permute-start.4 = (f32[32,128]{1,0:T(8,128)S(1)}, f32[32,128]{1,0:T(8,128)S(1)}, u32[]{:S(2)}, u32[]{:S(2)}) collective-permute-start(f32[32,128]{1,0:T(8,128)S(1)} %add.27), channel_id=1, source_target_pairs={{0,128},{1,129},{2,130},{3,131},{4,132},{5,133},{6,134},{7,135},{8... | collective-permute-start | bytes 49160 | tf_op jit(solution)/shard_map/ppermute | solution.py:119
  49.6 14.2 %collective-permute-done.4 = f32[32,128]{1,0:T(8,128)S(1)} collective-permute-done((f32[32,128]{1,0:T(8,128)S(1)}, f32[32,128]{1,0:T(8,128)S(1)}, u32[]{:S(2)}, u32[]{:S(2)}) %collective-permute-start.4) | collective-permute-done | bytes 16416 | tf_op jit(solution)/shard_map/ppermute | solution.py:119
  63.8 1.4 %collective-permute-start.5 = (f32[32,128]{1,0:T(8,128)S(1)}, f32[32,128]{1,0:T(8,128)S(1)}, u32[]{:S(2)}, u32[]{:S(2)}) collective-permute-start(f32[32,128]{1,0:T(8,128)S(1)} %add.28), channel_id=1, source_target_pairs={{0,256},{1,257},{2,258},{3,259},{4,260},{5,261},{6,262},{7,263},{8... | collective-permute-start | bytes 49160 | tf_op jit(solution)/shard_map/ppermute | solution.py:119
  65.2 5.8 %collective-permute-done.5 = f32[32,128]{1,0:T(8,128)S(1)} collective-permute-done((f32[32,128]{1,0:T(8,128)S(1)}, f32[32,128]{1,0:T(8,128)S(1)}, u32[]{:S(2)}, u32[]{:S(2)}) %collective-permute-start.5) | collective-permute-done | bytes 16416 | tf_op jit(solution)/shard_map/ppermute | solution.py:119
  71.1 0.0 copy-start.2
  71.1 0.7 base.1.base_ref
  71.8 0.5 copy-done.2
  72.3 1.4 %final.1 = (bf16[32,64,128]{2,1,0:T(8,128)(2,1)}, f32[32,64,128]{2,1,0:T(8,128)}) custom-call(bf16[32,64,128]{2,1,0:T(8,128)(2,1)S(1)} %copy-done.1, f32[32,64,128]{2,1,0:T(8,128)S(1)} %base.1.base_ref, bf16[32,64,128]{2,1,0:T(8,128)(2,1)S(1)} %collective-permute-done.6.tail_ref, bf16[32,128,128]{2,1,0:T(8,128)(2,1)S(1)} %copy-done.2), custom_call_target="tpu_custom_call" | custom-call | tf_op jit(solution)/shard_map/final/pallas_call | solution.py:184
  (24 shorter events, 0.1 us)
Async XLA Ops:
  0.6 37.7 %collective-permute-start.3 = (bf16[32,64,128]{2,1,0:T(8,128)(2,1)}, bf16[32,64,128]{2,1,0:T(8,128)(2,1)S(1)}, u32[]{:S(2)}, u32[]{:S(2)}) collective-permute-start(bf16[32,64,128]{2,1,0:T(8,128)(2,1)} %cur_ref.3), channel_id=1, source_target_pairs={{0,31},{1,2},{2,1},{3,4},{4,3},{5,6},{6,5},{7,8},{8,7},{9,10},{10,... | collective-permute-start | bytes 1572872 | tf_op jit(solution)/shard_map/ppermute | solution.py:119
  13.9 24.4 %collective-permute-start.2 = (bf16[32,64,128]{2,1,0:T(8,128)(2,1)}, bf16[32,64,128]{2,1,0:T(8,128)(2,1)}, u32[]{:S(2)}, u32[]{:S(2)}) collective-permute-start(bf16[32,64,128]{2,1,0:T(8,128)(2,1)} %cur_ref.3), channel_id=1, source_target_pairs={{0,1},{1,0},{2,3},{3,2},{4,5},{5,4},{6,7},{7,6},{8,9},{9,8},{10,11... | collective-permute-start | bytes 1572872 | tf_op jit(solution)/shard_map/ppermute | solution.py:119
  15.8 1.0 %copy-start = (bf16[32,64,128]{2,1,0:T(8,128)(2,1)S(1)}, bf16[32,64,128]{2,1,0:T(8,128)(2,1)}, u32[]{:S(2)}) copy-start(bf16[32,64,128]{2,1,0:T(8,128)(2,1)} %cur_ref.3) | copy-start | bytes 1572868
  16.9 1.2 %copy-start.3 = (bf16[30,128,128]{2,1,0:T(8,128)(2,1)S(1)}, bf16[30,128,128]{2,1,0:T(8,128)(2,1)}, u32[]{:S(2)}) copy-start(bf16[30,128,128]{2,1,0:T(8,128)(2,1)} %coup_ref.3) | copy-start | bytes 2949124
  18.1 0.8 %copy-start.7 = (bf16[128,128]{1,0:T(8,128)(2,1)S(1)}, bf16[128,128]{1,0:T(8,128)(2,1)}, u32[]{:S(2)}) copy-start(bf16[128,128]{1,0:T(8,128)(2,1)} %map_ref.1) | copy-start | bytes 98308
  18.8 5.0 %copy-start.8 = (bf16[30,64]{1,0:T(8,128)(2,1)S(1)}, bf16[30,64]{1,0:T(8,128)(2,1)}, u32[]{:S(2)}) copy-start(bf16[30,64]{1,0:T(8,128)(2,1)} %param.11) | copy-start | bytes 11524
  18.8 19.5 %copy-start.1 = (bf16[32,64,128]{2,1,0:T(8,128)(2,1)S(1)}, bf16[32,64,128]{2,1,0:T(8,128)(2,1)}, u32[]{:S(2)}) copy-start(bf16[32,64,128]{2,1,0:T(8,128)(2,1)} %cur_ref.3) | copy-start | bytes 1572868
  18.8 19.5 %copy-start.4 = (bf16[30,128,128]{2,1,0:T(8,128)(2,1)S(1)}, bf16[30,128,128]{2,1,0:T(8,128)(2,1)}, u32[]{:S(2)}) copy-start(bf16[30,128,128]{2,1,0:T(8,128)(2,1)} %coup_ref.3) | copy-start | bytes 2949124
  20.2 3.6 %copy-start.9 = (s32[32,30]{1,0:T(8,128)S(1)}, s32[32,30]{1,0:T(8,128)}, u32[]{:S(2)}) copy-start(s32[32,30]{1,0:T(8,128)} %param.10) | copy-start | bytes 11524
  20.3 10.6 %collective-permute-start = (f32[32,128]{1,0:T(8,128)S(1)}, f32[32,128]{1,0:T(8,128)S(1)}, u32[]{:S(2)}, u32[]{:S(2)}) collective-permute-start(f32[32,128]{1,0:T(8,128)S(1)} %get-tuple-element.10.totals_ref), channel_id=1, source_target_pairs={{0,32},{1,33},{2,34},{3,35},{4,36},{5,37},{6,38},{7,39},{8,40},{9,... | collective-permute-start | bytes 49160 | tf_op jit(solution)/shard_map/ppermute | solution.py:119
  30.9 7.4 %collective-permute-start.1 = (f32[32,128]{1,0:T(8,128)S(1)}, f32[32,128]{1,0:T(8,128)S(1)}, u32[]{:S(2)}, u32[]{:S(2)}) collective-permute-start(f32[32,128]{1,0:T(8,128)S(1)} %add.26), channel_id=1, source_target_pairs={{0,64},{1,65},{2,66},{3,67},{4,68},{5,69},{6,70},{7,71},{8,72},{9,... | collective-permute-start | bytes 49160 | tf_op jit(solution)/shard_map/ppermute | solution.py:119
  38.3 32.8 %copy-start.5 = (bf16[32,64,128]{2,1,0:T(8,128)(2,1)S(1)}, bf16[32,64,128]{2,1,0:T(8,128)(2,1)}, u32[]{:S(2)}) copy-start(bf16[32,64,128]{2,1,0:T(8,128)(2,1)} %exc_ref.1) | copy-start | bytes 1572868
  46.4 25.4 %collective-permute-start.6 = (bf16[32,64,128]{2,1,0:T(8,128)(2,1)S(1)}, bf16[32,64,128]{2,1,0:T(8,128)(2,1)S(1)}, u32[]{:S(2)}, u32[]{:S(2)}) collective-permute-start(bf16[32,64,128]{2,1,0:T(8,128)(2,1)S(1)} %get-tuple-element.17), channel_id=1, source_target_pairs={{0,32},{1,33},{2,34},{3,35},{4,36},{5,37},{6,38},{7,39},{8,40},{9,... | collective-permute-start | bytes 1572872 | tf_op jit(solution)/shard_map/ppermute | solution.py:119
  48.3 15.5 %collective-permute-start.4 = (f32[32,128]{1,0:T(8,128)S(1)}, f32[32,128]{1,0:T(8,128)S(1)}, u32[]{:S(2)}, u32[]{:S(2)}) collective-permute-start(f32[32,128]{1,0:T(8,128)S(1)} %add.27), channel_id=1, source_target_pairs={{0,128},{1,129},{2,130},{3,131},{4,132},{5,133},{6,134},{7,135},{8... | collective-permute-start | bytes 49160 | tf_op jit(solution)/shard_map/ppermute | solution.py:119
  63.8 7.3 %copy-start.6 = (bf16[128,128]{1,0:T(8,128)(2,1)S(1)}, bf16[128,128]{1,0:T(8,128)(2,1)}, u32[]{:S(2)}) copy-start(bf16[128,128]{1,0:T(8,128)(2,1)} %pot_ref.1) | copy-start | bytes 98308
  63.8 7.3 %collective-permute-start.5 = (f32[32,128]{1,0:T(8,128)S(1)}, f32[32,128]{1,0:T(8,128)S(1)}, u32[]{:S(2)}, u32[]{:S(2)}) collective-permute-start(f32[32,128]{1,0:T(8,128)S(1)} %add.28), channel_id=1, source_target_pairs={{0,256},{1,257},{2,258},{3,259},{4,260},{5,261},{6,262},{7,263},{8... | collective-permute-start | bytes 49160 | tf_op jit(solution)/shard_map/ppermute | solution.py:119
  71.1 1.2 %copy-start.2 = (bf16[32,128,128]{2,1,0:T(8,128)(2,1)S(1)}, bf16[32,128,128]{2,1,0:T(8,128)(2,1)}, u32[]{:S(2)}) copy-start(bf16[32,128,128]{2,1,0:T(8,128)(2,1)} %inv_ref.1) | copy-start | bytes 3145732

commit v3 on v2

--- a/solution.py
+++ b/solution.py
@@ -17,8 +17,7 @@
     return jnp.dot(a, b, preferred_element_type=F32)
 
 
-def prep_kernel(cur_ref, map_ref, coup_ref, running_ref, totals_ref):
-    del coup_ref
+def prep_kernel(cur_ref, map_ref, running_ref, totals_ref):
     per_dev, steps, unknowns = cur_ref.shape
     row = lax.broadcasted_iota(jnp.int32, (steps, 2 * steps), 0)
     col = lax.broadcasted_iota(jnp.int32, (steps, 2 * steps), 1)
@@ -42,14 +41,18 @@
 
 
 def near_kernel(
-    ids_ref, lag_ref, own_ref, inner_ref, outer_ref, coup_ref,
-    head_ref, tail_ref, field, toep_ref, terms,
+    ids_ref, lag_ref, own_ref, inner_ref, outer_ref, coup_hbm,
+    head_ref, tail_ref, field, coup_ref, toep_ref, terms, sems,
 ):
     per_dev, steps, unknowns = own_ref.shape
     slots = coup_ref.shape[0]
     group = min(16, per_dev)
+    copies = [pltpu.make_async_copy(coup_hbm, coup_ref, sems.at[3])]
     for part, ref in enumerate((own_ref, inner_ref, outer_ref)):
-        field[part * per_dev : (part + 1) * per_dev] = ref[...]
+        to = field.at[pl.ds(part * per_dev, per_dev)]
+        copies.append(pltpu.make_async_copy(ref, to, sems.at[part]))
+    for copy in copies:
+        copy.start()
     field[3 * per_dev] = jnp.zeros((steps, unknowns), BF16)
     lane = lax.broadcasted_iota(jnp.int32, (2 * steps, 2 * steps), 1)
     for p in range(slots // 2):
@@ -59,6 +62,8 @@
         odd = pltpu.roll(odd, steps, 1, stride=1, stride_axis=0)
         both = jnp.where(lane < steps, even, odd)
         toep_ref[:, p * 2 * steps : (p + 1) * 2 * steps] = both.astype(BF16)
+    for copy in copies:
+        copy.wait()
 
     @pl.loop(0, per_dev // group)
     def _(g):
@@ -78,15 +83,14 @@
                 tail_ref[first + i + j] = out[steps:, lanes].astype(BF16)
 
 
-def base_kernel(exc_ref, head_ref, running_ref, sums_ref, totals_ref, pot_ref, base_ref):
+def base_kernel(exc_ref, head_ref, running_ref, before_ref, pot_ref, base_ref):
     per_dev, steps, unknowns = exc_ref.shape
     group = 8
 
     @pl.loop(0, per_dev // group)
     def _(g):
         at = pl.ds(g * group, group)
-        before = sums_ref[at] - totals_ref[at]
-        charge = (running_ref[at] + before[:, None, :]).astype(BF16)
+        charge = (running_ref[at] + before_ref[at][:, None, :]).astype(BF16)
         field = dot(charge.reshape(group * steps, -1), pot_ref[...])
         field = field.reshape(group, steps, unknowns)
         base_ref[at] = exc_ref[at].astype(F32) - head_ref[at] - field
@@ -136,30 +140,34 @@
             sds(shape3, F32),
             sds((per_dev, unknowns), F32),
         ),
-        in_specs=[whole()] * 3,
+        in_specs=[whole()] * 2,
         out_specs=(whole(),) * 2,
         compiler_params=params(16),
-    )(currents, charge_map, couplings)
+    )(currents, charge_map)
 
     owner = neighbours // per_dev
     part = jnp.where(owner == me, 0, jnp.where(owner == me ^ 1, 1, 2))
     ids = jnp.where(neighbours >= 0, part * per_dev + neighbours % per_dev, 3 * per_dev)
 
-    sums = totals + behind(totals, 1)
-    sums = sums + behind(sums, 2)
-    ids, sums = lax.optimization_barrier((ids, sums))
+    later = jnp.arange(blocks) > lax.axis_index("tm")
+    before = lax.psum_scatter(
+        jnp.where(later[:, None, None], totals, 0.0), "tm", scatter_dimension=0
+    )
+    ids, running = lax.optimization_barrier((ids, running))
     head, tail = pl.pallas_call(
         near_kernel,
         name="near",
         out_shape=(sds(shape3, F32), sds(shape3, BF16)),
-        in_specs=[whole(pltpu.SMEM)] + [whole()] * 5,
+        in_specs=[whole(pltpu.SMEM), whole()] + [whole(pl.ANY)] * 4,
         out_specs=(whole(), whole()),
         scratch_shapes=[
             pltpu.VMEM((3 * per_dev + 1, steps, unknowns), BF16),
+            pltpu.VMEM(couplings.shape, BF16),
             pltpu.VMEM((2 * steps, slots * steps), BF16),
             pltpu.VMEM((8, slots * steps, 2 * unknowns), BF16),
+            pltpu.SemaphoreType.DMA((4,)),
         ],
-        compiler_params=params(24),
+        compiler_params=params(56),
         cost_estimate=pl.CostEstimate(
             flops=2 * per_dev * slots * steps * unknowns * (unknowns + 2 * steps),
             bytes_accessed=8 * MIB,
@@ -168,19 +176,14 @@
     )(ids, lag_rows, currents, inner, outer, couplings)
 
     tail_before = behind(tail, 1)
-    sums, head = lax.optimization_barrier((sums, head))
-    by = 4
-    while by < blocks:
-        sums = sums + behind(sums, by)
-        by *= 2
     base = pl.pallas_call(
         base_kernel,
         name="base",
         out_shape=sds(shape3, F32),
-        in_specs=[whole()] * 6,
+        in_specs=[whole()] * 5,
         out_specs=whole(),
         compiler_params=params(16),
-    )(excitation, head, running, sums, totals, potential)
+    )(excitation, head, running, before, potential)
     return pl.pallas_call(
         final_kernel,
         name="final",

time: 74.3 us -> 120 us (1.62)
  the two profiles are of different devices: /device:TPU:6 before, /device:TPU:8 now
where the time goes in v3:
time: 120 us
  waiting for transfers between devices  72.1 us (60%)
  between operations  14.1 us (12%)
  Pallas kernels  13.8 us (12%)
  starting transfers between devices  9.86 us (8%)
  local copies, waits for them, and re-layouts  7.47 us (6%)
  other arithmetic  2.12 us (2%)
    reduce_scatter x1, waiting for transfers between devices, on_device(): lax.psum_scatter(jnp.where(later[:, None, None], totals, 0.0), 'tm', scat...  72.1 us
    pallas_call x1, Pallas kernels, on_device(): pl.pallas_call(near_kernel, name='near', out_shape=(sds(shape3, F32), sds...  10.3 us
    ppermute x3, starting transfers between devices, send(): return lax.ppermute(x, ('tm', 'clus'), pairs)  9.83 us
    unnamed x24, local copies, waits for them, and re-layouts  7.32 us
  transfers between devices with their start and end apart: 4, of which 1 were waited for; matrix products, arithmetic and copies ran while one was open for 2% of the time, Pallas kernels for 10%

profile of v3, /device:TPU:8, one launch (start us, length us, event | category | flops | bytes accessed | tf_op | source)
XLA Modules:
  0.0 119.5 jit_solution(2576078558545180638)
XLA Ops:
  7.2 0.0 reduce-scatter.2.cloned.1.call-start
  7.2 1.9 %collective-permute-start.1 = (bf16[32,64,128]{2,1,0:T(8,128)(2,1)}, bf16[32,64,128]{2,1,0:T(8,128)(2,1)S(1)}, u32[]{:S(2)}, u32[]{:S(2)}) collective-permute-start(bf16[32,64,128]{2,1,0:T(8,128)(2,1)} %cur_ref.3), channel_id=1, source_target_pairs={{0,31},{1,2},{2,1},{3,4},{4,3},{5,6},{6,5},{7,8},{8,7},{9,10},{10,... | collective-permute-start | bytes 1572872 | tf_op jit(solution)/shard_map/ppermute | solution.py:123
  9.1 3.6 %collective-permute-start = (bf16[32,64,128]{2,1,0:T(8,128)(2,1)}, bf16[32,64,128]{2,1,0:T(8,128)(2,1)S(1)}, u32[]{:S(2)}, u32[]{:S(2)}) collective-permute-start(bf16[32,64,128]{2,1,0:T(8,128)(2,1)} %cur_ref.3), channel_id=1, source_target_pairs={{0,1},{1,0},{2,3},{3,2},{4,5},{5,4},{6,7},{7,6},{8,9},{9,8},{10,11... | collective-permute-start | bytes 1572872 | tf_op jit(solution)/shard_map/ppermute | solution.py:123
  12.8 1.0 copy-done
  13.8 0.8 copy-done.6
  14.6 1.4 %prep.1 = (f32[32,64,128]{2,1,0:T(8,128)S(1)}, f32[32,128]{1,0:T(8,128)S(1)}) custom-call(bf16[32,64,128]{2,1,0:T(8,128)(2,1)S(1)} %copy-done, bf16[128,128]{1,0:T(8,128)(2,1)S(1)} %copy-done.6), custom_call_target="tpu_custom_call" | custom-call | tf_op jit(solution)/shard_map/prep/pallas_call | solution.py:136
  16.0 0.8 broadcast_select_fusion
  16.8 0.7 copy-done.8
  17.5 0.1 pad_slice_fusion
  17.6 0.1 slice.15
  17.6 0.6 copy-done.9
  18.3 0.6 fusion.1.ids_ref
  18.9 0.7 pad_maximum_fusion.lag_ref
  19.6 0.8 copy-done.10
  20.4 0.8 copy-done.11
  21.2 10.3 %near.1 = (f32[32,64,128]{2,1,0:T(8,128)}, bf16[32,64,128]{2,1,0:T(8,128)(2,1)}) custom-call(s32[32,30]{1,0:T(8,128)} %fusion.1.ids_ref, f32[30,128]{1,0:T(8,128)} %pad_maximum_fusion.lag_ref, bf16[32,64,128]{2,1,0:T(8,128)(2,1)} %cur_ref.3, bf16[32,64,128]{2,1,0:T(8,128)(2,1)} %copy-done.11, bf16[32,64,128]{2,1,0:T(8,128)(2,1)} %copy-done.10, ...), custom_call_target="tpu_custom_call" | custom-call | flops 4026531840 | bytes 8388608 | tf_op jit(solution)/shard_map/near/pallas_call | solution.py:157
  31.5 4.3 %collective-permute-start.2 = (bf16[32,64,128]{2,1,0:T(8,128)(2,1)}, bf16[32,64,128]{2,1,0:T(8,128)(2,1)S(1)}, u32[]{:S(2)}, u32[]{:S(2)}) collective-permute-start(bf16[32,64,128]{2,1,0:T(8,128)(2,1)} %get-tuple-element.13), channel_id=1, source_target_pairs={{0,32},{1,33},{2,34},{3,35},{4,36},{5,37},{6,38},{7,39},{8,40},{9,... | collective-permute-start | bytes 1572872 | tf_op jit(solution)/shard_map/ppermute | solution.py:123
  35.9 72.1 %reduce-scatter.2.cloned.1.call-done = f32[1,32,128]{2,1,0:T(8,128)} async-done(((f32[16,32,128]{2,1,0:T(8,128)}), f32[1,32,128]{2,1,0:T(8,128)}) %reduce-scatter.2.cloned.1.call-update) | async-done | bytes 16400 | tf_op jit(solution)/shard_map/reduce_scatter | solution.py:153
  108.0 1.2 %copy-done.3 = f32[32,64,128]{2,1,0:T(8,128)S(1)} copy-done((f32[32,64,128]{2,1,0:T(8,128)S(1)}, f32[32,64,128]{2,1,0:T(8,128)}, u32[]{:S(2)}) %copy-start.3) | copy-done | bytes 1048600
  109.2 0.7 copy-done.7
  109.9 0.7 base.1.base_ref
  110.6 0.3 copy-done.1
  111.0 0.3 copy-done.2
  111.3 1.4 %final.1 = (bf16[32,64,128]{2,1,0:T(8,128)(2,1)}, f32[32,64,128]{2,1,0:T(8,128)}) custom-call(bf16[32,64,128]{2,1,0:T(8,128)(2,1)S(1)} %copy-done.1, f32[32,64,128]{2,1,0:T(8,128)S(1)} %base.1.base_ref, bf16[32,64,128]{2,1,0:T(8,128)(2,1)S(1)} %collective-permute-done.2.tail_ref, bf16[32,128,128]{2,1,0:T(8,128)(2,1)S(1)} %copy-done.2), custom_call_target="tpu_custom_call" | custom-call | tf_op jit(solution)/shard_map/final/pallas_call | solution.py:187
  (21 shorter events, 0.1 us)
Async XLA Ops:
  7.2 100.8 %reduce-scatter.2.cloned.1.call-start = ((), (), s32[]{:S(2)}) async-start(), calls=%async_computation.1 | async-start | bytes 278528 | tf_op jit(solution)/shard_map/reduce_scatter | solution.py:153
  7.2 12.4 %collective-permute-start.1 = (bf16[32,64,128]{2,1,0:T(8,128)(2,1)}, bf16[32,64,128]{2,1,0:T(8,128)(2,1)S(1)}, u32[]{:S(2)}, u32[]{:S(2)}) collective-permute-start(bf16[32,64,128]{2,1,0:T(8,128)(2,1)} %cur_ref.3), channel_id=1, source_target_pairs={{0,31},{1,2},{2,1},{3,4},{4,3},{5,6},{6,5},{7,8},{8,7},{9,10},{10,... | collective-permute-start | bytes 1572872 | tf_op jit(solution)/shard_map/ppermute | solution.py:123
  9.1 10.5 %collective-permute-start = (bf16[32,64,128]{2,1,0:T(8,128)(2,1)}, bf16[32,64,128]{2,1,0:T(8,128)(2,1)S(1)}, u32[]{:S(2)}, u32[]{:S(2)}) collective-permute-start(bf16[32,64,128]{2,1,0:T(8,128)(2,1)} %cur_ref.3), channel_id=1, source_target_pairs={{0,1},{1,0},{2,3},{3,2},{4,5},{5,4},{6,7},{7,6},{8,9},{9,8},{10,11... | collective-permute-start | bytes 1572872 | tf_op jit(solution)/shard_map/ppermute | solution.py:123
  12.8 1.0 copy-start
  13.8 0.8 copy-start.6
  16.8 0.7 copy-start.8
  17.6 0.7 copy-start.9
  19.6 88.4 %copy-start.4 = (bf16[32,64,128]{2,1,0:T(8,128)(2,1)S(1)}, bf16[32,64,128]{2,1,0:T(8,128)(2,1)}, u32[]{:S(2)}) copy-start(bf16[32,64,128]{2,1,0:T(8,128)(2,1)} %exc_ref.1) | copy-start | bytes 1572868
  19.6 88.4 %copy-start.5 = (bf16[128,128]{1,0:T(8,128)(2,1)S(1)}, bf16[128,128]{1,0:T(8,128)(2,1)}, u32[]{:S(2)}) copy-start(bf16[128,128]{1,0:T(8,128)(2,1)} %pot_ref.1) | copy-start | bytes 98308
  19.6 0.8 copy-start.10
  20.4 0.8 copy-start.11
  31.5 79.1 %collective-permute-start.2 = (bf16[32,64,128]{2,1,0:T(8,128)(2,1)}, bf16[32,64,128]{2,1,0:T(8,128)(2,1)S(1)}, u32[]{:S(2)}, u32[]{:S(2)}) collective-permute-start(bf16[32,64,128]{2,1,0:T(8,128)(2,1)} %get-tuple-element.13), channel_id=1, source_target_pairs={{0,32},{1,33},{2,34},{3,35},{4,36},{5,37},{6,38},{7,39},{8,40},{9,... | collective-permute-start | bytes 1572872 | tf_op jit(solution)/shard_map/ppermute | solution.py:123
  108.0 1.2 %copy-start.3 = (f32[32,64,128]{2,1,0:T(8,128)S(1)}, f32[32,64,128]{2,1,0:T(8,128)}, u32[]{:S(2)}) copy-start(f32[32,64,128]{2,1,0:T(8,128)} %get-tuple-element.10.head_ref) | copy-start | bytes 3145732
  109.2 0.7 copy-start.7
  109.9 1.0 copy-start.1
  109.9 1.4 %copy-start.2 = (bf16[32,128,128]{2,1,0:T(8,128)(2,1)S(1)}, bf16[32,128,128]{2,1,0:T(8,128)(2,1)}, u32[]{:S(2)}) copy-start(bf16[32,128,128]{2,1,0:T(8,128)(2,1)} %inv_ref.1) | copy-start | bytes 3145732
Sparse Core Ops, SparseCore 0:
  16.9 90.9 reduce-scatter.1

commit v4 on v3

--- a/solution.py
+++ b/solution.py
@@ -37,23 +37,14 @@
             run = dot(lower, jnp.concatenate([high[cut], low[cut]], axis=0))
             running_ref[first + i] = run
             last.append(run[steps - 1 : steps])
-        totals_ref[pl.ds(first, group)] = jnp.concatenate(last, axis=0)
-
-
-def near_kernel(
-    ids_ref, lag_ref, own_ref, inner_ref, outer_ref, coup_hbm,
-    head_ref, tail_ref, field, coup_ref, toep_ref, terms, sems,
-):
-    per_dev, steps, unknowns = own_ref.shape
-    slots = coup_ref.shape[0]
-    group = min(16, per_dev)
-    copies = [pltpu.make_async_copy(coup_hbm, coup_ref, sems.at[3])]
-    for part, ref in enumerate((own_ref, inner_ref, outer_ref)):
-        to = field.at[pl.ds(part * per_dev, per_dev)]
-        copies.append(pltpu.make_async_copy(ref, to, sems.at[part]))
-    for copy in copies:
-        copy.start()
-    field[3 * per_dev] = jnp.zeros((steps, unknowns), BF16)
+        totals = jnp.concatenate(last, axis=0)
+        for t in range(totals_ref.shape[0]):
+            totals_ref[t, pl.ds(first, group)] = totals
+
+
+def factor_kernel(lag_ref, coup_ref, own_ref, inner_ref, toep_ref, copy_ref, known_ref):
+    slots = lag_ref.shape[0]
+    steps = toep_ref.shape[1] // slots
     lane = lax.broadcasted_iota(jnp.int32, (2 * steps, 2 * steps), 1)
     for p in range(slots // 2):
         even = jnp.broadcast_to(lag_ref[2 * p : 2 * p + 1, :], lane.shape)
@@ -62,8 +53,22 @@
         odd = pltpu.roll(odd, steps, 1, stride=1, stride_axis=0)
         both = jnp.where(lane < steps, even, odd)
         toep_ref[:, p * 2 * steps : (p + 1) * 2 * steps] = both.astype(BF16)
-    for copy in copies:
-        copy.wait()
+    copy_ref[...] = coup_ref[...]
+    per_dev = own_ref.shape[0]
+    known_ref[:per_dev] = own_ref[...]
+    known_ref[per_dev:] = inner_ref[...]
+
+
+def near_kernel(
+    ids_ref, known_ref, outer_ref, coup_ref, toep_ref,
+    head_ref, tail_ref, field, terms,
+):
+    per_dev, steps, unknowns = outer_ref.shape
+    slots = coup_ref.shape[0]
+    group = min(16, per_dev)
+    field[: 2 * per_dev] = known_ref[...]
+    field[2 * per_dev : 3 * per_dev] = outer_ref[...]
+    field[3 * per_dev] = jnp.zeros((steps, unknowns), BF16)
 
     @pl.loop(0, per_dev // group)
     def _(g):
@@ -138,7 +143,7 @@
         name="prep",
         out_shape=(
             sds(shape3, F32),
-            sds((per_dev, unknowns), F32),
+            sds((blocks, per_dev, unknowns), F32),
         ),
         in_specs=[whole()] * 2,
         out_specs=(whole(),) * 2,
@@ -149,33 +154,42 @@
     part = jnp.where(owner == me, 0, jnp.where(owner == me ^ 1, 1, 2))
     ids = jnp.where(neighbours >= 0, part * per_dev + neighbours % per_dev, 3 * per_dev)
 
-    later = jnp.arange(blocks) > lax.axis_index("tm")
-    before = lax.psum_scatter(
-        jnp.where(later[:, None, None], totals, 0.0), "tm", scatter_dimension=0
-    )
-    ids, running = lax.optimization_barrier((ids, running))
+    pieces = lax.all_to_all(totals, "tm", 0, 0)
+    lag_rows, couplings, running = lax.optimization_barrier((lag_rows, couplings, running))
+    toeplitz, factors, known = pl.pallas_call(
+        factor_kernel,
+        name="factors",
+        out_shape=(
+            sds((2 * steps, slots * steps), BF16),
+            sds(couplings.shape, BF16),
+            sds((2 * per_dev, steps, unknowns), BF16),
+        ),
+        in_specs=[whole()] * 4,
+        out_specs=(whole(),) * 3,
+        compiler_params=params(16),
+    )(lag_rows, couplings, currents, inner)
     head, tail = pl.pallas_call(
         near_kernel,
         name="near",
         out_shape=(sds(shape3, F32), sds(shape3, BF16)),
-        in_specs=[whole(pltpu.SMEM), whole()] + [whole(pl.ANY)] * 4,
+        in_specs=[whole(pltpu.SMEM)] + [whole()] * 4,
         out_specs=(whole(), whole()),
         scratch_shapes=[
             pltpu.VMEM((3 * per_dev + 1, steps, unknowns), BF16),
-            pltpu.VMEM(couplings.shape, BF16),
-            pltpu.VMEM((2 * steps, slots * steps), BF16),
             pltpu.VMEM((8, slots * steps, 2 * unknowns), BF16),
-            pltpu.SemaphoreType.DMA((4,)),
         ],
-        compiler_params=params(56),
+        compiler_params=params(24),
         cost_estimate=pl.CostEstimate(
             flops=2 * per_dev * slots * steps * unknowns * (unknowns + 2 * steps),
             bytes_accessed=8 * MIB,
             transcendentals=0,
         ),
-    )(ids, lag_rows, currents, inner, outer, couplings)
+    )(ids, known, outer, factors, toeplitz)
 
     tail_before = behind(tail, 1)
+    earlier = jnp.arange(blocks) < lax.axis_index("tm")
+    pieces, head = lax.optimization_barrier((pieces, head))
+    before = jnp.sum(jnp.where(earlier[:, None, None], pieces, 0.0), axis=0)
     base = pl.pallas_call(
         base_kernel,
         name="base",

time: 120 us -> 58 us (0.48)
  the two profiles are of different devices: /device:TPU:8 before, /device:TPU:2 now
where the time goes in v4:
time: 58 us; the launch traced here: 57.3 us
  starting transfers between devices  26.9 us (46%)
  Pallas kernels  13.9 us (24%)
  waiting for transfers between devices  9.21 us (16%)
  local copies, waits for them, and re-layouts  6.29 us (11%)
  between operations  0.79 us (1%)
    ppermute x3, starting transfers between devices, send(): return lax.ppermute(x, ('tm', 'clus'), pairs)  19.2 us
    ppermute x3, waiting for transfers between devices, send(): return lax.ppermute(x, ('tm', 'clus'), pairs)  9.21 us
    pallas_call x1, Pallas kernels, on_device(): pl.pallas_call(near_kernel, name='near', out_shape=(sds(shape3, F32), sds...  8.26 us
    all_to_all x1, starting transfers between devices, on_device(): pieces = lax.all_to_all(totals, 'tm', 0, 0)  7.71 us
    unnamed x22, local copies, waits for them, and re-layouts  6.13 us
    pallas_call x1, Pallas kernels, on_device(): pl.pallas_call(final_kernel, name='final', out_shape=(sds(shape3, BF16),...  2.42 us
    pallas_call x1, Pallas kernels, on_device(): pl.pallas_call(prep_kernel, name='prep', out_shape=(sds(shape3, F32), sds...  2.15 us
  transfers between devices with their start and end apart: 4, of which 1 were waited for; matrix products, arithmetic and copies ran while one was open for 1% of the time, Pallas kernels for 20%

profile of v4, /device:TPU:2, one launch (start us, length us, event | category | flops | bytes accessed | tf_op | source)
XLA Modules:
  0.0 57.3 jit_solution(18092963995693799213)
XLA Ops:
  0.6 1.9 %collective-permute-start = (bf16[32,64,128]{2,1,0:T(8,128)(2,1)}, bf16[32,64,128]{2,1,0:T(8,128)(2,1)S(1)}, u32[]{:S(2)}, u32[]{:S(2)}) collective-permute-start(bf16[32,64,128]{2,1,0:T(8,128)(2,1)} %cur_ref.3), channel_id=1, source_target_pairs={{0,1},{1,0},{2,3},{3,2},{4,5},{5,4},{6,7},{7,6},{8,9},{9,8},{10,11... | collective-permute-start | bytes 1572872 | tf_op jit(solution)/shard_map/ppermute | solution.py:128
  2.6 13.9 %collective-permute-start.1 = (bf16[32,64,128]{2,1,0:T(8,128)(2,1)}, bf16[32,64,128]{2,1,0:T(8,128)(2,1)S(1)}, u32[]{:S(2)}, u32[]{:S(2)}) collective-permute-start(bf16[32,64,128]{2,1,0:T(8,128)(2,1)} %cur_ref.3), channel_id=1, source_target_pairs={{0,31},{1,2},{2,1},{3,4},{4,3},{5,6},{6,5},{7,8},{8,7},{9,10},{10,... | collective-permute-start | bytes 1572872 | tf_op jit(solution)/shard_map/ppermute | solution.py:128
  16.5 1.0 %copy-done = bf16[32,64,128]{2,1,0:T(8,128)(2,1)S(1)} copy-done((bf16[32,64,128]{2,1,0:T(8,128)(2,1)S(1)}, bf16[32,64,128]{2,1,0:T(8,128)(2,1)}, u32[]{:S(2)}) %copy-start) | copy-done | bytes 524312
  17.5 0.8 %copy-done.6 = bf16[128,128]{1,0:T(8,128)(2,1)S(1)} copy-done((bf16[128,128]{1,0:T(8,128)(2,1)S(1)}, bf16[128,128]{1,0:T(8,128)(2,1)}, u32[]{:S(2)}) %copy-start.6) | copy-done | bytes 32792
  18.3 2.2 %prep.1 = (f32[32,64,128]{2,1,0:T(8,128)S(1)}, f32[16,32,128]{2,1,0:T(8,128)}) custom-call(bf16[32,64,128]{2,1,0:T(8,128)(2,1)S(1)} %copy-done, bf16[128,128]{1,0:T(8,128)(2,1)S(1)} %copy-done.6), custom_call_target="tpu_custom_call" | custom-call | tf_op jit(solution)/shard_map/prep/pallas_call | solution.py:141
  20.5 7.7 %all-to-all-start = ((f32[16,32,128]{2,1,0:T(8,128)}), f32[16,32,128]{2,1,0:T(8,128)S(1)}, u32[]{:S(2)}, u32[]{:S(2)}) async-start(f32[16,32,128]{2,1,0:T(8,128)} %get-tuple-element.14), calls=%async_computation | async-start | bytes 524288 | tf_op jit(solution)/shard_map/all_to_all | solution.py:157
  28.2 0.1 pad_slice_fusion
  28.3 0.1 slice.15
  28.3 0.1 pad_maximum_fusion.lag_ref
  28.4 0.6 %copy-done.10 = s32[32,30]{1,0:T(8,128)S(1)} copy-done((s32[32,30]{1,0:T(8,128)S(1)}, s32[32,30]{1,0:T(8,128)}, u32[]{:S(2)}) %copy-start.10) | copy-done | bytes 3864
  29.1 0.0 copy-start.3
  29.1 1.2 %copy-done.3 = bf16[30,128,128]{2,1,0:T(8,128)(2,1)S(1)} copy-done((bf16[30,128,128]{2,1,0:T(8,128)(2,1)S(1)}, bf16[30,128,128]{2,1,0:T(8,128)(2,1)}, u32[]{:S(2)}) %copy-start.3) | copy-done | bytes 983064
  30.3 0.4 factors.1
  30.7 0.0 copy-start.7
  30.7 0.8 %copy-done.7 = bf16[32,64,128]{2,1,0:T(8,128)(2,1)} copy-done((bf16[32,64,128]{2,1,0:T(8,128)(2,1)}, bf16[32,64,128]{2,1,0:T(8,128)(2,1)S(1)}, u32[]{:S(2)}) %copy-start.7) | copy-done | bytes 524312
  31.5 1.0 %copy-done.8 = bf16[32,64,128]{2,1,0:T(8,128)(2,1)S(1)} copy-done((bf16[32,64,128]{2,1,0:T(8,128)(2,1)S(1)}, bf16[32,64,128]{2,1,0:T(8,128)(2,1)}, u32[]{:S(2)}) %copy-start.8) | copy-done | bytes 524312
  32.6 8.3 %near.1 = (f32[32,64,128]{2,1,0:T(8,128)S(1)}, bf16[32,64,128]{2,1,0:T(8,128)(2,1)}) custom-call(s32[32,30]{1,0:T(8,128)S(1)} %fusion.1.ids_ref, bf16[64,64,128]{2,1,0:T(8,128)(2,1)S(1)} %get-tuple-element.18.known_ref, bf16[32,64,128]{2,1,0:T(8,128)(2,1)S(1)} %copy-done.8, bf16[30,128,128]{2,1,0:T(8,128)(2,1)S(1)} %get-tuple-element.19.coup_ref, ...), custom_call_target="tpu_custom_call" | custom-call | flops 4026531840 | bytes 8388608 | tf_op jit(solution)/shard_map/near/pallas_call | solution.py:171
  40.8 3.4 %collective-permute-start.2 = (bf16[32,64,128]{2,1,0:T(8,128)(2,1)}, bf16[32,64,128]{2,1,0:T(8,128)(2,1)}, u32[]{:S(2)}, u32[]{:S(2)}) collective-permute-start(bf16[32,64,128]{2,1,0:T(8,128)(2,1)} %get-tuple-element.25), channel_id=1, source_target_pairs={{0,32},{1,33},{2,34},{3,35},{4,36},{5,37},{6,38},{7,39},{8,40},{9,... | collective-permute-start | bytes 1572872 | tf_op jit(solution)/shard_map/ppermute | solution.py:128
  44.2 0.0 copy-start.5
  44.2 0.1 select_reduce_fusion.before_ref
  44.3 0.6 %copy-done.5 = bf16[128,128]{1,0:T(8,128)(2,1)S(1)} copy-done((bf16[128,128]{1,0:T(8,128)(2,1)S(1)}, bf16[128,128]{1,0:T(8,128)(2,1)}, u32[]{:S(2)}) %copy-start.5) | copy-done | bytes 32792
  45.0 0.7 %base.1.base_ref = f32[32,64,128]{2,1,0:T(8,128)S(1)} custom-call(bf16[32,64,128]{2,1,0:T(8,128)(2,1)S(1)} %copy-done.4, f32[32,64,128]{2,1,0:T(8,128)S(1)} %get-tuple-element.22.head_ref, f32[32,64,128]{2,1,0:T(8,128)S(1)} %get-tuple-element.23.running_ref, f32[32,128]{1,0:T(8,128)S(1)} %select_reduce_fusion.before_ref, bf16[128,128]{1,0:T(8,128)(2,1)S(1)} %copy-done.5), custom_call_target="tpu_custom_call" | custom-call | tf_op jit(solution)/shard_map/base/pallas_call | solution.py:193
  45.7 9.2 %collective-permute-done.2.tail_ref = bf16[32,64,128]{2,1,0:T(8,128)(2,1)} collective-permute-done((bf16[32,64,128]{2,1,0:T(8,128)(2,1)}, bf16[32,64,128]{2,1,0:T(8,128)(2,1)}, u32[]{:S(2)}, u32[]{:S(2)}) %collective-permute-start.2) | collective-permute-done | bytes 524320 | tf_op jit(solution)/shard_map/ppermute | solution.py:128
  54.9 2.4 %final.1 = (bf16[32,64,128]{2,1,0:T(8,128)(2,1)}, f32[32,64,128]{2,1,0:T(8,128)}) custom-call(bf16[32,64,128]{2,1,0:T(8,128)(2,1)S(1)} %copy-done.1, f32[32,64,128]{2,1,0:T(8,128)S(1)} %base.1.base_ref, bf16[32,64,128]{2,1,0:T(8,128)(2,1)} %collective-permute-done.2.tail_ref, bf16[32,128,128]{2,1,0:T(8,128)(2,1)S(1)} %copy-done.2), custom_call_target="tpu_custom_call" | custom-call | tf_op jit(solution)/shard_map/final/pallas_call | solution.py:201
  (19 shorter events, 0.1 us)
Async XLA Ops:
  0.6 28.5 %collective-permute-start = (bf16[32,64,128]{2,1,0:T(8,128)(2,1)}, bf16[32,64,128]{2,1,0:T(8,128)(2,1)S(1)}, u32[]{:S(2)}, u32[]{:S(2)}) collective-permute-start(bf16[32,64,128]{2,1,0:T(8,128)(2,1)} %cur_ref.3), channel_id=1, source_target_pairs={{0,1},{1,0},{2,3},{3,2},{4,5},{5,4},{6,7},{7,6},{8,9},{9,8},{10,11... | collective-permute-start | bytes 1572872 | tf_op jit(solution)/shard_map/ppermute | solution.py:128
  2.6 28.2 %collective-permute-start.1 = (bf16[32,64,128]{2,1,0:T(8,128)(2,1)}, bf16[32,64,128]{2,1,0:T(8,128)(2,1)S(1)}, u32[]{:S(2)}, u32[]{:S(2)}) collective-permute-start(bf16[32,64,128]{2,1,0:T(8,128)(2,1)} %cur_ref.3), channel_id=1, source_target_pairs={{0,31},{1,2},{2,1},{3,4},{4,3},{5,6},{6,5},{7,8},{8,7},{9,10},{10,... | collective-permute-start | bytes 1572872 | tf_op jit(solution)/shard_map/ppermute | solution.py:128
  16.5 1.1 %copy-start = (bf16[32,64,128]{2,1,0:T(8,128)(2,1)S(1)}, bf16[32,64,128]{2,1,0:T(8,128)(2,1)}, u32[]{:S(2)}) copy-start(bf16[32,64,128]{2,1,0:T(8,128)(2,1)} %cur_ref.3) | copy-start | bytes 1572868
  17.5 0.8 %copy-start.6 = (bf16[128,128]{1,0:T(8,128)(2,1)S(1)}, bf16[128,128]{1,0:T(8,128)(2,1)}, u32[]{:S(2)}) copy-start(bf16[128,128]{1,0:T(8,128)(2,1)} %map_ref.1) | copy-start | bytes 98308
  18.3 10.8 %copy-start.1 = (bf16[32,64,128]{2,1,0:T(8,128)(2,1)S(1)}, bf16[32,64,128]{2,1,0:T(8,128)(2,1)}, u32[]{:S(2)}) copy-start(bf16[32,64,128]{2,1,0:T(8,128)(2,1)} %cur_ref.3) | copy-start | bytes 1572868
  20.5 7.7 %copy-start.9 = (bf16[30,64]{1,0:T(8,128)(2,1)S(1)}, bf16[30,64]{1,0:T(8,128)(2,1)}, u32[]{:S(2)}) copy-start(bf16[30,64]{1,0:T(8,128)(2,1)} %param.11) | copy-start | bytes 11524
  20.5 23.8 %all-to-all-start = ((f32[16,32,128]{2,1,0:T(8,128)}), f32[16,32,128]{2,1,0:T(8,128)S(1)}, u32[]{:S(2)}, u32[]{:S(2)}) async-start(f32[16,32,128]{2,1,0:T(8,128)} %get-tuple-element.14), calls=%async_computation | async-start | bytes 524288 | tf_op jit(solution)/shard_map/all_to_all | solution.py:157
  28.3 0.7 %copy-start.10 = (s32[32,30]{1,0:T(8,128)S(1)}, s32[32,30]{1,0:T(8,128)}, u32[]{:S(2)}) copy-start(s32[32,30]{1,0:T(8,128)} %param.10) | copy-start | bytes 11524
  29.1 1.2 %copy-start.3 = (bf16[30,128,128]{2,1,0:T(8,128)(2,1)S(1)}, bf16[30,128,128]{2,1,0:T(8,128)(2,1)}, u32[]{:S(2)}) copy-start(bf16[30,128,128]{2,1,0:T(8,128)(2,1)} %coup_ref) | copy-start | bytes 2949124
  30.7 0.8 %copy-start.7 = (bf16[32,64,128]{2,1,0:T(8,128)(2,1)}, bf16[32,64,128]{2,1,0:T(8,128)(2,1)S(1)}, u32[]{:S(2)}) copy-start(bf16[32,64,128]{2,1,0:T(8,128)(2,1)S(1)} %collective-permute-done.1.outer_ref) | copy-start | bytes 1572868
  31.5 1.0 %copy-start.8 = (bf16[32,64,128]{2,1,0:T(8,128)(2,1)S(1)}, bf16[32,64,128]{2,1,0:T(8,128)(2,1)}, u32[]{:S(2)}) copy-start(bf16[32,64,128]{2,1,0:T(8,128)(2,1)} %copy-done.7) | copy-start | bytes 1572868
  32.6 11.8 %copy-start.4 = (bf16[32,64,128]{2,1,0:T(8,128)(2,1)S(1)}, bf16[32,64,128]{2,1,0:T(8,128)(2,1)}, u32[]{:S(2)}) copy-start(bf16[32,64,128]{2,1,0:T(8,128)(2,1)} %exc_ref.1) | copy-start | bytes 1572868
  40.8 14.1 %collective-permute-start.2 = (bf16[32,64,128]{2,1,0:T(8,128)(2,1)}, bf16[32,64,128]{2,1,0:T(8,128)(2,1)}, u32[]{:S(2)}, u32[]{:S(2)}) collective-permute-start(bf16[32,64,128]{2,1,0:T(8,128)(2,1)} %get-tuple-element.25), channel_id=1, source_target_pairs={{0,32},{1,33},{2,34},{3,35},{4,36},{5,37},{6,38},{7,39},{8,40},{9,... | collective-permute-start | bytes 1572872 | tf_op jit(solution)/shard_map/ppermute | solution.py:128
  44.2 0.8 %copy-start.5 = (bf16[128,128]{1,0:T(8,128)(2,1)S(1)}, bf16[128,128]{1,0:T(8,128)(2,1)}, u32[]{:S(2)}) copy-start(bf16[128,128]{1,0:T(8,128)(2,1)} %pot_ref.1) | copy-start | bytes 98308
  45.0 9.9 %copy-start.2 = (bf16[32,128,128]{2,1,0:T(8,128)(2,1)S(1)}, bf16[32,128,128]{2,1,0:T(8,128)(2,1)}, u32[]{:S(2)}) copy-start(bf16[32,128,128]{2,1,0:T(8,128)(2,1)} %inv_ref.1) | copy-start | bytes 3145732

commit v5 on v4

--- a/solution.py
+++ b/solution.py
@@ -7,6 +7,7 @@
 
 F32, BF16 = jnp.float32, jnp.bfloat16
 MIB = 1 << 20
+LANE = 4
 
 
 def whole(space=pltpu.VMEM):
@@ -42,9 +43,11 @@
             totals_ref[t, pl.ds(first, group)] = totals
 
 
-def factor_kernel(lag_ref, coup_ref, own_ref, inner_ref, toep_ref, copy_ref, known_ref):
+def layout_kernel(
+    edge_ref, lag_ref, own_ref, inner_ref, outer_ref, nearer_ref, relayed_ref, field_ref, toep_ref,
+):
+    per_dev, steps, unknowns = own_ref.shape
     slots = lag_ref.shape[0]
-    steps = toep_ref.shape[1] // slots
     lane = lax.broadcasted_iota(jnp.int32, (2 * steps, 2 * steps), 1)
     for p in range(slots // 2):
         even = jnp.broadcast_to(lag_ref[2 * p : 2 * p + 1, :], lane.shape)
@@ -53,22 +56,27 @@
         odd = pltpu.roll(odd, steps, 1, stride=1, stride_axis=0)
         both = jnp.where(lane < steps, even, odd)
         toep_ref[:, p * 2 * steps : (p + 1) * 2 * steps] = both.astype(BF16)
-    copy_ref[...] = coup_ref[...]
-    per_dev = own_ref.shape[0]
-    known_ref[:per_dev] = own_ref[...]
-    known_ref[per_dev:] = inner_ref[...]
+    cut = 2 * per_dev + outer_ref.shape[0]
+    field_ref[:per_dev] = own_ref[...]
+    field_ref[per_dev : 2 * per_dev] = inner_ref[...]
+    field_ref[2 * per_dev : cut] = outer_ref[...]
+    field_ref[3 * per_dev] = jnp.zeros((steps, unknowns), BF16)
+
+    @pl.when(edge_ref[0] > 0)
+    def _():
+        field_ref[cut : 3 * per_dev] = relayed_ref[...]
+
+    @pl.when(edge_ref[0] <= 0)
+    def _():
+        field_ref[cut : 3 * per_dev] = nearer_ref[...]
 
 
 def near_kernel(
-    ids_ref, known_ref, outer_ref, coup_ref, toep_ref,
-    head_ref, tail_ref, field, terms,
+    ids_ref, field, coup_ref, toep_ref, head_ref, tail_ref, terms,
 ):
-    per_dev, steps, unknowns = outer_ref.shape
+    per_dev, steps, unknowns = head_ref.shape
     slots = coup_ref.shape[0]
     group = min(16, per_dev)
-    field[: 2 * per_dev] = known_ref[...]
-    field[2 * per_dev : 3 * per_dev] = outer_ref[...]
-    field[3 * per_dev] = jnp.zeros((steps, unknowns), BF16)
 
     @pl.loop(0, per_dev // group)
     def _(g):
@@ -130,8 +138,33 @@
     def behind(x, by):
         return send(x, lambda t, c: (t + by, c))
 
-    outer = send(currents, lambda t, c: (t, c + 1 if c % 2 else c - 1))
+    lane, half = min(LANE, blocks), peers // 2
+
+    def is_wrap(c):
+        return c % half in (0, half - 1)
+
+    def along(t, c, by):
+        z = (c // half * lane + t % lane + by) % (2 * lane)
+        return t // lane * lane + z % lane, z // lane * half + c % half
+
+    def across(t, c):
+        return t, c + 1 if c % 2 else c - 1
+
+    def opposite(t, c):
+        return t, c // half * half + half - 1 - c % half
+
+    kept = 5 * per_dev // 8
+    outer = send(currents[:kept], across)
+    nearer = send(
+        currents[kept:], lambda t, c: along(t, c, 1) if is_wrap(c) else across(t, c)
+    )
+
     inner = send(currents, lambda t, c: (t, c ^ 1))
+    relayed = send(
+        nearer,
+        lambda t, c: opposite(*along(t, c, lane - 1)) if is_wrap(c) else (blocks, c),
+    )
+    is_edge = ((me % half == 0) | (me % half == half - 1)).astype(jnp.int32).reshape(1)
 
     shape3 = (per_dev, steps, unknowns)
     sds = jax.ShapeDtypeStruct
@@ -154,28 +187,27 @@
     part = jnp.where(owner == me, 0, jnp.where(owner == me ^ 1, 1, 2))
     ids = jnp.where(neighbours >= 0, part * per_dev + neighbours % per_dev, 3 * per_dev)
 
+    lag_rows, running = lax.optimization_barrier((lag_rows, running))
+    totals, nearer = lax.optimization_barrier((totals, nearer))
     pieces = lax.all_to_all(totals, "tm", 0, 0)
-    lag_rows, couplings, running = lax.optimization_barrier((lag_rows, couplings, running))
-    toeplitz, factors, known = pl.pallas_call(
-        factor_kernel,
-        name="factors",
+    field, toeplitz = pl.pallas_call(
+        layout_kernel,
+        name="layout",
         out_shape=(
+            sds((3 * per_dev + 1, steps, unknowns), BF16),
             sds((2 * steps, slots * steps), BF16),
-            sds(couplings.shape, BF16),
-            sds((2 * per_dev, steps, unknowns), BF16),
         ),
-        in_specs=[whole()] * 4,
-        out_specs=(whole(),) * 3,
-        compiler_params=params(16),
-    )(lag_rows, couplings, currents, inner)
+        in_specs=[whole(pltpu.SMEM)] + [whole()] * 6,
+        out_specs=(whole(), whole()),
+        compiler_params=params(16),
+    )(is_edge, lag_rows, currents, inner, outer, nearer, relayed)
     head, tail = pl.pallas_call(
         near_kernel,
         name="near",
         out_shape=(sds(shape3, F32), sds(shape3, BF16)),
-        in_specs=[whole(pltpu.SMEM)] + [whole()] * 4,
+        in_specs=[whole(pltpu.SMEM)] + [whole()] * 3,
         out_specs=(whole(), whole()),
         scratch_shapes=[
-            pltpu.VMEM((3 * per_dev + 1, steps, unknowns), BF16),
             pltpu.VMEM((8, slots * steps, 2 * unknowns), BF16),
         ],
         compiler_params=params(24),
@@ -184,7 +216,7 @@
             bytes_accessed=8 * MIB,
             transcendentals=0,
         ),
-    )(ids, known, outer, factors, toeplitz)
+    )(ids, field, couplings, toeplitz)
 
     tail_before = behind(tail, 1)
     earlier = jnp.arange(blocks) < lax.axis_index("tm")

time: 58 us -> 70.5 us (1.22)
  waiting for transfers between devices: 9.21 us -> 20.1 us
  starting transfers between devices: 26.9 us -> 29.6 us
  local copies, waits for them, and re-layouts: 6.29 us -> 4.63 us
    ppermute x3 -> x5, waiting for transfers between devices: 9.21 us -> 20.1 us  [send(): return lax.ppermute(x, ('tm', 'clus'), pairs)]
    ppermute x3 -> x5, starting transfers between devices: 19.2 us -> 23.8 us  [send(): return lax.ppermute(x, ('tm', 'clus'), pairs)]
    unnamed x22 -> x16, local copies, waits for them, and re-layouts: 6.13 us -> 1.83 us
    all_to_all x1, starting transfers between devices: 7.71 us -> 5.76 us  [on_device(): pieces = lax.all_to_all(totals, 'tm', 0, 0)]
    slice x0 -> x2, local copies, waits for them, and re-layouts: none -> 1.94 us  [the longest x1 1 us: on_device(): outer = send(currents[:kept], across)]
  transfers between devices with their start and end apart: 4 -> 6, of which waited for: 1 -> 2; matrix products, arithmetic and copies ran while one was open for 1% -> 5% of each run, Pallas kernels for 20% -> 16%
where the time goes in v5:
time: 70.5 us; the launch traced here: 69.9 us
  starting transfers between devices  29.6 us (42%)
  waiting for transfers between devices  20.1 us (29%)
  Pallas kernels  13.8 us (20%)
  local copies, waits for them, and re-layouts  4.63 us (7%)
  other arithmetic  0.9 us (1%)
  between operations  0.84 us (1%)
    ppermute x5, starting transfers between devices, send(): return lax.ppermute(x, ('tm', 'clus'), pairs)  23.8 us
    ppermute x5, waiting for transfers between devices, send(): return lax.ppermute(x, ('tm', 'clus'), pairs)  20.1 us
    pallas_call x1, Pallas kernels, on_device(): pl.pallas_call(near_kernel, name='near', out_shape=(sds(shape3, F32), sds...  8.17 us
    all_to_all x1, starting transfers between devices, on_device(): pieces = lax.all_to_all(totals, 'tm', 0, 0)  5.76 us
    pallas_call x1, Pallas kernels, on_device(): pl.pallas_call(final_kernel, name='final', out_shape=(sds(shape3, BF16),...  2.42 us
    pallas_call x1, Pallas kernels, on_device(): pl.pallas_call(prep_kernel, name='prep', out_shape=(sds(shape3, F32), sds...  2.16 us
    unnamed x16, local copies, waits for them, and re-layouts  1.83 us
  transfers between devices with their start and end apart: 6, of which 2 were waited for; matrix products, arithmetic and copies ran while one was open for 5% of the time, Pallas kernels for 16%

profile of v5, /device:TPU:2, one launch (start us, length us, event | category | flops | bytes accessed | tf_op | source)
XLA Modules:
  0.0 69.9 jit_solution(6180754332299221201)
XLA Ops:
  0.6 0.0 copy-start.1
  0.7 2.1 %collective-permute-start.1 = (bf16[32,64,128]{2,1,0:T(8,128)(2,1)}, bf16[32,64,128]{2,1,0:T(8,128)(2,1)S(1)}, u32[]{:S(2)}, u32[]{:S(2)}) collective-permute-start(bf16[32,64,128]{2,1,0:T(8,128)(2,1)} %cur_ref.3), channel_id=1, source_target_pairs={{0,1},{1,0},{2,3},{3,2},{4,5},{5,4},{6,7},{7,6},{8,9},{9,8},{10,11... | collective-permute-start | bytes 1572872 | tf_op jit(solution)/shard_map/ppermute | solution.py:136
  2.7 0.9 %slice.19 = bf16[12,64,128]{2,1,0:T(8,128)(2,1)S(1)} slice(bf16[32,64,128]{2,1,0:T(8,128)(2,1)} %cur_ref.3), slice={[20:32], [0:64], [0:128]} | slice | bytes 393216 | tf_op jit(solution)/shard_map/slice | solution.py:159
  3.7 4.3 %collective-permute-start = (bf16[12,64,128]{2,1,0:T(8,128)(2,1)S(1)}, bf16[12,64,128]{2,1,0:T(8,128)(2,1)S(1)}, u32[]{:S(2)}, u32[]{:S(2)}) collective-permute-start(bf16[12,64,128]{2,1,0:T(8,128)(2,1)S(1)} %slice.19), channel_id=1, source_target_pairs={{0,32},{1,2},{2,1},{3,4},{4,3},{5,6},{6,5},{7,8},{8,7},{9,10},{10,... | collective-permute-start | bytes 589832 | tf_op jit(solution)/shard_map/ppermute | solution.py:136
  7.9 1.0 %slice.23 = bf16[20,64,128]{2,1,0:T(8,128)(2,1)S(1)} slice(bf16[32,64,128]{2,1,0:T(8,128)(2,1)} %cur_ref.3), slice={[0:20], [0:64], [0:128]} | slice | bytes 655360 | tf_op jit(solution)/shard_map/slice | solution.py:157
  8.9 12.7 %collective-permute-start.2 = (bf16[20,64,128]{2,1,0:T(8,128)(2,1)S(1)}, bf16[20,64,128]{2,1,0:T(8,128)(2,1)S(1)}, u32[]{:S(2)}, u32[]{:S(2)}) collective-permute-start(bf16[20,64,128]{2,1,0:T(8,128)(2,1)S(1)} %slice.23), channel_id=1, source_target_pairs={{0,31},{1,2},{2,1},{3,4},{4,3},{5,6},{6,5},{7,8},{8,7},{9,10},{10,... | collective-permute-start | bytes 983048 | tf_op jit(solution)/shard_map/ppermute | solution.py:136
  21.7 0.7 %slice.24 = f32[30,1]{1,0:T(8,128)S(1)} slice(bf16[30,64]{1,0:T(8,128)(2,1)} %param.11), slice={[0:30], [0:1]} | slice | bytes 240 | tf_op jit(solution)/shard_map/jit(_roll_static)/slice | solution.py:173
  22.4 0.7 %convert_element_type.6 = f32[30,64]{1,0:T(8,128)S(1)} convert(bf16[30,64]{1,0:T(8,128)(2,1)} %param.11) | non-fusion elementwise | flops 1920 | bytes 11520 | tf_op jit(solution)/shard_map/convert_element_type | solution.py:172
  23.1 0.1 pad_slice_fusion
  23.2 0.1 slice.22
  23.3 1.0 %copy-done = bf16[32,64,128]{2,1,0:T(8,128)(2,1)S(1)} copy-done((bf16[32,64,128]{2,1,0:T(8,128)(2,1)S(1)}, bf16[32,64,128]{2,1,0:T(8,128)(2,1)}, u32[]{:S(2)}) %copy-start) | copy-done | bytes 524312
  24.3 0.8 %copy-done.5 = bf16[128,128]{1,0:T(8,128)(2,1)S(1)} copy-done((bf16[128,128]{1,0:T(8,128)(2,1)S(1)}, bf16[128,128]{1,0:T(8,128)(2,1)}, u32[]{:S(2)}) %copy-start.5) | copy-done | bytes 32792
  25.1 2.2 %prep.1 = (f32[32,64,128]{2,1,0:T(8,128)S(1)}, f32[16,32,128]{2,1,0:T(8,128)}) custom-call(bf16[32,64,128]{2,1,0:T(8,128)(2,1)S(1)} %copy-done, bf16[128,128]{1,0:T(8,128)(2,1)S(1)} %copy-done.5), custom_call_target="tpu_custom_call" | custom-call | tf_op jit(solution)/shard_map/prep/pallas_call | solution.py:174
  27.2 0.1 pad_maximum_fusion.lag_ref
  27.3 2.8 %collective-permute-start.3 = (bf16[12,64,128]{2,1,0:T(8,128)(2,1)S(1)}, bf16[12,64,128]{2,1,0:T(8,128)(2,1)S(1)}, u32[]{:S(2)}, u32[]{:S(2)}) collective-permute-start(bf16[12,64,128]{2,1,0:T(8,128)(2,1)S(1)} %collective-permute-done.nearer_ref), channel_id=1, source_target_pairs={{0,111},{15,96},{16,127},{31,112},{32,31},{47,16},{48,15},{63,0},{... | collective-permute-start | bytes 589832 | tf_op jit(solution)/shard_map/ppermute | solution.py:136
  30.2 5.8 %all-to-all-start = ((f32[16,32,128]{2,1,0:T(8,128)}), f32[16,32,128]{2,1,0:T(8,128)S(1)}, u32[]{:S(2)}, u32[]{:S(2)}) async-start(f32[16,32,128]{2,1,0:T(8,128)} %get-tuple-element.15), calls=%async_computation | async-start | bytes 524288 | tf_op jit(solution)/shard_map/all_to_all | solution.py:192
  36.0 8.8 %collective-permute-done.3.relayed_ref = bf16[12,64,128]{2,1,0:T(8,128)(2,1)S(1)} collective-permute-done((bf16[12,64,128]{2,1,0:T(8,128)(2,1)S(1)}, bf16[12,64,128]{2,1,0:T(8,128)(2,1)S(1)}, u32[]{:S(2)}, u32[]{:S(2)}) %collective-permute-start.3) | collective-permute-done | bytes 196640 | tf_op jit(solution)/shard_map/ppermute | solution.py:136
  44.8 0.4 layout.1
  45.2 8.2 %near.1 = (f32[32,64,128]{2,1,0:T(8,128)S(1)}, bf16[32,64,128]{2,1,0:T(8,128)(2,1)}) custom-call(s32[32,30]{1,0:T(8,128)S(1)} %fusion.1.ids_ref, bf16[97,64,128]{2,1,0:T(8,128)(2,1)S(1)} %get-tuple-element.19.field, bf16[30,128,128]{2,1,0:T(8,128)(2,1)S(1)} %copy-done.6, bf16[128,1920]{1,0:T(8,128)(2,1)S(1)} %get-tuple-element.20.toep_ref), custom_call_target="tpu_custom_call" | custom-call | flops 4026531840 | bytes 8388608 | tf_op jit(solution)/shard_map/near/pallas_call | solution.py:204
  53.4 1.9 %collective-permute-start.4 = (bf16[32,64,128]{2,1,0:T(8,128)(2,1)}, bf16[32,64,128]{2,1,0:T(8,128)(2,1)}, u32[]{:S(2)}, u32[]{:S(2)}) collective-permute-start(bf16[32,64,128]{2,1,0:T(8,128)(2,1)} %get-tuple-element.25), channel_id=1, source_target_pairs={{0,32},{1,33},{2,34},{3,35},{4,36},{5,37},{6,38},{7,39},{8,40},{9,... | collective-permute-start | bytes 1572872 | tf_op jit(solution)/shard_map/ppermute | solution.py:136
  55.3 0.1 select_reduce_fusion.before_ref
  55.4 0.7 %base.1.base_ref = f32[32,64,128]{2,1,0:T(8,128)S(1)} custom-call(bf16[32,64,128]{2,1,0:T(8,128)(2,1)S(1)} %copy-done.3, f32[32,64,128]{2,1,0:T(8,128)S(1)} %get-tuple-element.22.head_ref, f32[32,64,128]{2,1,0:T(8,128)S(1)} %get-tuple-element.23.running_ref, f32[32,128]{1,0:T(8,128)S(1)} %select_reduce_fusion.before_ref, bf16[128,128]{1,0:T(8,128)(2,1)S(1)} %copy-done.4), custom_call_target="tpu_custom_call" | custom-call | tf_op jit(solution)/shard_map/base/pallas_call | solution.py:225
  56.1 11.3 %collective-permute-done.4.tail_ref = bf16[32,64,128]{2,1,0:T(8,128)(2,1)} collective-permute-done((bf16[32,64,128]{2,1,0:T(8,128)(2,1)}, bf16[32,64,128]{2,1,0:T(8,128)(2,1)}, u32[]{:S(2)}, u32[]{:S(2)}) %collective-permute-start.4) | collective-permute-done | bytes 524320 | tf_op jit(solution)/shard_map/ppermute | solution.py:136
  67.4 2.4 %final.1 = (bf16[32,64,128]{2,1,0:T(8,128)(2,1)}, f32[32,64,128]{2,1,0:T(8,128)}) custom-call(bf16[32,64,128]{2,1,0:T(8,128)(2,1)S(1)} %copy-done.1, f32[32,64,128]{2,1,0:T(8,128)S(1)} %base.1.base_ref, bf16[32,64,128]{2,1,0:T(8,128)(2,1)} %collective-permute-done.4.tail_ref, bf16[32,128,128]{2,1,0:T(8,128)(2,1)S(1)} %copy-done.2), custom_call_target="tpu_custom_call" | custom-call | tf_op jit(solution)/shard_map/final/pallas_call | solution.py:233
  (19 shorter events, 0.1 us)
Async XLA Ops:
  0.6 44.1 %copy-start.1 = (bf16[32,64,128]{2,1,0:T(8,128)(2,1)S(1)}, bf16[32,64,128]{2,1,0:T(8,128)(2,1)}, u32[]{:S(2)}) copy-start(bf16[32,64,128]{2,1,0:T(8,128)(2,1)} %cur_ref.3) | copy-start | bytes 1572868
  0.6 29.5 %copy-start.7 = (s32[32,30]{1,0:T(8,128)S(1)}, s32[32,30]{1,0:T(8,128)}, u32[]{:S(2)}) copy-start(s32[32,30]{1,0:T(8,128)} %param.10) | copy-start | bytes 11524
  0.7 44.1 %collective-permute-start.1 = (bf16[32,64,128]{2,1,0:T(8,128)(2,1)}, bf16[32,64,128]{2,1,0:T(8,128)(2,1)S(1)}, u32[]{:S(2)}, u32[]{:S(2)}) collective-permute-start(bf16[32,64,128]{2,1,0:T(8,128)(2,1)} %cur_ref.3), channel_id=1, source_target_pairs={{0,1},{1,0},{2,3},{3,2},{4,5},{5,4},{6,7},{7,6},{8,9},{9,8},{10,11... | collective-permute-start | bytes 1572872 | tf_op jit(solution)/shard_map/ppermute | solution.py:136
  3.7 23.7 %collective-permute-start = (bf16[12,64,128]{2,1,0:T(8,128)(2,1)S(1)}, bf16[12,64,128]{2,1,0:T(8,128)(2,1)S(1)}, u32[]{:S(2)}, u32[]{:S(2)}) collective-permute-start(bf16[12,64,128]{2,1,0:T(8,128)(2,1)S(1)} %slice.19), channel_id=1, source_target_pairs={{0,32},{1,2},{2,1},{3,4},{4,3},{5,6},{6,5},{7,8},{8,7},{9,10},{10,... | collective-permute-start | bytes 589832 | tf_op jit(solution)/shard_map/ppermute | solution.py:136
  8.9 27.0 %collective-permute-start.2 = (bf16[20,64,128]{2,1,0:T(8,128)(2,1)S(1)}, bf16[20,64,128]{2,1,0:T(8,128)(2,1)S(1)}, u32[]{:S(2)}, u32[]{:S(2)}) collective-permute-start(bf16[20,64,128]{2,1,0:T(8,128)(2,1)S(1)} %slice.23), channel_id=1, source_target_pairs={{0,31},{1,2},{2,1},{3,4},{4,3},{5,6},{6,5},{7,8},{8,7},{9,10},{10,... | collective-permute-start | bytes 983048 | tf_op jit(solution)/shard_map/ppermute | solution.py:136
  23.3 1.0 %copy-start = (bf16[32,64,128]{2,1,0:T(8,128)(2,1)S(1)}, bf16[32,64,128]{2,1,0:T(8,128)(2,1)}, u32[]{:S(2)}) copy-start(bf16[32,64,128]{2,1,0:T(8,128)(2,1)} %cur_ref.3) | copy-start | bytes 1572868
  24.3 0.8 %copy-start.5 = (bf16[128,128]{1,0:T(8,128)(2,1)S(1)}, bf16[128,128]{1,0:T(8,128)(2,1)}, u32[]{:S(2)}) copy-start(bf16[128,128]{1,0:T(8,128)(2,1)} %map_ref.1) | copy-start | bytes 98308
  27.3 17.4 %collective-permute-start.3 = (bf16[12,64,128]{2,1,0:T(8,128)(2,1)S(1)}, bf16[12,64,128]{2,1,0:T(8,128)(2,1)S(1)}, u32[]{:S(2)}, u32[]{:S(2)}) collective-permute-start(bf16[12,64,128]{2,1,0:T(8,128)(2,1)S(1)} %collective-permute-done.nearer_ref), channel_id=1, source_target_pairs={{0,111},{15,96},{16,127},{31,112},{32,31},{47,16},{48,15},{63,0},{... | collective-permute-start | bytes 589832 | tf_op jit(solution)/shard_map/ppermute | solution.py:136
  30.2 25.1 %all-to-all-start = ((f32[16,32,128]{2,1,0:T(8,128)}), f32[16,32,128]{2,1,0:T(8,128)S(1)}, u32[]{:S(2)}, u32[]{:S(2)}) async-start(f32[16,32,128]{2,1,0:T(8,128)} %get-tuple-element.15), calls=%async_computation | async-start | bytes 524288 | tf_op jit(solution)/shard_map/all_to_all | solution.py:192
  36.0 9.2 %copy-start.6 = (bf16[30,128,128]{2,1,0:T(8,128)(2,1)S(1)}, bf16[30,128,128]{2,1,0:T(8,128)(2,1)}, u32[]{:S(2)}) copy-start(bf16[30,128,128]{2,1,0:T(8,128)(2,1)} %coup_ref.1) | copy-start | bytes 2949124
  45.2 10.2 %copy-start.3 = (bf16[32,64,128]{2,1,0:T(8,128)(2,1)S(1)}, bf16[32,64,128]{2,1,0:T(8,128)(2,1)}, u32[]{:S(2)}) copy-start(bf16[32,64,128]{2,1,0:T(8,128)(2,1)} %exc_ref.1) | copy-start | bytes 1572868
  45.2 10.2 %copy-start.4 = (bf16[128,128]{1,0:T(8,128)(2,1)S(1)}, bf16[128,128]{1,0:T(8,128)(2,1)}, u32[]{:S(2)}) copy-start(bf16[128,128]{1,0:T(8,128)(2,1)} %pot_ref.1) | copy-start | bytes 98308
  53.4 14.1 %collective-permute-start.4 = (bf16[32,64,128]{2,1,0:T(8,128)(2,1)}, bf16[32,64,128]{2,1,0:T(8,128)(2,1)}, u32[]{:S(2)}, u32[]{:S(2)}) collective-permute-start(bf16[32,64,128]{2,1,0:T(8,128)(2,1)} %get-tuple-element.25), channel_id=1, source_target_pairs={{0,32},{1,33},{2,34},{3,35},{4,36},{5,37},{6,38},{7,39},{8,40},{9,... | collective-permute-start | bytes 1572872 | tf_op jit(solution)/shard_map/ppermute | solution.py:136
  55.4 12.0 %copy-start.2 = (bf16[32,128,128]{2,1,0:T(8,128)(2,1)S(1)}, bf16[32,128,128]{2,1,0:T(8,128)(2,1)}, u32[]{:S(2)}) copy-start(bf16[32,128,128]{2,1,0:T(8,128)(2,1)} %inv_ref.1) | copy-start | bytes 3145732

commit v6 on v4

--- a/solution.py
+++ b/solution.py
@@ -42,9 +42,9 @@
             totals_ref[t, pl.ds(first, group)] = totals
 
 
-def factor_kernel(lag_ref, coup_ref, own_ref, inner_ref, toep_ref, copy_ref, known_ref):
+def layout_kernel(lag_ref, own_ref, inner_ref, outer_ref, field_ref, toep_ref):
+    per_dev, steps, unknowns = own_ref.shape
     slots = lag_ref.shape[0]
-    steps = toep_ref.shape[1] // slots
     lane = lax.broadcasted_iota(jnp.int32, (2 * steps, 2 * steps), 1)
     for p in range(slots // 2):
         even = jnp.broadcast_to(lag_ref[2 * p : 2 * p + 1, :], lane.shape)
@@ -53,22 +53,17 @@
         odd = pltpu.roll(odd, steps, 1, stride=1, stride_axis=0)
         both = jnp.where(lane < steps, even, odd)
         toep_ref[:, p * 2 * steps : (p + 1) * 2 * steps] = both.astype(BF16)
-    copy_ref[...] = coup_ref[...]
-    per_dev = own_ref.shape[0]
-    known_ref[:per_dev] = own_ref[...]
-    known_ref[per_dev:] = inner_ref[...]
+    for part, ref in enumerate((own_ref, inner_ref, outer_ref)):
+        field_ref[part * per_dev : (part + 1) * per_dev] = ref[...]
+    field_ref[3 * per_dev] = jnp.zeros((steps, unknowns), BF16)
 
 
 def near_kernel(
-    ids_ref, known_ref, outer_ref, coup_ref, toep_ref,
-    head_ref, tail_ref, field, terms,
+    ids_ref, field, coup_ref, toep_ref, head_ref, tail_ref, terms,
 ):
-    per_dev, steps, unknowns = outer_ref.shape
+    per_dev, steps, unknowns = head_ref.shape
     slots = coup_ref.shape[0]
     group = min(16, per_dev)
-    field[: 2 * per_dev] = known_ref[...]
-    field[2 * per_dev : 3 * per_dev] = outer_ref[...]
-    field[3 * per_dev] = jnp.zeros((steps, unknowns), BF16)
 
     @pl.loop(0, per_dev // group)
     def _(g):
@@ -132,7 +127,6 @@
 
     outer = send(currents, lambda t, c: (t, c + 1 if c % 2 else c - 1))
     inner = send(currents, lambda t, c: (t, c ^ 1))
-
     shape3 = (per_dev, steps, unknowns)
     sds = jax.ShapeDtypeStruct
     params = lambda mib: pltpu.CompilerParams(vmem_limit_bytes=mib * MIB)
@@ -154,28 +148,26 @@
     part = jnp.where(owner == me, 0, jnp.where(owner == me ^ 1, 1, 2))
     ids = jnp.where(neighbours >= 0, part * per_dev + neighbours % per_dev, 3 * per_dev)
 
+    lag_rows, running = lax.optimization_barrier((lag_rows, running))
     pieces = lax.all_to_all(totals, "tm", 0, 0)
-    lag_rows, couplings, running = lax.optimization_barrier((lag_rows, couplings, running))
-    toeplitz, factors, known = pl.pallas_call(
-        factor_kernel,
-        name="factors",
+    field, toeplitz = pl.pallas_call(
+        layout_kernel,
+        name="layout",
         out_shape=(
+            sds((3 * per_dev + 1, steps, unknowns), BF16),
             sds((2 * steps, slots * steps), BF16),
-            sds(couplings.shape, BF16),
-            sds((2 * per_dev, steps, unknowns), BF16),
         ),
         in_specs=[whole()] * 4,
-        out_specs=(whole(),) * 3,
-        compiler_params=params(16),
-    )(lag_rows, couplings, currents, inner)
+        out_specs=(whole(), whole()),
+        compiler_params=params(16),
+    )(lag_rows, currents, inner, outer)
     head, tail = pl.pallas_call(
         near_kernel,
         name="near",
         out_shape=(sds(shape3, F32), sds(shape3, BF16)),
-        in_specs=[whole(pltpu.SMEM)] + [whole()] * 4,
+        in_specs=[whole(pltpu.SMEM)] + [whole()] * 3,
         out_specs=(whole(), whole()),
         scratch_shapes=[
-            pltpu.VMEM((3 * per_dev + 1, steps, unknowns), BF16),
             pltpu.VMEM((8, slots * steps, 2 * unknowns), BF16),
         ],
         compiler_params=params(24),
@@ -184,12 +176,15 @@
             bytes_accessed=8 * MIB,
             transcendentals=0,
         ),
-    )(ids, known, outer, factors, toeplitz)
+    )(ids, field, couplings, toeplitz)
 
     tail_before = behind(tail, 1)
     earlier = jnp.arange(blocks) < lax.axis_index("tm")
     pieces, head = lax.optimization_barrier((pieces, head))
     before = jnp.sum(jnp.where(earlier[:, None, None], pieces, 0.0), axis=0)
+    def piece(rows):
+        return pl.BlockSpec((per_dev // 4, rows, unknowns), lambda i: (i, 0, 0))
+
     base = pl.pallas_call(
         base_kernel,
         name="base",
@@ -202,8 +197,9 @@
         final_kernel,
         name="final",
         out_shape=(sds(shape3, BF16), sds(shape3, F32)),
-        in_specs=[whole()] * 4,
-        out_specs=(whole(), whole()),
+        grid=(4,),
+        in_specs=[piece(steps)] * 3 + [piece(unknowns)],
+        out_specs=(piece(steps), piece(steps)),
         compiler_params=params(16),
     )(currents, base, tail_before, block_inverses)
 

time: 58 us -> 61.2 us (1.055)
  waiting for transfers between devices: 9.21 us -> 14.4 us
  local copies, waits for them, and re-layouts: 6.29 us -> 2.67 us
  other arithmetic: 0.2 us -> 1.7 us
  Pallas kernels: 13.9 us -> 15 us
  starting transfers between devices: 26.9 us -> 26.1 us
    ppermute x3, waiting for transfers between devices: 9.21 us -> 14.4 us  [send(): return lax.ppermute(x, ('tm', 'clus'), pairs)]
    unnamed x22 -> x14, local copies, waits for them, and re-layouts: 6.13 us -> 1.82 us
    pallas_call x1, Pallas kernels: 2.42 us -> 3.56 us  [on_device(): pl.pallas_call(final_kernel, name='final', out_shape=(sds(shape3, BF16),...]
    select_n x1, other arithmetic: 0.03 us -> 0.83 us  [on_device(): jnp.where(neighbours >= 0, part * per_dev + neighbours % per_dev, 3 * per...]
    slice x3, local copies, waits for them, and re-layouts: 0.15 us -> 0.85 us  [on_device(): lag_rows = jnp.roll(lag_rows[:, ::-1], 1, axis=1)]
    convert_element_type x1, other arithmetic: 0.01 us -> 0.7 us  [on_device(): lag_rows = jnp.pad(lag_profile.astype(F32), ((0, 0), (0, 2 * steps - lags)))]
    ppermute x3, starting transfers between devices: 19.2 us -> 18.5 us  [send(): return lax.ppermute(x, ('tm', 'clus'), pairs)]
  transfers between devices with their start and end apart: 4 -> 4, of which waited for: 1 -> 1; matrix products, arithmetic and copies ran while one was open for 1% -> 4% of each run, Pallas kernels for 20% -> 19%
where the time goes in v6:
time: 61.2 us; the launch traced here: 60.7 us
  starting transfers between devices  26.1 us (43%)
  Pallas kernels  15 us (25%)
  waiting for transfers between devices  14.4 us (24%)
  local copies, waits for them, and re-layouts  2.67 us (4%)
  other arithmetic  1.7 us (3%)
  between operations  0.78 us (1%)
    ppermute x3, starting transfers between devices, send(): return lax.ppermute(x, ('tm', 'clus'), pairs)  18.5 us
    ppermute x3, waiting for transfers between devices, send(): return lax.ppermute(x, ('tm', 'clus'), pairs)  14.4 us
    pallas_call x1, Pallas kernels, on_device(): pl.pallas_call(near_kernel, name='near', out_shape=(sds(shape3, F32), sds...  8.17 us
    all_to_all x1, starting transfers between devices, on_device(): pieces = lax.all_to_all(totals, 'tm', 0, 0)  7.58 us
    pallas_call x1, Pallas kernels, on_device(): pl.pallas_call(final_kernel, name='final', out_shape=(sds(shape3, BF16),...  3.56 us
    pallas_call x1, Pallas kernels, on_device(): pl.pallas_call(prep_kernel, name='prep', out_shape=(sds(shape3, F32), sds...  2.15 us
    unnamed x14, local copies, waits for them, and re-layouts  1.82 us
  transfers between devices with their start and end apart: 4, of which 1 were waited for; matrix products, arithmetic and copies ran while one was open for 4% of the time, Pallas kernels for 19%

profile of v6, /device:TPU:2, one launch (start us, length us, event | category | flops | bytes accessed | tf_op | source)
XLA Modules:
  0.0 60.7 jit_solution(6750696359608694491)
XLA Ops:
  0.6 13.3 %collective-permute-start.1 = (bf16[32,64,128]{2,1,0:T(8,128)(2,1)}, bf16[32,64,128]{2,1,0:T(8,128)(2,1)S(1)}, u32[]{:S(2)}, u32[]{:S(2)}) collective-permute-start(bf16[32,64,128]{2,1,0:T(8,128)(2,1)} %cur_ref.3), channel_id=1, source_target_pairs={{0,31},{1,2},{2,1},{3,4},{4,3},{5,6},{6,5},{7,8},{8,7},{9,10},{10,... | collective-permute-start | bytes 1572872 | tf_op jit(solution)/shard_map/ppermute | solution.py:123
  13.9 1.9 %collective-permute-start = (bf16[32,64,128]{2,1,0:T(8,128)(2,1)}, bf16[32,64,128]{2,1,0:T(8,128)(2,1)S(1)}, u32[]{:S(2)}, u32[]{:S(2)}) collective-permute-start(bf16[32,64,128]{2,1,0:T(8,128)(2,1)} %cur_ref.3), channel_id=1, source_target_pairs={{0,1},{1,0},{2,3},{3,2},{4,5},{5,4},{6,7},{7,6},{8,9},{9,8},{10,11... | collective-permute-start | bytes 1572872 | tf_op jit(solution)/shard_map/ppermute | solution.py:123
  15.8 1.0 %copy-done = bf16[32,64,128]{2,1,0:T(8,128)(2,1)S(1)} copy-done((bf16[32,64,128]{2,1,0:T(8,128)(2,1)S(1)}, bf16[32,64,128]{2,1,0:T(8,128)(2,1)}, u32[]{:S(2)}) %copy-start) | copy-done | bytes 524312
  16.9 0.8 %copy-done.5 = bf16[128,128]{1,0:T(8,128)(2,1)S(1)} copy-done((bf16[128,128]{1,0:T(8,128)(2,1)S(1)}, bf16[128,128]{1,0:T(8,128)(2,1)}, u32[]{:S(2)}) %copy-start.5) | copy-done | bytes 32792
  17.6 2.2 %prep.1 = (f32[32,64,128]{2,1,0:T(8,128)S(1)}, f32[16,32,128]{2,1,0:T(8,128)}) custom-call(bf16[32,64,128]{2,1,0:T(8,128)(2,1)S(1)} %copy-done, bf16[128,128]{1,0:T(8,128)(2,1)S(1)} %copy-done.5), custom_call_target="tpu_custom_call" | custom-call | tf_op jit(solution)/shard_map/prep/pallas_call | solution.py:135
  19.8 7.6 %all-to-all-start = ((f32[16,32,128]{2,1,0:T(8,128)}), f32[16,32,128]{2,1,0:T(8,128)S(1)}, u32[]{:S(2)}, u32[]{:S(2)}) async-start(f32[16,32,128]{2,1,0:T(8,128)} %get-tuple-element.12), calls=%async_computation | async-start | bytes 524288 | tf_op jit(solution)/shard_map/all_to_all | solution.py:152
  27.4 0.7 %slice.16 = f32[30,1]{1,0:T(8,128)S(1)} slice(bf16[30,64]{1,0:T(8,128)(2,1)} %param.11), slice={[0:30], [0:1]} | slice | bytes 240 | tf_op jit(solution)/shard_map/jit(_roll_static)/slice | solution.py:134
  28.1 0.7 %convert_element_type.5 = f32[30,64]{1,0:T(8,128)S(1)} convert(bf16[30,64]{1,0:T(8,128)(2,1)} %param.11) | non-fusion elementwise | flops 1920 | bytes 11520 | tf_op jit(solution)/shard_map/convert_element_type | solution.py:133
  28.8 0.1 pad_slice_fusion
  28.8 0.1 slice.15
  28.9 0.1 pad_maximum_fusion.lag_ref
  29.0 0.8 %fusion.1.ids_ref = s32[32,30]{1,0:T(8,128)S(1)} fusion(s32[32,30]{1,0:T(8,128)} %param.10, s32[]{:T(128)S(6)} %xor.3, s32[]{:T(128)S(6)} %axis_index.22), kind=kLoop, calls=%fused_computation.7 | loop fusion | flops 25920 | bytes 7688 | tf_op jit(solution)/shard_map/jit(_where)/select_n | solution.py:149
  29.8 0.0 collective-permute-done.1.outer_ref
  29.8 0.0 collective-permute-done.inner_ref
  29.9 0.4 layout.1
  30.2 0.0 copy-start.3
  30.3 0.0 copy-start.4
  30.3 8.2 %near.1 = (f32[32,64,128]{2,1,0:T(8,128)S(1)}, bf16[32,64,128]{2,1,0:T(8,128)(2,1)}) custom-call(s32[32,30]{1,0:T(8,128)S(1)} %fusion.1.ids_ref, bf16[97,64,128]{2,1,0:T(8,128)(2,1)S(1)} %get-tuple-element.15.field, bf16[30,128,128]{2,1,0:T(8,128)(2,1)S(1)} %copy-done.6, bf16[128,1920]{1,0:T(8,128)(2,1)S(1)} %get-tuple-element.16.toep_ref), custom_call_target="tpu_custom_call" | custom-call | flops 4026531840 | bytes 8388608 | tf_op jit(solution)/shard_map/near/pallas_call | solution.py:164
  38.4 3.4 %collective-permute-start.2 = (bf16[32,64,128]{2,1,0:T(8,128)(2,1)}, bf16[32,64,128]{2,1,0:T(8,128)(2,1)}, u32[]{:S(2)}, u32[]{:S(2)}) collective-permute-start(bf16[32,64,128]{2,1,0:T(8,128)(2,1)} %get-tuple-element.21), channel_id=1, source_target_pairs={{0,32},{1,33},{2,34},{3,35},{4,36},{5,37},{6,38},{7,39},{8,40},{9,... | collective-permute-start | bytes 1572872 | tf_op jit(solution)/shard_map/ppermute | solution.py:123
  41.8 0.1 select_reduce_fusion.before_ref
  41.9 0.0 copy-start.2
  42.0 0.7 %base.1.base_ref = f32[32,64,128]{2,1,0:T(8,128)S(1)} custom-call(bf16[32,64,128]{2,1,0:T(8,128)(2,1)S(1)} %copy-done.3, f32[32,64,128]{2,1,0:T(8,128)S(1)} %get-tuple-element.18.head_ref, f32[32,64,128]{2,1,0:T(8,128)S(1)} %get-tuple-element.19.running_ref, f32[32,128]{1,0:T(8,128)S(1)} %select_reduce_fusion.before_ref, bf16[128,128]{1,0:T(8,128)(2,1)S(1)} %copy-done.4), custom_call_target="tpu_custom_call" | custom-call | tf_op jit(solution)/shard_map/base/pallas_call | solution.py:188
  42.7 14.4 %collective-permute-done.2.tail_ref = bf16[32,64,128]{2,1,0:T(8,128)(2,1)} collective-permute-done((bf16[32,64,128]{2,1,0:T(8,128)(2,1)}, bf16[32,64,128]{2,1,0:T(8,128)(2,1)}, u32[]{:S(2)}, u32[]{:S(2)}) %collective-permute-start.2) | collective-permute-done | bytes 524320 | tf_op jit(solution)/shard_map/ppermute | solution.py:123
  57.1 3.6 %final.1 = (bf16[32,64,128]{2,1,0:T(8,128)(2,1)}, f32[32,64,128]{2,1,0:T(8,128)}) custom-call(bf16[32,64,128]{2,1,0:T(8,128)(2,1)S(1)} %copy-done.1, f32[32,64,128]{2,1,0:T(8,128)S(1)} %base.1.base_ref, bf16[32,64,128]{2,1,0:T(8,128)(2,1)} %collective-permute-done.2.tail_ref, bf16[32,128,128]{2,1,0:T(8,128)(2,1)S(1)} %copy-done.2), custom_call_target="tpu_custom_call" | custom-call | tf_op jit(solution)/shard_map/final/pallas_call | solution.py:196
  (11 shorter events, 0.0 us)
Async XLA Ops:
  0.6 29.2 %collective-permute-start.1 = (bf16[32,64,128]{2,1,0:T(8,128)(2,1)}, bf16[32,64,128]{2,1,0:T(8,128)(2,1)S(1)}, u32[]{:S(2)}, u32[]{:S(2)}) collective-permute-start(bf16[32,64,128]{2,1,0:T(8,128)(2,1)} %cur_ref.3), channel_id=1, source_target_pairs={{0,31},{1,2},{2,1},{3,4},{4,3},{5,6},{6,5},{7,8},{8,7},{9,10},{10,... | collective-permute-start | bytes 1572872 | tf_op jit(solution)/shard_map/ppermute | solution.py:123
  13.9 15.9 %collective-permute-start = (bf16[32,64,128]{2,1,0:T(8,128)(2,1)}, bf16[32,64,128]{2,1,0:T(8,128)(2,1)S(1)}, u32[]{:S(2)}, u32[]{:S(2)}) collective-permute-start(bf16[32,64,128]{2,1,0:T(8,128)(2,1)} %cur_ref.3), channel_id=1, source_target_pairs={{0,1},{1,0},{2,3},{3,2},{4,5},{5,4},{6,7},{7,6},{8,9},{9,8},{10,11... | collective-permute-start | bytes 1572872 | tf_op jit(solution)/shard_map/ppermute | solution.py:123
  15.8 1.0 %copy-start = (bf16[32,64,128]{2,1,0:T(8,128)(2,1)S(1)}, bf16[32,64,128]{2,1,0:T(8,128)(2,1)}, u32[]{:S(2)}) copy-start(bf16[32,64,128]{2,1,0:T(8,128)(2,1)} %cur_ref.3) | copy-start | bytes 1572868
  16.9 0.8 %copy-start.5 = (bf16[128,128]{1,0:T(8,128)(2,1)S(1)}, bf16[128,128]{1,0:T(8,128)(2,1)}, u32[]{:S(2)}) copy-start(bf16[128,128]{1,0:T(8,128)(2,1)} %map_ref.1) | copy-start | bytes 98308
  17.6 12.2 %copy-start.1 = (bf16[32,64,128]{2,1,0:T(8,128)(2,1)S(1)}, bf16[32,64,128]{2,1,0:T(8,128)(2,1)}, u32[]{:S(2)}) copy-start(bf16[32,64,128]{2,1,0:T(8,128)(2,1)} %cur_ref.3) | copy-start | bytes 1572868
  19.8 22.0 %all-to-all-start = ((f32[16,32,128]{2,1,0:T(8,128)}), f32[16,32,128]{2,1,0:T(8,128)S(1)}, u32[]{:S(2)}, u32[]{:S(2)}) async-start(f32[16,32,128]{2,1,0:T(8,128)} %get-tuple-element.12), calls=%async_computation | async-start | bytes 524288 | tf_op jit(solution)/shard_map/all_to_all | solution.py:152
  29.0 1.2 %copy-start.6 = (bf16[30,128,128]{2,1,0:T(8,128)(2,1)S(1)}, bf16[30,128,128]{2,1,0:T(8,128)(2,1)}, u32[]{:S(2)}) copy-start(bf16[30,128,128]{2,1,0:T(8,128)(2,1)} %coup_ref.1) | copy-start | bytes 2949124
  30.2 11.7 %copy-start.3 = (bf16[32,64,128]{2,1,0:T(8,128)(2,1)S(1)}, bf16[32,64,128]{2,1,0:T(8,128)(2,1)}, u32[]{:S(2)}) copy-start(bf16[32,64,128]{2,1,0:T(8,128)(2,1)} %exc_ref.1) | copy-start | bytes 1572868
  30.3 11.7 %copy-start.4 = (bf16[128,128]{1,0:T(8,128)(2,1)S(1)}, bf16[128,128]{1,0:T(8,128)(2,1)}, u32[]{:S(2)}) copy-start(bf16[128,128]{1,0:T(8,128)(2,1)} %pot_ref.1) | copy-start | bytes 98308
  38.4 18.7 %collective-permute-start.2 = (bf16[32,64,128]{2,1,0:T(8,128)(2,1)}, bf16[32,64,128]{2,1,0:T(8,128)(2,1)}, u32[]{:S(2)}, u32[]{:S(2)}) collective-permute-start(bf16[32,64,128]{2,1,0:T(8,128)(2,1)} %get-tuple-element.21), channel_id=1, source_target_pairs={{0,32},{1,33},{2,34},{3,35},{4,36},{5,37},{6,38},{7,39},{8,40},{9,... | collective-permute-start | bytes 1572872 | tf_op jit(solution)/shard_map/ppermute | solution.py:123
  41.9 15.2 %copy-start.2 = (bf16[32,128,128]{2,1,0:T(8,128)(2,1)S(1)}, bf16[32,128,128]{2,1,0:T(8,128)(2,1)}, u32[]{:S(2)}) copy-start(bf16[32,128,128]{2,1,0:T(8,128)(2,1)} %inv_ref.1) | copy-start | bytes 3145732

commit v7 on v6

--- a/solution.py
+++ b/solution.py
@@ -1,3 +1,5 @@
+import functools
+
 import jax
 import jax.numpy as jnp
 from jax import lax
@@ -59,17 +61,17 @@
 
 
 def near_kernel(
-    ids_ref, field, coup_ref, toep_ref, head_ref, tail_ref, terms,
+    start, ids_ref, field, coup_ref, toep_ref, head_ref, tail_ref, terms,
 ):
-    per_dev, steps, unknowns = head_ref.shape
+    count, steps, unknowns = head_ref.shape
     slots = coup_ref.shape[0]
-    group = min(16, per_dev)
-
-    @pl.loop(0, per_dev // group)
+    group = min(16, count)
+
+    @pl.loop(0, count // group)
     def _(g):
         first = g * group
         for k in range(slots):
-            rows = [field[ids_ref[first + i, k]] for i in range(group)]
+            rows = [field[ids_ref[start + first + i, k]] for i in range(group)]
             z = dot(jnp.concatenate(rows, axis=0), coup_ref[k]).astype(BF16)
             at = slice(k * steps, (k + 1) * steps)
             for i in range(group):
@@ -83,20 +85,20 @@
                 tail_ref[first + i + j] = out[steps:, lanes].astype(BF16)
 
 
-def base_kernel(exc_ref, head_ref, running_ref, before_ref, pot_ref, base_ref):
+def base_kernel(exc_ref, low_ref, high_ref, running_ref, before_ref, pot_ref, base_ref):
     per_dev, steps, unknowns = exc_ref.shape
-    group = 8
-
-    @pl.loop(0, per_dev // group)
-    def _(g):
-        at = pl.ds(g * group, group)
+    group = per_dev // 4
+    for g in range(4):
+        at = slice(g * group, (g + 1) * group)
+        head = (low_ref, high_ref)[g // 2][g % 2 * group : (g % 2 + 1) * group]
         charge = (running_ref[at] + before_ref[at][:, None, :]).astype(BF16)
         field = dot(charge.reshape(group * steps, -1), pot_ref[...])
         field = field.reshape(group, steps, unknowns)
-        base_ref[at] = exc_ref[at].astype(F32) - head_ref[at] - field
-
-
-def final_kernel(cur_ref, base_ref, tail_ref, inv_ref, updated_ref, residual_ref):
+        base_ref[at] = exc_ref[at].astype(F32) - head - field
+
+
+def final_kernel(cur_ref, base_ref, tail_ref, inv_ref, *refs):
+    updated_ref, residual_ref = refs[-2:]
     for i in range(cur_ref.shape[0]):
         residual = base_ref[i] - tail_ref[i].astype(F32)
         residual_ref[i] = residual
@@ -161,47 +163,53 @@
         out_specs=(whole(), whole()),
         compiler_params=params(16),
     )(lag_rows, currents, inner, outer)
-    head, tail = pl.pallas_call(
-        near_kernel,
-        name="near",
-        out_shape=(sds(shape3, F32), sds(shape3, BF16)),
-        in_specs=[whole(pltpu.SMEM)] + [whole()] * 3,
-        out_specs=(whole(), whole()),
-        scratch_shapes=[
-            pltpu.VMEM((8, slots * steps, 2 * unknowns), BF16),
-        ],
-        compiler_params=params(24),
-        cost_estimate=pl.CostEstimate(
-            flops=2 * per_dev * slots * steps * unknowns * (unknowns + 2 * steps),
-            bytes_accessed=8 * MIB,
-            transcendentals=0,
-        ),
-    )(ids, field, couplings, toeplitz)
-
-    tail_before = behind(tail, 1)
+    part = per_dev // 2
+    heads, tails = [], []
+    for h in range(2):
+        head, tail = pl.pallas_call(
+            functools.partial(near_kernel, h * part),
+            name="near",
+            out_shape=(sds((part, steps, unknowns), F32), sds((part, steps, unknowns), BF16)),
+            in_specs=[whole(pltpu.SMEM)] + [whole()] * 3,
+            out_specs=(whole(), whole()),
+            scratch_shapes=[pltpu.VMEM((8, slots * steps, 2 * unknowns), BF16)],
+            compiler_params=params(24),
+            cost_estimate=pl.CostEstimate(
+                flops=2 * part * slots * steps * unknowns * (unknowns + 2 * steps),
+                bytes_accessed=4 * MIB,
+                transcendentals=0,
+            ),
+        )(ids, field, couplings, toeplitz)
+        ids, head = lax.optimization_barrier((ids, head))
+        heads.append(head)
+        tails.append(behind(tail, 1))
     earlier = jnp.arange(blocks) < lax.axis_index("tm")
-    pieces, head = lax.optimization_barrier((pieces, head))
+    pieces, heads[1] = lax.optimization_barrier((pieces, heads[1]))
     before = jnp.sum(jnp.where(earlier[:, None, None], pieces, 0.0), axis=0)
-    def piece(rows):
-        return pl.BlockSpec((per_dev // 4, rows, unknowns), lambda i: (i, 0, 0))
-
     base = pl.pallas_call(
         base_kernel,
         name="base",
         out_shape=sds(shape3, F32),
-        in_specs=[whole()] * 5,
+        in_specs=[whole()] * 6,
         out_specs=whole(),
         compiler_params=params(16),
-    )(excitation, head, running, before, potential)
-    return pl.pallas_call(
-        final_kernel,
-        name="final",
-        out_shape=(sds(shape3, BF16), sds(shape3, F32)),
-        grid=(4,),
-        in_specs=[piece(steps)] * 3 + [piece(unknowns)],
-        out_specs=(piece(steps), piece(steps)),
-        compiler_params=params(16),
-    )(currents, base, tail_before, block_inverses)
+    )(excitation, *heads, running, before, potential)
+    done = ()
+    for h in range(2):
+        at = lambda i, h=h: (h, 0, 0)
+        mine = pl.BlockSpec((part, steps, unknowns), at)
+        done = pl.pallas_call(
+            final_kernel,
+            name="final",
+            grid=(1,),
+            out_shape=(sds(shape3, BF16), sds(shape3, F32)),
+            in_specs=[mine, mine, whole(), pl.BlockSpec((part, unknowns, unknowns), at)]
+            + [whole(pl.ANY)] * len(done),
+            out_specs=(mine, mine),
+            input_output_aliases={4: 0, 5: 1} if done else {},
+            compiler_params=params(16),
+        )(currents, base, tails[h], block_inverses, *done)
+    return done
 
 
 def solution(mesh):

time: 61.2 us -> 57.6 us (0.941)
  waiting for transfers between devices: 14.4 us -> 5.15 us
  starting transfers between devices: 26.1 us -> 29.6 us
  other arithmetic: 1.7 us -> 2.65 us
  local copies, waits for them, and re-layouts: 2.67 us -> 3.46 us
    ppermute x3 -> x4, waiting for transfers between devices: 14.4 us -> 5.15 us  [send(): return lax.ppermute(x, ('tm', 'clus'), pairs)]
    ppermute x3 -> x4, starting transfers between devices: 18.5 us -> 22 us  [send(): return lax.ppermute(x, ('tm', 'clus'), pairs)]
    reduce_sum x1, other arithmetic: 0.09 us -> 1.04 us  [on_device(): before = jnp.sum(jnp.where(earlier[:, None, None], pieces, 0.0), axis=0)]
    pallas_call x2 -> x4, Pallas kernels: 11.7 us -> 12.5 us  [the longest x2 9.58 us: on_device(): pl.pallas_call(functools.partial(near_kernel, h * part), name='near', out...]
    unnamed x14, local copies, waits for them, and re-layouts: 1.82 us -> 2.61 us
  transfers between devices with their start and end apart: 4 -> 5, of which waited for: 1 -> 2; matrix products, arithmetic and copies ran while one was open for 4% -> 6% of each run, Pallas kernels for 19% -> 25%
where the time goes in v7:
time: 57.6 us; the launch traced here: 57 us
  starting transfers between devices  29.6 us (51%)
  Pallas kernels  15.3 us (27%)
  waiting for transfers between devices  5.15 us (9%)
  local copies, waits for them, and re-layouts  3.46 us (6%)
  other arithmetic  2.65 us (5%)
  between operations  0.78 us (1%)
    ppermute x4, starting transfers between devices, send(): return lax.ppermute(x, ('tm', 'clus'), pairs)  22 us
    pallas_call x2, Pallas kernels, on_device(): pl.pallas_call(functools.partial(near_kernel, h * part), name='near', out...  9.58 us
    all_to_all x1, starting transfers between devices, on_device(): pieces = lax.all_to_all(totals, 'tm', 0, 0)  7.58 us
    ppermute x4, waiting for transfers between devices, send(): return lax.ppermute(x, ('tm', 'clus'), pairs)  5.15 us
    pallas_call x2, Pallas kernels, on_device(): pl.pallas_call(final_kernel, name='final', grid=(1,), out_shape=(sds(shap...  2.96 us
    unnamed x14, local copies, waits for them, and re-layouts  2.61 us
    pallas_call x1, Pallas kernels, on_device(): pl.pallas_call(prep_kernel, name='prep', out_shape=(sds(shape3, F32), sds...  2.15 us
  transfers between devices with their start and end apart: 5, of which 2 were waited for; matrix products, arithmetic and copies ran while one was open for 6% of the time, Pallas kernels for 25%

profile of v7, /device:TPU:2, one launch (start us, length us, event | category | flops | bytes accessed | tf_op | source)
XLA Modules:
  0.0 57.0 jit_solution(12029123299410099106)
XLA Ops:
  0.6 13.3 %collective-permute-start.1 = (bf16[32,64,128]{2,1,0:T(8,128)(2,1)}, bf16[32,64,128]{2,1,0:T(8,128)(2,1)S(1)}, u32[]{:S(2)}, u32[]{:S(2)}) collective-permute-start(bf16[32,64,128]{2,1,0:T(8,128)(2,1)} %cur_ref.5), channel_id=1, source_target_pairs={{0,31},{1,2},{2,1},{3,4},{4,3},{5,6},{6,5},{7,8},{8,7},{9,10},{10,... | collective-permute-start | bytes 1572872 | tf_op jit(solution)/shard_map/ppermute | solution.py:125
  13.9 1.9 %collective-permute-start = (bf16[32,64,128]{2,1,0:T(8,128)(2,1)}, bf16[32,64,128]{2,1,0:T(8,128)(2,1)S(1)}, u32[]{:S(2)}, u32[]{:S(2)}) collective-permute-start(bf16[32,64,128]{2,1,0:T(8,128)(2,1)} %cur_ref.5), channel_id=1, source_target_pairs={{0,1},{1,0},{2,3},{3,2},{4,5},{5,4},{6,7},{7,6},{8,9},{9,8},{10,11... | collective-permute-start | bytes 1572872 | tf_op jit(solution)/shard_map/ppermute | solution.py:125
  15.8 1.0 %copy-done = bf16[32,64,128]{2,1,0:T(8,128)(2,1)S(1)} copy-done((bf16[32,64,128]{2,1,0:T(8,128)(2,1)S(1)}, bf16[32,64,128]{2,1,0:T(8,128)(2,1)}, u32[]{:S(2)}) %copy-start) | copy-done | bytes 524312
  16.9 0.8 %copy-done.5 = bf16[128,128]{1,0:T(8,128)(2,1)S(1)} copy-done((bf16[128,128]{1,0:T(8,128)(2,1)S(1)}, bf16[128,128]{1,0:T(8,128)(2,1)}, u32[]{:S(2)}) %copy-start.5) | copy-done | bytes 32792
  17.6 2.2 %prep.1 = (f32[32,64,128]{2,1,0:T(8,128)S(1)}, f32[16,32,128]{2,1,0:T(8,128)}) custom-call(bf16[32,64,128]{2,1,0:T(8,128)(2,1)S(1)} %copy-done, bf16[128,128]{1,0:T(8,128)(2,1)S(1)} %copy-done.5), custom_call_target="tpu_custom_call" | custom-call | tf_op jit(solution)/shard_map/prep/pallas_call | solution.py:137
  19.8 7.6 %all-to-all-start = ((f32[16,32,128]{2,1,0:T(8,128)}), f32[16,32,128]{2,1,0:T(8,128)}, u32[]{:S(2)}, u32[]{:S(2)}) async-start(f32[16,32,128]{2,1,0:T(8,128)} %get-tuple-element.25), calls=%async_computation | async-start | bytes 524288 | tf_op jit(solution)/shard_map/all_to_all | solution.py:154
  27.4 0.7 %slice.16 = f32[30,1]{1,0:T(8,128)S(1)} slice(bf16[30,64]{1,0:T(8,128)(2,1)} %param.11), slice={[0:30], [0:1]} | slice | bytes 240 | tf_op jit(solution)/shard_map/jit(_roll_static)/slice | solution.py:136
  28.1 0.7 %convert_element_type.5 = f32[30,64]{1,0:T(8,128)S(1)} convert(bf16[30,64]{1,0:T(8,128)(2,1)} %param.11) | non-fusion elementwise | flops 1920 | bytes 11520 | tf_op jit(solution)/shard_map/convert_element_type | solution.py:135
  28.8 0.1 pad_slice_fusion
  28.8 0.1 slice.15
  28.9 0.1 pad_maximum_fusion.lag_ref
  29.0 0.8 %fusion.1.ids_ref = s32[32,30]{1,0:T(8,128)S(1)} fusion(s32[32,30]{1,0:T(8,128)} %param.10, s32[]{:T(128)S(6)} %xor.3, s32[]{:T(128)S(6)} %axis_index.22), kind=kLoop, calls=%fused_computation.7 | loop fusion | flops 25920 | bytes 7688 | tf_op jit(solution)/shard_map/jit(_where)/select_n | solution.py:151
  29.9 0.4 layout.1
  30.2 4.8 %near.2 = (f32[16,64,128]{2,1,0:T(8,128)S(1)}, bf16[16,64,128]{2,1,0:T(8,128)(2,1)}) custom-call(s32[32,30]{1,0:T(8,128)S(1)} %fusion.1.ids_ref, bf16[97,64,128]{2,1,0:T(8,128)(2,1)S(1)} %get-tuple-element.21.field, bf16[30,128,128]{2,1,0:T(8,128)(2,1)S(1)} %copy-done.6, bf16[128,1920]{1,0:T(8,128)(2,1)S(1)} %get-tuple-element.22.toep_ref), custom_call_target="tpu_custom_call" | custom-call | flops 2013265920 | bytes 4194304 | tf_op jit(solution)/shard_map/near/pallas_call | solution.py:169
  35.0 3.5 %collective-permute-start.3 = (bf16[16,64,128]{2,1,0:T(8,128)(2,1)}, bf16[16,64,128]{2,1,0:T(8,128)(2,1)}, u32[]{:S(2)}, u32[]{:S(2)}) collective-permute-start(bf16[16,64,128]{2,1,0:T(8,128)(2,1)} %get-tuple-element.33), channel_id=1, source_target_pairs={{0,32},{1,33},{2,34},{3,35},{4,36},{5,37},{6,38},{7,39},{8,40},{9,... | collective-permute-start | bytes 786440 | tf_op jit(solution)/shard_map/ppermute | solution.py:125
  38.5 4.8 %near.3 = (f32[16,64,128]{2,1,0:T(8,128)S(1)}, bf16[16,64,128]{2,1,0:T(8,128)(2,1)}) custom-call(s32[32,30]{1,0:T(8,128)S(1)} %fusion.1.ids_ref, bf16[97,64,128]{2,1,0:T(8,128)(2,1)S(1)} %get-tuple-element.21.field, bf16[30,128,128]{2,1,0:T(8,128)(2,1)S(1)} %copy-done.6, bf16[128,1920]{1,0:T(8,128)(2,1)S(1)} %get-tuple-element.22.toep_ref), custom_call_target="tpu_custom_call" | custom-call | flops 2013265920 | bytes 4194304 | tf_op jit(solution)/shard_map/near/pallas_call | solution.py:169
  43.3 3.4 %collective-permute-start.2 = (bf16[16,64,128]{2,1,0:T(8,128)(2,1)}, bf16[16,64,128]{2,1,0:T(8,128)(2,1)S(1)}, u32[]{:S(2)}, u32[]{:S(2)}) collective-permute-start(bf16[16,64,128]{2,1,0:T(8,128)(2,1)} %get-tuple-element.32), channel_id=1, source_target_pairs={{0,32},{1,33},{2,34},{3,35},{4,36},{5,37},{6,38},{7,39},{8,40},{9,... | collective-permute-start | bytes 786440 | tf_op jit(solution)/shard_map/ppermute | solution.py:125
  46.7 1.0 %select_reduce_fusion.before_ref = f32[32,128]{1,0:T(8,128)S(1)} fusion(f32[16,32,128]{2,1,0:T(8,128)} %all-to-all-done, pred[16]{0:T(512)(128)(4,1)S(1)} %iota_compare_fusion), kind=kLoop, calls=%fused_computation | loop fusion | flops 126976 | bytes 278544 | tf_op jit(solution)/shard_map/reduce_sum | solution.py:188
  47.8 0.3 base.1.base_ref
  48.1 0.1 collective-permute-done.3.tail_ref
  48.2 0.8 %copy-done.2 = bf16[32,128,128]{2,1,0:T(8,128)(2,1)S(1)} copy-done((bf16[32,128,128]{2,1,0:T(8,128)(2,1)S(1)}, bf16[32,128,128]{2,1,0:T(8,128)(2,1)}, u32[]{:S(2)}) %copy-start.2) | copy-done | bytes 1048600
  49.0 1.9 %final.2 = (bf16[32,64,128]{2,1,0:T(8,128)(2,1)}, f32[32,64,128]{2,1,0:T(8,128)}) custom-call(bf16[32,64,128]{2,1,0:T(8,128)(2,1)S(1)} %copy-done.1, f32[32,64,128]{2,1,0:T(8,128)S(1)} %base.1.base_ref, bf16[16,64,128]{2,1,0:T(8,128)(2,1)} %collective-permute-done.3.tail_ref, bf16[32,128,128]{2,1,0:T(8,128)(2,1)S(1)} %copy-done.2), custom_call_target="tpu_custom_call" | custom-call | tf_op jit(solution)/shard_map/final/pallas_call | solution.py:201
  51.0 5.0 %collective-permute-done.2.tail_ref = bf16[16,64,128]{2,1,0:T(8,128)(2,1)S(1)} collective-permute-done((bf16[16,64,128]{2,1,0:T(8,128)(2,1)}, bf16[16,64,128]{2,1,0:T(8,128)(2,1)S(1)}, u32[]{:S(2)}, u32[]{:S(2)}) %collective-permute-start.2) | collective-permute-done | bytes 262176 | tf_op jit(solution)/shard_map/ppermute | solution.py:125
  56.0 1.0 %final.3 = (bf16[32,64,128]{2,1,0:T(8,128)(2,1)}, f32[32,64,128]{2,1,0:T(8,128)}) custom-call(bf16[32,64,128]{2,1,0:T(8,128)(2,1)S(1)} %copy-done.1, f32[32,64,128]{2,1,0:T(8,128)S(1)} %base.1.base_ref, bf16[16,64,128]{2,1,0:T(8,128)(2,1)S(1)} %collective-permute-done.2.tail_ref, ...), custom_call_target="tpu_custom_call", output_to_operand_aliasing={{0}: (4, {}), {1}: (5, {})} | custom-call | tf_op jit(solution)/shard_map/final/pallas_call | solution.py:201
  (15 shorter events, 0.0 us)
Async XLA Ops:
  0.6 29.2 %collective-permute-start.1 = (bf16[32,64,128]{2,1,0:T(8,128)(2,1)}, bf16[32,64,128]{2,1,0:T(8,128)(2,1)S(1)}, u32[]{:S(2)}, u32[]{:S(2)}) collective-permute-start(bf16[32,64,128]{2,1,0:T(8,128)(2,1)} %cur_ref.5), channel_id=1, source_target_pairs={{0,31},{1,2},{2,1},{3,4},{4,3},{5,6},{6,5},{7,8},{8,7},{9,10},{10,... | collective-permute-start | bytes 1572872 | tf_op jit(solution)/shard_map/ppermute | solution.py:125
  13.9 15.9 %collective-permute-start = (bf16[32,64,128]{2,1,0:T(8,128)(2,1)}, bf16[32,64,128]{2,1,0:T(8,128)(2,1)S(1)}, u32[]{:S(2)}, u32[]{:S(2)}) collective-permute-start(bf16[32,64,128]{2,1,0:T(8,128)(2,1)} %cur_ref.5), channel_id=1, source_target_pairs={{0,1},{1,0},{2,3},{3,2},{4,5},{5,4},{6,7},{7,6},{8,9},{9,8},{10,11... | collective-permute-start | bytes 1572872 | tf_op jit(solution)/shard_map/ppermute | solution.py:125
  15.8 1.0 %copy-start = (bf16[32,64,128]{2,1,0:T(8,128)(2,1)S(1)}, bf16[32,64,128]{2,1,0:T(8,128)(2,1)}, u32[]{:S(2)}) copy-start(bf16[32,64,128]{2,1,0:T(8,128)(2,1)} %cur_ref.5) | copy-start | bytes 1572868
  16.9 0.8 %copy-start.5 = (bf16[128,128]{1,0:T(8,128)(2,1)S(1)}, bf16[128,128]{1,0:T(8,128)(2,1)}, u32[]{:S(2)}) copy-start(bf16[128,128]{1,0:T(8,128)(2,1)} %map_ref.1) | copy-start | bytes 98308
  17.6 12.2 %copy-start.1 = (bf16[32,64,128]{2,1,0:T(8,128)(2,1)S(1)}, bf16[32,64,128]{2,1,0:T(8,128)(2,1)}, u32[]{:S(2)}) copy-start(bf16[32,64,128]{2,1,0:T(8,128)(2,1)} %cur_ref.5) | copy-start | bytes 1572868
  19.8 26.9 %all-to-all-start = ((f32[16,32,128]{2,1,0:T(8,128)}), f32[16,32,128]{2,1,0:T(8,128)}, u32[]{:S(2)}, u32[]{:S(2)}) async-start(f32[16,32,128]{2,1,0:T(8,128)} %get-tuple-element.25), calls=%async_computation | async-start | bytes 524288 | tf_op jit(solution)/shard_map/all_to_all | solution.py:154
  29.0 1.2 %copy-start.6 = (bf16[30,128,128]{2,1,0:T(8,128)(2,1)S(1)}, bf16[30,128,128]{2,1,0:T(8,128)(2,1)}, u32[]{:S(2)}) copy-start(bf16[30,128,128]{2,1,0:T(8,128)(2,1)} %coup_ref.3) | copy-start | bytes 2949124
  35.0 12.7 %copy-start.3 = (bf16[32,64,128]{2,1,0:T(8,128)(2,1)S(1)}, bf16[32,64,128]{2,1,0:T(8,128)(2,1)}, u32[]{:S(2)}) copy-start(bf16[32,64,128]{2,1,0:T(8,128)(2,1)} %exc_ref.1) | copy-start | bytes 1572868
  35.0 12.7 %copy-start.4 = (bf16[128,128]{1,0:T(8,128)(2,1)S(1)}, bf16[128,128]{1,0:T(8,128)(2,1)}, u32[]{:S(2)}) copy-start(bf16[128,128]{1,0:T(8,128)(2,1)} %pot_ref.1) | copy-start | bytes 98308
  35.0 13.2 %collective-permute-start.3 = (bf16[16,64,128]{2,1,0:T(8,128)(2,1)}, bf16[16,64,128]{2,1,0:T(8,128)(2,1)}, u32[]{:S(2)}, u32[]{:S(2)}) collective-permute-start(bf16[16,64,128]{2,1,0:T(8,128)(2,1)} %get-tuple-element.33), channel_id=1, source_target_pairs={{0,32},{1,33},{2,34},{3,35},{4,36},{5,37},{6,38},{7,39},{8,40},{9,... | collective-permute-start | bytes 786440 | tf_op jit(solution)/shard_map/ppermute | solution.py:125
  43.3 12.7 %collective-permute-start.2 = (bf16[16,64,128]{2,1,0:T(8,128)(2,1)}, bf16[16,64,128]{2,1,0:T(8,128)(2,1)S(1)}, u32[]{:S(2)}, u32[]{:S(2)}) collective-permute-start(bf16[16,64,128]{2,1,0:T(8,128)(2,1)} %get-tuple-element.32), channel_id=1, source_target_pairs={{0,32},{1,33},{2,34},{3,35},{4,36},{5,37},{6,38},{7,39},{8,40},{9,... | collective-permute-start | bytes 786440 | tf_op jit(solution)/shard_map/ppermute | solution.py:125
  47.8 1.2 %copy-start.2 = (bf16[32,128,128]{2,1,0:T(8,128)(2,1)S(1)}, bf16[32,128,128]{2,1,0:T(8,128)(2,1)}, u32[]{:S(2)}) copy-start(bf16[32,128,128]{2,1,0:T(8,128)(2,1)} %inv_ref.3) | copy-start | bytes 3145732

commit v8 on v7

--- a/solution.py
+++ b/solution.py
@@ -65,7 +65,7 @@
 ):
     count, steps, unknowns = head_ref.shape
     slots = coup_ref.shape[0]
-    group = min(16, count)
+    group = min(8, count)
 
     @pl.loop(0, count // group)
     def _(g):
@@ -172,7 +172,7 @@
             out_shape=(sds((part, steps, unknowns), F32), sds((part, steps, unknowns), BF16)),
             in_specs=[whole(pltpu.SMEM)] + [whole()] * 3,
             out_specs=(whole(), whole()),
-            scratch_shapes=[pltpu.VMEM((8, slots * steps, 2 * unknowns), BF16)],
+            scratch_shapes=[pltpu.VMEM((4, slots * steps, 2 * unknowns), BF16)],
             compiler_params=params(24),
             cost_estimate=pl.CostEstimate(
                 flops=2 * part * slots * steps * unknowns * (unknowns + 2 * steps),

time: 57.6 us -> 57.9 us (level)
  transfers between devices with their start and end apart: 5 -> 5, of which waited for: 2 -> 1; matrix products, arithmetic and copies ran while one was open for 6% -> 6% of each run, Pallas kernels for 25% -> 26%
where the time goes in v8:
time: 57.9 us; the launch traced here: 57.3 us
  starting transfers between devices  29.6 us (51%)
  Pallas kernels  15.6 us (27%)
  waiting for transfers between devices  5.03 us (9%)
  local copies, waits for them, and re-layouts  3.58 us (6%)
  other arithmetic  2.65 us (5%)
  between operations  0.78 us (1%)
    ppermute x4, starting transfers between devices, send(): return lax.ppermute(x, ('tm', 'clus'), pairs)  22 us
    pallas_call x2, Pallas kernels, on_device(): pl.pallas_call(functools.partial(near_kernel, h * part), name='near', out...  9.87 us
    all_to_all x1, starting transfers between devices, on_device(): pieces = lax.all_to_all(totals, 'tm', 0, 0)  7.58 us
    ppermute x4, waiting for transfers between devices, send(): return lax.ppermute(x, ('tm', 'clus'), pairs)  5.03 us
    pallas_call x2, Pallas kernels, on_device(): pl.pallas_call(final_kernel, name='final', grid=(1,), out_shape=(sds(shap...  2.95 us
    unnamed x14, local copies, waits for them, and re-layouts  2.73 us
    pallas_call x1, Pallas kernels, on_device(): pl.pallas_call(prep_kernel, name='prep', out_shape=(sds(shape3, F32), sds...  2.15 us
  transfers between devices with their start and end apart: 5, of which 1 were waited for; matrix products, arithmetic and copies ran while one was open for 6% of the time, Pallas kernels for 26%

profile of v8, /device:TPU:2, one launch (start us, length us, event | category | flops | bytes accessed | tf_op | source)
XLA Modules:
  0.0 57.3 jit_solution(16139071850573858689)
XLA Ops:
  0.6 13.3 %collective-permute-start.1 = (bf16[32,64,128]{2,1,0:T(8,128)(2,1)}, bf16[32,64,128]{2,1,0:T(8,128)(2,1)S(1)}, u32[]{:S(2)}, u32[]{:S(2)}) collective-permute-start(bf16[32,64,128]{2,1,0:T(8,128)(2,1)} %cur_ref.5), channel_id=1, source_target_pairs={{0,31},{1,2},{2,1},{3,4},{4,3},{5,6},{6,5},{7,8},{8,7},{9,10},{10,... | collective-permute-start | bytes 1572872 | tf_op jit(solution)/shard_map/ppermute | solution.py:125
  13.9 1.9 %collective-permute-start = (bf16[32,64,128]{2,1,0:T(8,128)(2,1)}, bf16[32,64,128]{2,1,0:T(8,128)(2,1)S(1)}, u32[]{:S(2)}, u32[]{:S(2)}) collective-permute-start(bf16[32,64,128]{2,1,0:T(8,128)(2,1)} %cur_ref.5), channel_id=1, source_target_pairs={{0,1},{1,0},{2,3},{3,2},{4,5},{5,4},{6,7},{7,6},{8,9},{9,8},{10,11... | collective-permute-start | bytes 1572872 | tf_op jit(solution)/shard_map/ppermute | solution.py:125
  15.8 1.0 %copy-done = bf16[32,64,128]{2,1,0:T(8,128)(2,1)S(1)} copy-done((bf16[32,64,128]{2,1,0:T(8,128)(2,1)S(1)}, bf16[32,64,128]{2,1,0:T(8,128)(2,1)}, u32[]{:S(2)}) %copy-start) | copy-done | bytes 524312
  16.9 0.8 %copy-done.5 = bf16[128,128]{1,0:T(8,128)(2,1)S(1)} copy-done((bf16[128,128]{1,0:T(8,128)(2,1)S(1)}, bf16[128,128]{1,0:T(8,128)(2,1)}, u32[]{:S(2)}) %copy-start.5) | copy-done | bytes 32792
  17.6 2.2 %prep.1 = (f32[32,64,128]{2,1,0:T(8,128)S(1)}, f32[16,32,128]{2,1,0:T(8,128)}) custom-call(bf16[32,64,128]{2,1,0:T(8,128)(2,1)S(1)} %copy-done, bf16[128,128]{1,0:T(8,128)(2,1)S(1)} %copy-done.5), custom_call_target="tpu_custom_call" | custom-call | tf_op jit(solution)/shard_map/prep/pallas_call | solution.py:137
  19.8 7.6 %all-to-all-start = ((f32[16,32,128]{2,1,0:T(8,128)}), f32[16,32,128]{2,1,0:T(8,128)}, u32[]{:S(2)}, u32[]{:S(2)}) async-start(f32[16,32,128]{2,1,0:T(8,128)} %get-tuple-element.25), calls=%async_computation | async-start | bytes 524288 | tf_op jit(solution)/shard_map/all_to_all | solution.py:154
  27.4 0.7 %slice.16 = f32[30,1]{1,0:T(8,128)S(1)} slice(bf16[30,64]{1,0:T(8,128)(2,1)} %param.11), slice={[0:30], [0:1]} | slice | bytes 240 | tf_op jit(solution)/shard_map/jit(_roll_static)/slice | solution.py:136
  28.1 0.7 %convert_element_type.5 = f32[30,64]{1,0:T(8,128)S(1)} convert(bf16[30,64]{1,0:T(8,128)(2,1)} %param.11) | non-fusion elementwise | flops 1920 | bytes 11520 | tf_op jit(solution)/shard_map/convert_element_type | solution.py:135
  28.8 0.1 pad_slice_fusion
  28.8 0.1 slice.15
  28.9 0.1 pad_maximum_fusion.lag_ref
  29.0 0.8 %fusion.1.ids_ref = s32[32,30]{1,0:T(8,128)S(1)} fusion(s32[32,30]{1,0:T(8,128)} %param.10, s32[]{:T(128)S(6)} %xor.3, s32[]{:T(128)S(6)} %axis_index.22), kind=kLoop, calls=%fused_computation.7 | loop fusion | flops 25920 | bytes 7688 | tf_op jit(solution)/shard_map/jit(_where)/select_n | solution.py:151
  29.9 0.4 layout.1
  30.2 4.9 %near.2 = (f32[16,64,128]{2,1,0:T(8,128)S(1)}, bf16[16,64,128]{2,1,0:T(8,128)(2,1)}) custom-call(s32[32,30]{1,0:T(8,128)S(1)} %fusion.1.ids_ref, bf16[97,64,128]{2,1,0:T(8,128)(2,1)S(1)} %get-tuple-element.21.field, bf16[30,128,128]{2,1,0:T(8,128)(2,1)S(1)} %copy-done.6, bf16[128,1920]{1,0:T(8,128)(2,1)S(1)} %get-tuple-element.22.toep_ref), custom_call_target="tpu_custom_call" | custom-call | flops 2013265920 | bytes 4194304 | tf_op jit(solution)/shard_map/near/pallas_call | solution.py:169
  35.2 3.5 %collective-permute-start.3 = (bf16[16,64,128]{2,1,0:T(8,128)(2,1)}, bf16[16,64,128]{2,1,0:T(8,128)(2,1)}, u32[]{:S(2)}, u32[]{:S(2)}) collective-permute-start(bf16[16,64,128]{2,1,0:T(8,128)(2,1)} %get-tuple-element.33), channel_id=1, source_target_pairs={{0,32},{1,33},{2,34},{3,35},{4,36},{5,37},{6,38},{7,39},{8,40},{9,... | collective-permute-start | bytes 786440 | tf_op jit(solution)/shard_map/ppermute | solution.py:125
  38.7 4.9 %near.3 = (f32[16,64,128]{2,1,0:T(8,128)S(1)}, bf16[16,64,128]{2,1,0:T(8,128)(2,1)}) custom-call(s32[32,30]{1,0:T(8,128)S(1)} %fusion.1.ids_ref, bf16[97,64,128]{2,1,0:T(8,128)(2,1)S(1)} %get-tuple-element.21.field, bf16[30,128,128]{2,1,0:T(8,128)(2,1)S(1)} %copy-done.6, bf16[128,1920]{1,0:T(8,128)(2,1)S(1)} %get-tuple-element.22.toep_ref), custom_call_target="tpu_custom_call" | custom-call | flops 2013265920 | bytes 4194304 | tf_op jit(solution)/shard_map/near/pallas_call | solution.py:169
  43.6 3.4 %collective-permute-start.2 = (bf16[16,64,128]{2,1,0:T(8,128)(2,1)}, bf16[16,64,128]{2,1,0:T(8,128)(2,1)S(1)}, u32[]{:S(2)}, u32[]{:S(2)}) collective-permute-start(bf16[16,64,128]{2,1,0:T(8,128)(2,1)} %get-tuple-element.32), channel_id=1, source_target_pairs={{0,32},{1,33},{2,34},{3,35},{4,36},{5,37},{6,38},{7,39},{8,40},{9,... | collective-permute-start | bytes 786440 | tf_op jit(solution)/shard_map/ppermute | solution.py:125
  47.0 1.0 %select_reduce_fusion.before_ref = f32[32,128]{1,0:T(8,128)S(1)} fusion(f32[16,32,128]{2,1,0:T(8,128)} %all-to-all-done, pred[16]{0:T(512)(128)(4,1)S(1)} %iota_compare_fusion), kind=kLoop, calls=%fused_computation | loop fusion | flops 126976 | bytes 278544 | tf_op jit(solution)/shard_map/reduce_sum | solution.py:188
  48.1 0.0 copy-start.2
  48.1 0.3 base.1.base_ref
  48.4 0.9 %copy-done.2 = bf16[32,128,128]{2,1,0:T(8,128)(2,1)S(1)} copy-done((bf16[32,128,128]{2,1,0:T(8,128)(2,1)S(1)}, bf16[32,128,128]{2,1,0:T(8,128)(2,1)}, u32[]{:S(2)}) %copy-start.2) | copy-done | bytes 1048600
  49.3 2.0 %final.2 = (bf16[32,64,128]{2,1,0:T(8,128)(2,1)}, f32[32,64,128]{2,1,0:T(8,128)}) custom-call(bf16[32,64,128]{2,1,0:T(8,128)(2,1)S(1)} %copy-done.1, f32[32,64,128]{2,1,0:T(8,128)S(1)} %base.1.base_ref, bf16[16,64,128]{2,1,0:T(8,128)(2,1)} %collective-permute-done.3.tail_ref, bf16[32,128,128]{2,1,0:T(8,128)(2,1)S(1)} %copy-done.2), custom_call_target="tpu_custom_call" | custom-call | tf_op jit(solution)/shard_map/final/pallas_call | solution.py:201
  51.3 5.0 %collective-permute-done.2.tail_ref = bf16[16,64,128]{2,1,0:T(8,128)(2,1)S(1)} collective-permute-done((bf16[16,64,128]{2,1,0:T(8,128)(2,1)}, bf16[16,64,128]{2,1,0:T(8,128)(2,1)S(1)}, u32[]{:S(2)}, u32[]{:S(2)}) %collective-permute-start.2) | collective-permute-done | bytes 262176 | tf_op jit(solution)/shard_map/ppermute | solution.py:125
  56.3 1.0 %final.3 = (bf16[32,64,128]{2,1,0:T(8,128)(2,1)}, f32[32,64,128]{2,1,0:T(8,128)}) custom-call(bf16[32,64,128]{2,1,0:T(8,128)(2,1)S(1)} %copy-done.1, f32[32,64,128]{2,1,0:T(8,128)S(1)} %base.1.base_ref, bf16[16,64,128]{2,1,0:T(8,128)(2,1)S(1)} %collective-permute-done.2.tail_ref, ...), custom_call_target="tpu_custom_call", output_to_operand_aliasing={{0}: (4, {}), {1}: (5, {})} | custom-call | tf_op jit(solution)/shard_map/final/pallas_call | solution.py:201
  (15 shorter events, 0.0 us)
Async XLA Ops:
  0.6 29.2 %collective-permute-start.1 = (bf16[32,64,128]{2,1,0:T(8,128)(2,1)}, bf16[32,64,128]{2,1,0:T(8,128)(2,1)S(1)}, u32[]{:S(2)}, u32[]{:S(2)}) collective-permute-start(bf16[32,64,128]{2,1,0:T(8,128)(2,1)} %cur_ref.5), channel_id=1, source_target_pairs={{0,31},{1,2},{2,1},{3,4},{4,3},{5,6},{6,5},{7,8},{8,7},{9,10},{10,... | collective-permute-start | bytes 1572872 | tf_op jit(solution)/shard_map/ppermute | solution.py:125
  13.9 15.9 %collective-permute-start = (bf16[32,64,128]{2,1,0:T(8,128)(2,1)}, bf16[32,64,128]{2,1,0:T(8,128)(2,1)S(1)}, u32[]{:S(2)}, u32[]{:S(2)}) collective-permute-start(bf16[32,64,128]{2,1,0:T(8,128)(2,1)} %cur_ref.5), channel_id=1, source_target_pairs={{0,1},{1,0},{2,3},{3,2},{4,5},{5,4},{6,7},{7,6},{8,9},{9,8},{10,11... | collective-permute-start | bytes 1572872 | tf_op jit(solution)/shard_map/ppermute | solution.py:125
  15.8 1.0 %copy-start = (bf16[32,64,128]{2,1,0:T(8,128)(2,1)S(1)}, bf16[32,64,128]{2,1,0:T(8,128)(2,1)}, u32[]{:S(2)}) copy-start(bf16[32,64,128]{2,1,0:T(8,128)(2,1)} %cur_ref.5) | copy-start | bytes 1572868
  16.9 0.8 %copy-start.5 = (bf16[128,128]{1,0:T(8,128)(2,1)S(1)}, bf16[128,128]{1,0:T(8,128)(2,1)}, u32[]{:S(2)}) copy-start(bf16[128,128]{1,0:T(8,128)(2,1)} %map_ref.1) | copy-start | bytes 98308
  17.6 12.2 %copy-start.1 = (bf16[32,64,128]{2,1,0:T(8,128)(2,1)S(1)}, bf16[32,64,128]{2,1,0:T(8,128)(2,1)}, u32[]{:S(2)}) copy-start(bf16[32,64,128]{2,1,0:T(8,128)(2,1)} %cur_ref.5) | copy-start | bytes 1572868
  19.8 27.2 %all-to-all-start = ((f32[16,32,128]{2,1,0:T(8,128)}), f32[16,32,128]{2,1,0:T(8,128)}, u32[]{:S(2)}, u32[]{:S(2)}) async-start(f32[16,32,128]{2,1,0:T(8,128)} %get-tuple-element.25), calls=%async_computation | async-start | bytes 524288 | tf_op jit(solution)/shard_map/all_to_all | solution.py:154
  29.0 1.2 %copy-start.6 = (bf16[30,128,128]{2,1,0:T(8,128)(2,1)S(1)}, bf16[30,128,128]{2,1,0:T(8,128)(2,1)}, u32[]{:S(2)}) copy-start(bf16[30,128,128]{2,1,0:T(8,128)(2,1)} %coup_ref.3) | copy-start | bytes 2949124
  35.2 12.9 %copy-start.3 = (bf16[32,64,128]{2,1,0:T(8,128)(2,1)S(1)}, bf16[32,64,128]{2,1,0:T(8,128)(2,1)}, u32[]{:S(2)}) copy-start(bf16[32,64,128]{2,1,0:T(8,128)(2,1)} %exc_ref.1) | copy-start | bytes 1572868
  35.2 12.9 %copy-start.4 = (bf16[128,128]{1,0:T(8,128)(2,1)S(1)}, bf16[128,128]{1,0:T(8,128)(2,1)}, u32[]{:S(2)}) copy-start(bf16[128,128]{1,0:T(8,128)(2,1)} %pot_ref.1) | copy-start | bytes 98308
  35.2 13.2 %collective-permute-start.3 = (bf16[16,64,128]{2,1,0:T(8,128)(2,1)}, bf16[16,64,128]{2,1,0:T(8,128)(2,1)}, u32[]{:S(2)}, u32[]{:S(2)}) collective-permute-start(bf16[16,64,128]{2,1,0:T(8,128)(2,1)} %get-tuple-element.33), channel_id=1, source_target_pairs={{0,32},{1,33},{2,34},{3,35},{4,36},{5,37},{6,38},{7,39},{8,40},{9,... | collective-permute-start | bytes 786440 | tf_op jit(solution)/shard_map/ppermute | solution.py:125
  43.6 12.7 %collective-permute-start.2 = (bf16[16,64,128]{2,1,0:T(8,128)(2,1)}, bf16[16,64,128]{2,1,0:T(8,128)(2,1)S(1)}, u32[]{:S(2)}, u32[]{:S(2)}) collective-permute-start(bf16[16,64,128]{2,1,0:T(8,128)(2,1)} %get-tuple-element.32), channel_id=1, source_target_pairs={{0,32},{1,33},{2,34},{3,35},{4,36},{5,37},{6,38},{7,39},{8,40},{9,... | collective-permute-start | bytes 786440 | tf_op jit(solution)/shard_map/ppermute | solution.py:125
  48.1 1.2 %copy-start.2 = (bf16[32,128,128]{2,1,0:T(8,128)(2,1)S(1)}, bf16[32,128,128]{2,1,0:T(8,128)(2,1)}, u32[]{:S(2)}) copy-start(bf16[32,128,128]{2,1,0:T(8,128)(2,1)} %inv_ref.3) | copy-start | bytes 3145732

commit v9 on v8

--- a/solution.py
+++ b/solution.py
@@ -85,13 +85,16 @@
                 tail_ref[first + i + j] = out[steps:, lanes].astype(BF16)
 
 
-def base_kernel(exc_ref, low_ref, high_ref, running_ref, before_ref, pot_ref, base_ref):
+def base_kernel(block_ref, exc_ref, low_ref, high_ref, running_ref, pieces_ref, pot_ref, base_ref):
     per_dev, steps, unknowns = exc_ref.shape
+    before = jnp.zeros(pieces_ref.shape[1:], F32)
+    for t in range(pieces_ref.shape[0] - 1):
+        before += jnp.where(t < block_ref[0], pieces_ref[t], 0.0)
     group = per_dev // 4
     for g in range(4):
         at = slice(g * group, (g + 1) * group)
-        head = (low_ref, high_ref)[g // 2][g % 2 * group : (g % 2 + 1) * group]
-        charge = (running_ref[at] + before_ref[at][:, None, :]).astype(BF16)
+        head = low_ref[at] if g < 3 else high_ref[...]
+        charge = (running_ref[at] + before[at][:, None, :]).astype(BF16)
         field = dot(charge.reshape(group * steps, -1), pot_ref[...])
         field = field.reshape(group, steps, unknowns)
         base_ref[at] = exc_ref[at].astype(F32) - head - field
@@ -163,11 +166,12 @@
         out_specs=(whole(), whole()),
         compiler_params=params(16),
     )(lag_rows, currents, inner, outer)
-    part = per_dev // 2
+    most = 3 * per_dev // 4
+    cuts = ((0, most), (most, per_dev - most))
     heads, tails = [], []
-    for h in range(2):
+    for first, part in cuts:
         head, tail = pl.pallas_call(
-            functools.partial(near_kernel, h * part),
+            functools.partial(near_kernel, first),
             name="near",
             out_shape=(sds((part, steps, unknowns), F32), sds((part, steps, unknowns), BF16)),
             in_specs=[whole(pltpu.SMEM)] + [whole()] * 3,
@@ -183,32 +187,31 @@
         ids, head = lax.optimization_barrier((ids, head))
         heads.append(head)
         tails.append(behind(tail, 1))
-    earlier = jnp.arange(blocks) < lax.axis_index("tm")
+    mine = lax.axis_index("tm").astype(jnp.int32).reshape(1)
     pieces, heads[1] = lax.optimization_barrier((pieces, heads[1]))
-    before = jnp.sum(jnp.where(earlier[:, None, None], pieces, 0.0), axis=0)
     base = pl.pallas_call(
         base_kernel,
         name="base",
         out_shape=sds(shape3, F32),
-        in_specs=[whole()] * 6,
+        in_specs=[whole(pltpu.SMEM)] + [whole()] * 6,
         out_specs=whole(),
         compiler_params=params(16),
-    )(excitation, *heads, running, before, potential)
+    )(mine, excitation, *heads, running, pieces, potential)
     done = ()
-    for h in range(2):
-        at = lambda i, h=h: (h, 0, 0)
-        mine = pl.BlockSpec((part, steps, unknowns), at)
+    for tail, (first, part) in zip(tails, cuts):
+        at = lambda i, n=first // part: (n, 0, 0)
+        block = pl.BlockSpec((part, steps, unknowns), at)
         done = pl.pallas_call(
             final_kernel,
             name="final",
             grid=(1,),
             out_shape=(sds(shape3, BF16), sds(shape3, F32)),
-            in_specs=[mine, mine, whole(), pl.BlockSpec((part, unknowns, unknowns), at)]
+            in_specs=[block, block, whole(), pl.BlockSpec((part, unknowns, unknowns), at)]
             + [whole(pl.ANY)] * len(done),
-            out_specs=(mine, mine),
+            out_specs=(block, block),
             input_output_aliases={4: 0, 5: 1} if done else {},
             compiler_params=params(16),
-        )(currents, base, tails[h], block_inverses, *done)
+        )(currents, base, tail, block_inverses, *done)
     return done
 
 

time: 57.9 us -> 58 us (level)
  local copies, waits for them, and re-layouts: 3.58 us -> 5.06 us
  other arithmetic: 2.65 us -> 1.61 us
    unnamed x14 -> x18, local copies, waits for them, and re-layouts: 2.73 us -> 4.21 us
    reduce_sum x1 -> x0, other arithmetic: 1.04 us -> none  [on_device(): before = jnp.sum(jnp.where(earlier[:, None, None], pieces, 0.0), axis=0)]
  transfers between devices with their start and end apart: 5 -> 5, of which waited for: 1 -> 2; matrix products, arithmetic and copies ran while one was open for 6% -> 4% of each run, Pallas kernels for 26% -> 24%
where the time goes in v9:
time: 58 us; the launch traced here: 57.4 us
  starting transfers between devices  29.5 us (51%)
  Pallas kernels  15.6 us (27%)
  local copies, waits for them, and re-layouts  5.06 us (9%)
  waiting for transfers between devices  4.81 us (8%)
  other arithmetic  1.61 us (3%)
  between operations  0.77 us (1%)
    ppermute x4, starting transfers between devices, send(): return lax.ppermute(x, ('tm', 'clus'), pairs)  21.9 us
    pallas_call x2, Pallas kernels, on_device(): pl.pallas_call(functools.partial(near_kernel, first), name='near', out_sh...  9.86 us
    all_to_all x1, starting transfers between devices, on_device(): pieces = lax.all_to_all(totals, 'tm', 0, 0)  7.58 us
    ppermute x4, waiting for transfers between devices, send(): return lax.ppermute(x, ('tm', 'clus'), pairs)  4.81 us
    unnamed x18, local copies, waits for them, and re-layouts  4.21 us
    pallas_call x2, Pallas kernels, on_device(): pl.pallas_call(final_kernel, name='final', grid=(1,), out_shape=(sds(shap...  2.96 us
    pallas_call x1, Pallas kernels, on_device(): pl.pallas_call(prep_kernel, name='prep', out_shape=(sds(shape3, F32), sds...  2.14 us
  transfers between devices with their start and end apart: 5, of which 2 were waited for; matrix products, arithmetic and copies ran while one was open for 4% of the time, Pallas kernels for 24%

profile of v9, /device:TPU:2, one launch (start us, length us, event | category | flops | bytes accessed | tf_op | source)
XLA Modules:
  0.0 57.4 jit_solution(16867394700821812010)
XLA Ops:
  0.6 13.3 %collective-permute-start.1 = (bf16[32,64,128]{2,1,0:T(8,128)(2,1)}, bf16[32,64,128]{2,1,0:T(8,128)(2,1)S(1)}, u32[]{:S(2)}, u32[]{:S(2)}) collective-permute-start(bf16[32,64,128]{2,1,0:T(8,128)(2,1)} %cur_ref.5), channel_id=1, source_target_pairs={{0,31},{1,2},{2,1},{3,4},{4,3},{5,6},{6,5},{7,8},{8,7},{9,10},{10,... | collective-permute-start | bytes 1572872 | tf_op jit(solution)/shard_map/ppermute | solution.py:128
  13.9 1.9 %collective-permute-start = (bf16[32,64,128]{2,1,0:T(8,128)(2,1)}, bf16[32,64,128]{2,1,0:T(8,128)(2,1)S(1)}, u32[]{:S(2)}, u32[]{:S(2)}) collective-permute-start(bf16[32,64,128]{2,1,0:T(8,128)(2,1)} %cur_ref.5), channel_id=1, source_target_pairs={{0,1},{1,0},{2,3},{3,2},{4,5},{5,4},{6,7},{7,6},{8,9},{9,8},{10,11... | collective-permute-start | bytes 1572872 | tf_op jit(solution)/shard_map/ppermute | solution.py:128
  15.8 1.0 %copy-done = bf16[32,64,128]{2,1,0:T(8,128)(2,1)S(1)} copy-done((bf16[32,64,128]{2,1,0:T(8,128)(2,1)S(1)}, bf16[32,64,128]{2,1,0:T(8,128)(2,1)}, u32[]{:S(2)}) %copy-start) | copy-done | bytes 524312
  16.9 0.8 %copy-done.7 = bf16[128,128]{1,0:T(8,128)(2,1)S(1)} copy-done((bf16[128,128]{1,0:T(8,128)(2,1)S(1)}, bf16[128,128]{1,0:T(8,128)(2,1)}, u32[]{:S(2)}) %copy-start.7) | copy-done | bytes 32792
  17.6 2.1 %prep.1 = (f32[32,64,128]{2,1,0:T(8,128)S(1)}, f32[16,32,128]{2,1,0:T(8,128)}) custom-call(bf16[32,64,128]{2,1,0:T(8,128)(2,1)S(1)} %copy-done, bf16[128,128]{1,0:T(8,128)(2,1)S(1)} %copy-done.7), custom_call_target="tpu_custom_call" | custom-call | tf_op jit(solution)/shard_map/prep/pallas_call | solution.py:140
  19.8 7.6 %all-to-all-start = ((f32[16,32,128]{2,1,0:T(8,128)}), f32[16,32,128]{2,1,0:T(8,128)S(1)}, u32[]{:S(2)}, u32[]{:S(2)}) async-start(f32[16,32,128]{2,1,0:T(8,128)} %get-tuple-element.25), calls=%async_computation | async-start | bytes 524288 | tf_op jit(solution)/shard_map/all_to_all | solution.py:157
  27.3 0.7 %slice.16 = f32[30,1]{1,0:T(8,128)S(1)} slice(bf16[30,64]{1,0:T(8,128)(2,1)} %param.11), slice={[0:30], [0:1]} | slice | bytes 240 | tf_op jit(solution)/shard_map/jit(_roll_static)/slice | solution.py:139
  28.0 0.7 %convert_element_type.5 = f32[30,64]{1,0:T(8,128)S(1)} convert(bf16[30,64]{1,0:T(8,128)(2,1)} %param.11) | non-fusion elementwise | flops 1920 | bytes 11520 | tf_op jit(solution)/shard_map/convert_element_type | solution.py:138
  28.7 0.1 pad_slice_fusion
  28.9 0.1 pad_maximum_fusion.lag_ref
  29.0 0.8 %fusion.1.ids_ref = s32[32,30]{1,0:T(8,128)S(1)} fusion(s32[32,30]{1,0:T(8,128)} %param.10, s32[]{:T(128)S(6)} %xor.3, s32[]{:T(128)S(6)} %axis_index.25), kind=kLoop, calls=%fused_computation.6 | loop fusion | flops 25920 | bytes 7688 | tf_op jit(solution)/shard_map/jit(_where)/select_n | solution.py:154
  29.8 0.4 layout.1
  30.2 6.7 %near.2 = (f32[24,64,128]{2,1,0:T(8,128)S(1)}, bf16[24,64,128]{2,1,0:T(8,128)(2,1)}) custom-call(s32[32,30]{1,0:T(8,128)S(1)} %fusion.1.ids_ref, bf16[97,64,128]{2,1,0:T(8,128)(2,1)S(1)} %get-tuple-element.21.field, bf16[30,128,128]{2,1,0:T(8,128)(2,1)S(1)} %copy-done.8, bf16[128,1920]{1,0:T(8,128)(2,1)S(1)} %get-tuple-element.22.toep_ref), custom_call_target="tpu_custom_call" | custom-call | flops 3019898880 | bytes 4194304 | tf_op jit(solution)/shard_map/near/pallas_call | solution.py:173
  36.9 3.4 %collective-permute-start.3 = (bf16[24,64,128]{2,1,0:T(8,128)(2,1)}, bf16[24,64,128]{2,1,0:T(8,128)(2,1)S(1)}, u32[]{:S(2)}, u32[]{:S(2)}) collective-permute-start(bf16[24,64,128]{2,1,0:T(8,128)(2,1)} %get-tuple-element.33), channel_id=1, source_target_pairs={{0,32},{1,33},{2,34},{3,35},{4,36},{5,37},{6,38},{7,39},{8,40},{9,... | collective-permute-start | bytes 1179656 | tf_op jit(solution)/shard_map/ppermute | solution.py:128
  40.3 3.2 %near.3 = (f32[8,64,128]{2,1,0:T(8,128)S(1)}, bf16[8,64,128]{2,1,0:T(8,128)(2,1)}) custom-call(s32[32,30]{1,0:T(8,128)S(1)} %fusion.1.ids_ref, bf16[97,64,128]{2,1,0:T(8,128)(2,1)S(1)} %get-tuple-element.21.field, bf16[30,128,128]{2,1,0:T(8,128)(2,1)S(1)} %copy-done.8, bf16[128,1920]{1,0:T(8,128)(2,1)S(1)} %get-tuple-element.22.toep_ref), custom_call_target="tpu_custom_call" | custom-call | flops 1006632960 | bytes 4194304 | tf_op jit(solution)/shard_map/near/pallas_call | solution.py:173
  43.5 0.7 %copy-done.4 = f32[8,64,128]{2,1,0:T(8,128)} copy-done((f32[8,64,128]{2,1,0:T(8,128)}, f32[8,64,128]{2,1,0:T(8,128)S(1)}, u32[]{:S(2)}) %copy-start.4) | copy-done | bytes 262168
  44.2 3.4 %collective-permute-start.2 = (bf16[8,64,128]{2,1,0:T(8,128)(2,1)}, bf16[8,64,128]{2,1,0:T(8,128)(2,1)}, u32[]{:S(2)}, u32[]{:S(2)}) collective-permute-start(bf16[8,64,128]{2,1,0:T(8,128)(2,1)} %get-tuple-element.32), channel_id=1, source_target_pairs={{0,32},{1,33},{2,34},{3,35},{4,36},{5,37},{6,38},{7,39},{8,40},{9,... | collective-permute-start | bytes 393224 | tf_op jit(solution)/shard_map/ppermute | solution.py:128
  47.6 0.9 %copy-done.5 = f32[8,64,128]{2,1,0:T(8,128)S(1)} copy-done((f32[8,64,128]{2,1,0:T(8,128)S(1)}, f32[8,64,128]{2,1,0:T(8,128)}, u32[]{:S(2)}) %copy-start.5) | copy-done | bytes 262168
  48.5 0.8 %copy-done.6 = bf16[128,128]{1,0:T(8,128)(2,1)S(1)} copy-done((bf16[128,128]{1,0:T(8,128)(2,1)S(1)}, bf16[128,128]{1,0:T(8,128)(2,1)}, u32[]{:S(2)}) %copy-start.6) | copy-done | bytes 32792
  49.3 0.3 base.1.base_ref
  49.6 4.1 %collective-permute-done.3.tail_ref = bf16[24,64,128]{2,1,0:T(8,128)(2,1)S(1)} collective-permute-done((bf16[24,64,128]{2,1,0:T(8,128)(2,1)}, bf16[24,64,128]{2,1,0:T(8,128)(2,1)S(1)}, u32[]{:S(2)}, u32[]{:S(2)}) %collective-permute-start.3) | collective-permute-done | bytes 393248 | tf_op jit(solution)/shard_map/ppermute | solution.py:128
  53.7 1.2 %final.2 = (bf16[32,64,128]{2,1,0:T(8,128)(2,1)}, f32[32,64,128]{2,1,0:T(8,128)}) custom-call(bf16[32,64,128]{2,1,0:T(8,128)(2,1)S(1)} %copy-done.1, f32[32,64,128]{2,1,0:T(8,128)S(1)} %base.1.base_ref, bf16[24,64,128]{2,1,0:T(8,128)(2,1)S(1)} %collective-permute-done.3.tail_ref, bf16[32,128,128]{2,1,0:T(8,128)(2,1)S(1)} %copy-done.2), custom_call_target="tpu_custom_call" | custom-call | tf_op jit(solution)/shard_map/final/pallas_call | solution.py:204
  54.9 0.7 %collective-permute-done.2.tail_ref = bf16[8,64,128]{2,1,0:T(8,128)(2,1)} collective-permute-done((bf16[8,64,128]{2,1,0:T(8,128)(2,1)}, bf16[8,64,128]{2,1,0:T(8,128)(2,1)}, u32[]{:S(2)}, u32[]{:S(2)}) %collective-permute-start.2) | collective-permute-done | bytes 131104 | tf_op jit(solution)/shard_map/ppermute | solution.py:128
  55.6 1.8 %final.3 = (bf16[32,64,128]{2,1,0:T(8,128)(2,1)}, f32[32,64,128]{2,1,0:T(8,128)}) custom-call(bf16[32,64,128]{2,1,0:T(8,128)(2,1)S(1)} %copy-done.1, f32[32,64,128]{2,1,0:T(8,128)S(1)} %base.1.base_ref, bf16[8,64,128]{2,1,0:T(8,128)(2,1)} %collective-permute-done.2.tail_ref, ...), custom_call_target="tpu_custom_call", output_to_operand_aliasing={{0}: (4, {}), {1}: (5, {})} | custom-call | tf_op jit(solution)/shard_map/final/pallas_call | solution.py:204
  (17 shorter events, 0.1 us)
Async XLA Ops:
  0.6 29.2 %collective-permute-start.1 = (bf16[32,64,128]{2,1,0:T(8,128)(2,1)}, bf16[32,64,128]{2,1,0:T(8,128)(2,1)S(1)}, u32[]{:S(2)}, u32[]{:S(2)}) collective-permute-start(bf16[32,64,128]{2,1,0:T(8,128)(2,1)} %cur_ref.5), channel_id=1, source_target_pairs={{0,31},{1,2},{2,1},{3,4},{4,3},{5,6},{6,5},{7,8},{8,7},{9,10},{10,... | collective-permute-start | bytes 1572872 | tf_op jit(solution)/shard_map/ppermute | solution.py:128
  13.9 15.9 %collective-permute-start = (bf16[32,64,128]{2,1,0:T(8,128)(2,1)}, bf16[32,64,128]{2,1,0:T(8,128)(2,1)S(1)}, u32[]{:S(2)}, u32[]{:S(2)}) collective-permute-start(bf16[32,64,128]{2,1,0:T(8,128)(2,1)} %cur_ref.5), channel_id=1, source_target_pairs={{0,1},{1,0},{2,3},{3,2},{4,5},{5,4},{6,7},{7,6},{8,9},{9,8},{10,11... | collective-permute-start | bytes 1572872 | tf_op jit(solution)/shard_map/ppermute | solution.py:128
  15.8 1.0 %copy-start = (bf16[32,64,128]{2,1,0:T(8,128)(2,1)S(1)}, bf16[32,64,128]{2,1,0:T(8,128)(2,1)}, u32[]{:S(2)}) copy-start(bf16[32,64,128]{2,1,0:T(8,128)(2,1)} %cur_ref.5) | copy-start | bytes 1572868
  16.9 0.8 %copy-start.7 = (bf16[128,128]{1,0:T(8,128)(2,1)S(1)}, bf16[128,128]{1,0:T(8,128)(2,1)}, u32[]{:S(2)}) copy-start(bf16[128,128]{1,0:T(8,128)(2,1)} %map_ref.1) | copy-start | bytes 98308
  17.6 12.2 %copy-start.1 = (bf16[32,64,128]{2,1,0:T(8,128)(2,1)S(1)}, bf16[32,64,128]{2,1,0:T(8,128)(2,1)}, u32[]{:S(2)}) copy-start(bf16[32,64,128]{2,1,0:T(8,128)(2,1)} %cur_ref.5) | copy-start | bytes 1572868
  19.8 27.8 %all-to-all-start = ((f32[16,32,128]{2,1,0:T(8,128)}), f32[16,32,128]{2,1,0:T(8,128)S(1)}, u32[]{:S(2)}, u32[]{:S(2)}) async-start(f32[16,32,128]{2,1,0:T(8,128)} %get-tuple-element.25), calls=%async_computation | async-start | bytes 524288 | tf_op jit(solution)/shard_map/all_to_all | solution.py:157
  29.0 1.2 %copy-start.8 = (bf16[30,128,128]{2,1,0:T(8,128)(2,1)S(1)}, bf16[30,128,128]{2,1,0:T(8,128)(2,1)}, u32[]{:S(2)}) copy-start(bf16[30,128,128]{2,1,0:T(8,128)(2,1)} %coup_ref.3) | copy-start | bytes 2949124
  36.9 16.8 %collective-permute-start.3 = (bf16[24,64,128]{2,1,0:T(8,128)(2,1)}, bf16[24,64,128]{2,1,0:T(8,128)(2,1)S(1)}, u32[]{:S(2)}, u32[]{:S(2)}) collective-permute-start(bf16[24,64,128]{2,1,0:T(8,128)(2,1)} %get-tuple-element.33), channel_id=1, source_target_pairs={{0,32},{1,33},{2,34},{3,35},{4,36},{5,37},{6,38},{7,39},{8,40},{9,... | collective-permute-start | bytes 1179656 | tf_op jit(solution)/shard_map/ppermute | solution.py:128
  40.3 7.3 %copy-start.3 = (bf16[32,64,128]{2,1,0:T(8,128)(2,1)S(1)}, bf16[32,64,128]{2,1,0:T(8,128)(2,1)}, u32[]{:S(2)}) copy-start(bf16[32,64,128]{2,1,0:T(8,128)(2,1)} %exc_ref.1) | copy-start | bytes 1572868
  43.5 0.7 %copy-start.4 = (f32[8,64,128]{2,1,0:T(8,128)}, f32[8,64,128]{2,1,0:T(8,128)S(1)}, u32[]{:S(2)}) copy-start(f32[8,64,128]{2,1,0:T(8,128)S(1)} %get-tuple-element.29.high_ref) | copy-start | bytes 786436
  44.2 11.4 %collective-permute-start.2 = (bf16[8,64,128]{2,1,0:T(8,128)(2,1)}, bf16[8,64,128]{2,1,0:T(8,128)(2,1)}, u32[]{:S(2)}, u32[]{:S(2)}) collective-permute-start(bf16[8,64,128]{2,1,0:T(8,128)(2,1)} %get-tuple-element.32), channel_id=1, source_target_pairs={{0,32},{1,33},{2,34},{3,35},{4,36},{5,37},{6,38},{7,39},{8,40},{9,... | collective-permute-start | bytes 393224 | tf_op jit(solution)/shard_map/ppermute | solution.py:128
  47.6 1.0 %copy-start.5 = (f32[8,64,128]{2,1,0:T(8,128)S(1)}, f32[8,64,128]{2,1,0:T(8,128)}, u32[]{:S(2)}) copy-start(f32[8,64,128]{2,1,0:T(8,128)} %copy-done.4) | copy-start | bytes 786436
  48.5 0.8 %copy-start.6 = (bf16[128,128]{1,0:T(8,128)(2,1)S(1)}, bf16[128,128]{1,0:T(8,128)(2,1)}, u32[]{:S(2)}) copy-start(bf16[128,128]{1,0:T(8,128)(2,1)} %pot_ref.1) | copy-start | bytes 98308
  49.3 4.4 %copy-start.2 = (bf16[32,128,128]{2,1,0:T(8,128)(2,1)S(1)}, bf16[32,128,128]{2,1,0:T(8,128)(2,1)}, u32[]{:S(2)}) copy-start(bf16[32,128,128]{2,1,0:T(8,128)(2,1)} %inv_ref.3) | copy-start | bytes 3145732

commit v10 on v7

--- a/solution.py
+++ b/solution.py
@@ -44,13 +44,24 @@
             totals_ref[t, pl.ds(first, group)] = totals
 
 
-def layout_kernel(lag_ref, own_ref, inner_ref, outer_ref, field_ref, toep_ref):
+def layout_kernel(
+    me_ref, near_ref, lag_ref, own_ref, inner_ref, outer_ref, ids_ref, field_ref, toep_ref,
+):
     per_dev, steps, unknowns = own_ref.shape
-    slots = lag_ref.shape[0]
+    slots, lags = lag_ref.shape
+    wide = 2 * steps
+    source = lax.broadcasted_iota(jnp.int32, (lags, wide), 0)
+    target = lax.broadcasted_iota(jnp.int32, (lags, wide), 1)
+    flip = ((source + target) % wide == 0).astype(F32).astype(BF16)
+    lag_rows = dot(lag_ref[...], flip)
+    owner = near_ref[...] // per_dev
+    part = jnp.where(owner == me_ref[0], 0, jnp.where(owner == me_ref[0] ^ 1, 1, 2))
+    inside = part * per_dev + near_ref[...] % per_dev
+    ids_ref[...] = jnp.where(near_ref[...] >= 0, inside, 3 * per_dev)
     lane = lax.broadcasted_iota(jnp.int32, (2 * steps, 2 * steps), 1)
     for p in range(slots // 2):
-        even = jnp.broadcast_to(lag_ref[2 * p : 2 * p + 1, :], lane.shape)
-        odd = jnp.broadcast_to(lag_ref[2 * p + 1 : 2 * p + 2, :], lane.shape)
+        even = jnp.broadcast_to(lag_rows[2 * p : 2 * p + 1, :], lane.shape)
+        odd = jnp.broadcast_to(lag_rows[2 * p + 1 : 2 * p + 2, :], lane.shape)
         even = pltpu.roll(even, 0, 1, stride=1, stride_axis=0)
         odd = pltpu.roll(odd, steps, 1, stride=1, stride_axis=0)
         both = jnp.where(lane < steps, even, odd)
@@ -132,8 +143,6 @@
     shape3 = (per_dev, steps, unknowns)
     sds = jax.ShapeDtypeStruct
     params = lambda mib: pltpu.CompilerParams(vmem_limit_bytes=mib * MIB)
-    lag_rows = jnp.pad(lag_profile.astype(F32), ((0, 0), (0, 2 * steps - lags)))
-    lag_rows = jnp.roll(lag_rows[:, ::-1], 1, axis=1)
     running, totals = pl.pallas_call(
         prep_kernel,
         name="prep",
@@ -146,23 +155,19 @@
         compiler_params=params(16),
     )(currents, charge_map)
 
-    owner = neighbours // per_dev
-    part = jnp.where(owner == me, 0, jnp.where(owner == me ^ 1, 1, 2))
-    ids = jnp.where(neighbours >= 0, part * per_dev + neighbours % per_dev, 3 * per_dev)
-
-    lag_rows, running = lax.optimization_barrier((lag_rows, running))
     pieces = lax.all_to_all(totals, "tm", 0, 0)
-    field, toeplitz = pl.pallas_call(
+    ids, field, toeplitz = pl.pallas_call(
         layout_kernel,
         name="layout",
         out_shape=(
+            sds(neighbours.shape, jnp.int32),
             sds((3 * per_dev + 1, steps, unknowns), BF16),
             sds((2 * steps, slots * steps), BF16),
         ),
-        in_specs=[whole()] * 4,
-        out_specs=(whole(), whole()),
+        in_specs=[whole(pltpu.SMEM)] + [whole()] * 5,
+        out_specs=(whole(),) * 3,
         compiler_params=params(16),
-    )(lag_rows, currents, inner, outer)
+    )(me.astype(jnp.int32).reshape(1), neighbours, lag_profile, currents, inner, outer)
     part = per_dev // 2
     heads, tails = [], []
     for h in range(2):

time: 57.6 us -> 57.1 us (level)
  local copies, waits for them, and re-layouts: 3.46 us -> 5.34 us
  other arithmetic: 2.65 us -> 1.05 us
  Pallas kernels: 15.3 us -> 13.8 us
  waiting for transfers between devices: 5.15 us -> 5.81 us
    unnamed x14 -> x22, local copies, waits for them, and re-layouts: 2.61 us -> 5.34 us
    pallas_call x2, Pallas kernels: 2.96 us -> 2.01 us  [on_device(): pl.pallas_call(final_kernel, name='final', grid=(1,), out_shape=(sds(shap...]
    slice x3 -> x0, local copies, waits for them, and re-layouts: 0.85 us -> none  [on_device(): lag_rows = jnp.roll(lag_rows[:, ::-1], 1, axis=1)]
    select_n x1 -> x0, other arithmetic: 0.83 us -> none  [on_device(): jnp.where(neighbours >= 0, part * per_dev + neighbours % per_dev, 3 * per...]
    pallas_call x2, Pallas kernels: 9.58 us -> 8.86 us  [on_device(): pl.pallas_call(functools.partial(near_kernel, h * part), name='near', out...]
    convert_element_type x1 -> x0, other arithmetic: 0.7 us -> none  [on_device(): lag_rows = jnp.pad(lag_profile.astype(F32), ((0, 0), (0, 2 * steps - lags)))]
    ppermute x4, waiting for transfers between devices: 5.15 us -> 5.81 us  [send(): return lax.ppermute(x, ('tm', 'clus'), pairs)]
  transfers between devices with their start and end apart: 5 -> 5, of which waited for: 2 -> 1; matrix products, arithmetic and copies ran while one was open for 6% -> 2% of each run, Pallas kernels for 25% -> 23%
where the time goes in v10:
time: 57.1 us; the launch traced here: 56.5 us
  starting transfers between devices  29.6 us (52%)
  Pallas kernels  13.8 us (24%)
  waiting for transfers between devices  5.81 us (10%)
  local copies, waits for them, and re-layouts  5.34 us (9%)
  other arithmetic  1.05 us (2%)
  between operations  0.82 us (1%)
    ppermute x4, starting transfers between devices, send(): return lax.ppermute(x, ('tm', 'clus'), pairs)  22 us
    pallas_call x2, Pallas kernels, on_device(): pl.pallas_call(functools.partial(near_kernel, h * part), name='near', out...  8.86 us
    all_to_all x1, starting transfers between devices, on_device(): pieces = lax.all_to_all(totals, 'tm', 0, 0)  7.58 us
    ppermute x4, waiting for transfers between devices, send(): return lax.ppermute(x, ('tm', 'clus'), pairs)  5.81 us
    unnamed x22, local copies, waits for them, and re-layouts  5.34 us
    pallas_call x1, Pallas kernels, on_device(): pl.pallas_call(prep_kernel, name='prep', out_shape=(sds(shape3, F32), sds...  2.16 us
    pallas_call x2, Pallas kernels, on_device(): pl.pallas_call(final_kernel, name='final', grid=(1,), out_shape=(sds(shap...  2.01 us
  transfers between devices with their start and end apart: 5, of which 1 were waited for; matrix products, arithmetic and copies ran while one was open for 2% of the time, Pallas kernels for 23%

profile of v10, /device:TPU:2, one launch (start us, length us, event | category | flops | bytes accessed | tf_op | source)
XLA Modules:
  0.0 56.5 jit_solution(16363746360477678054)
XLA Ops:
  0.6 13.3 %collective-permute-start.1 = (bf16[32,64,128]{2,1,0:T(8,128)(2,1)}, bf16[32,64,128]{2,1,0:T(8,128)(2,1)S(1)}, u32[]{:S(2)}, u32[]{:S(2)}) collective-permute-start(bf16[32,64,128]{2,1,0:T(8,128)(2,1)} %cur_ref.5), channel_id=1, source_target_pairs={{0,31},{1,2},{2,1},{3,4},{4,3},{5,6},{6,5},{7,8},{8,7},{9,10},{10,... | collective-permute-start | bytes 1572872 | tf_op jit(solution)/shard_map/ppermute | solution.py:136
  13.9 1.9 %collective-permute-start = (bf16[32,64,128]{2,1,0:T(8,128)(2,1)}, bf16[32,64,128]{2,1,0:T(8,128)(2,1)S(1)}, u32[]{:S(2)}, u32[]{:S(2)}) collective-permute-start(bf16[32,64,128]{2,1,0:T(8,128)(2,1)} %cur_ref.5), channel_id=1, source_target_pairs={{0,1},{1,0},{2,3},{3,2},{4,5},{5,4},{6,7},{7,6},{8,9},{9,8},{10,11... | collective-permute-start | bytes 1572872 | tf_op jit(solution)/shard_map/ppermute | solution.py:136
  15.8 0.0 copy-start
  15.8 1.0 %copy-done = bf16[32,64,128]{2,1,0:T(8,128)(2,1)S(1)} copy-done((bf16[32,64,128]{2,1,0:T(8,128)(2,1)S(1)}, bf16[32,64,128]{2,1,0:T(8,128)(2,1)}, u32[]{:S(2)}) %copy-start) | copy-done | bytes 524312
  16.9 0.8 %copy-done.6 = bf16[128,128]{1,0:T(8,128)(2,1)S(1)} copy-done((bf16[128,128]{1,0:T(8,128)(2,1)S(1)}, bf16[128,128]{1,0:T(8,128)(2,1)}, u32[]{:S(2)}) %copy-start.6) | copy-done | bytes 32792
  17.6 2.2 %prep.1 = (f32[32,64,128]{2,1,0:T(8,128)S(1)}, f32[16,32,128]{2,1,0:T(8,128)}) custom-call(bf16[32,64,128]{2,1,0:T(8,128)(2,1)S(1)} %copy-done, bf16[128,128]{1,0:T(8,128)(2,1)S(1)} %copy-done.6), custom_call_target="tpu_custom_call" | custom-call | tf_op jit(solution)/shard_map/prep/pallas_call | solution.py:146
  19.8 7.6 %all-to-all-start = ((f32[16,32,128]{2,1,0:T(8,128)}), f32[16,32,128]{2,1,0:T(8,128)}, u32[]{:S(2)}, u32[]{:S(2)}) async-start(f32[16,32,128]{2,1,0:T(8,128)} %get-tuple-element.23), calls=%async_computation | async-start | bytes 524288 | tf_op jit(solution)/shard_map/all_to_all | solution.py:158
  27.4 1.0 %copy-done.1 = bf16[32,64,128]{2,1,0:T(8,128)(2,1)S(1)} copy-done((bf16[32,64,128]{2,1,0:T(8,128)(2,1)S(1)}, bf16[32,64,128]{2,1,0:T(8,128)(2,1)}, u32[]{:S(2)}) %copy-start.1) | copy-done | bytes 524312
  28.4 0.7 %copy-done.7 = s32[32,30]{1,0:T(8,128)S(1)} copy-done((s32[32,30]{1,0:T(8,128)S(1)}, s32[32,30]{1,0:T(8,128)}, u32[]{:S(2)}) %copy-start.7) | copy-done | bytes 3864
  29.1 0.7 %copy-done.8 = bf16[30,64]{1,0:T(8,128)(2,1)S(1)} copy-done((bf16[30,64]{1,0:T(8,128)(2,1)S(1)}, bf16[30,64]{1,0:T(8,128)(2,1)}, u32[]{:S(2)}) %copy-start.8) | copy-done | bytes 3864
  29.8 0.5 layout.1
  30.4 4.1 %near.2 = (f32[16,64,128]{2,1,0:T(8,128)S(1)}, bf16[16,64,128]{2,1,0:T(8,128)(2,1)S(1)}) custom-call(s32[32,30]{1,0:T(8,128)S(1)} %get-tuple-element.24.ids_ref, bf16[97,64,128]{2,1,0:T(8,128)(2,1)S(1)} %get-tuple-element.19.field, bf16[30,128,128]{2,1,0:T(8,128)(2,1)S(1)} %copy-done.9, bf16[128,1920]{1,0:T(8,128)(2,1)S(1)} %get-tuple-element.20.toep_ref), custom_call_target="tpu_custom_call" | custom-call | flops 2013265920 | bytes 4194304 | tf_op jit(solution)/shard_map/near/pallas_call | solution.py:174
  34.5 3.5 %collective-permute-start.3 = (bf16[16,64,128]{2,1,0:T(8,128)(2,1)S(1)}, bf16[16,64,128]{2,1,0:T(8,128)(2,1)S(1)}, u32[]{:S(2)}, u32[]{:S(2)}) collective-permute-start(bf16[16,64,128]{2,1,0:T(8,128)(2,1)S(1)} %get-tuple-element.31), channel_id=1, source_target_pairs={{0,32},{1,33},{2,34},{3,35},{4,36},{5,37},{6,38},{7,39},{8,40},{9,... | collective-permute-start | bytes 786440 | tf_op jit(solution)/shard_map/ppermute | solution.py:136
  38.0 4.8 %near.3 = (f32[16,64,128]{2,1,0:T(8,128)S(1)}, bf16[16,64,128]{2,1,0:T(8,128)(2,1)}) custom-call(s32[32,30]{1,0:T(8,128)S(1)} %get-tuple-element.24.ids_ref, bf16[97,64,128]{2,1,0:T(8,128)(2,1)S(1)} %get-tuple-element.19.field, bf16[30,128,128]{2,1,0:T(8,128)(2,1)S(1)} %copy-done.10, bf16[128,1920]{1,0:T(8,128)(2,1)S(1)} %get-tuple-element.20.toep_ref), custom_call_target="tpu_custom_call" | custom-call | flops 2013265920 | bytes 4194304 | tf_op jit(solution)/shard_map/near/pallas_call | solution.py:174
  42.8 3.4 %collective-permute-start.2 = (bf16[16,64,128]{2,1,0:T(8,128)(2,1)}, bf16[16,64,128]{2,1,0:T(8,128)(2,1)S(1)}, u32[]{:S(2)}, u32[]{:S(2)}) collective-permute-start(bf16[16,64,128]{2,1,0:T(8,128)(2,1)} %get-tuple-element.30), channel_id=1, source_target_pairs={{0,32},{1,33},{2,34},{3,35},{4,36},{5,37},{6,38},{7,39},{8,40},{9,... | collective-permute-start | bytes 786440 | tf_op jit(solution)/shard_map/ppermute | solution.py:136
  46.2 1.0 %select_reduce_fusion.before_ref = f32[32,128]{1,0:T(8,128)S(1)} fusion(f32[16,32,128]{2,1,0:T(8,128)} %all-to-all-done, pred[16]{0:T(512)(128)(4,1)S(1)} %iota_compare_fusion), kind=kLoop, calls=%fused_computation | loop fusion | flops 126976 | bytes 278544 | tf_op jit(solution)/shard_map/reduce_sum | solution.py:193
  47.2 0.0 copy-start.2
  47.3 0.0 copy-start.3
  47.3 0.3 base.1.base_ref
  47.6 0.7 %copy-done.2 = bf16[32,64,128]{2,1,0:T(8,128)(2,1)S(1)} copy-done((bf16[32,64,128]{2,1,0:T(8,128)(2,1)S(1)}, bf16[32,64,128]{2,1,0:T(8,128)(2,1)}, u32[]{:S(2)}) %copy-start.2) | copy-done | bytes 524312
  48.3 0.3 copy-done.3
  48.6 1.0 %final.2 = (bf16[32,64,128]{2,1,0:T(8,128)(2,1)}, f32[32,64,128]{2,1,0:T(8,128)}) custom-call(bf16[32,64,128]{2,1,0:T(8,128)(2,1)S(1)} %copy-done.2, f32[32,64,128]{2,1,0:T(8,128)S(1)} %base.1.base_ref, bf16[16,64,128]{2,1,0:T(8,128)(2,1)S(1)} %collective-permute-done.3.tail_ref, bf16[32,128,128]{2,1,0:T(8,128)(2,1)S(1)} %copy-done.3), custom_call_target="tpu_custom_call" | custom-call | tf_op jit(solution)/shard_map/final/pallas_call | solution.py:206
  49.7 5.8 %collective-permute-done.2.tail_ref = bf16[16,64,128]{2,1,0:T(8,128)(2,1)S(1)} collective-permute-done((bf16[16,64,128]{2,1,0:T(8,128)(2,1)}, bf16[16,64,128]{2,1,0:T(8,128)(2,1)S(1)}, u32[]{:S(2)}, u32[]{:S(2)}) %collective-permute-start.2) | collective-permute-done | bytes 262176 | tf_op jit(solution)/shard_map/ppermute | solution.py:136
  55.5 1.0 %final.3 = (bf16[32,64,128]{2,1,0:T(8,128)(2,1)}, f32[32,64,128]{2,1,0:T(8,128)}) custom-call(bf16[32,64,128]{2,1,0:T(8,128)(2,1)S(1)} %copy-done.2, f32[32,64,128]{2,1,0:T(8,128)S(1)} %base.1.base_ref, bf16[16,64,128]{2,1,0:T(8,128)(2,1)S(1)} %collective-permute-done.2.tail_ref, ...), custom_call_target="tpu_custom_call", output_to_operand_aliasing={{0}: (4, {}), {1}: (5, {})} | custom-call | tf_op jit(solution)/shard_map/final/pallas_call | solution.py:206
  (17 shorter events, 0.0 us)
Async XLA Ops:
  0.6 26.7 %collective-permute-start.1 = (bf16[32,64,128]{2,1,0:T(8,128)(2,1)}, bf16[32,64,128]{2,1,0:T(8,128)(2,1)S(1)}, u32[]{:S(2)}, u32[]{:S(2)}) collective-permute-start(bf16[32,64,128]{2,1,0:T(8,128)(2,1)} %cur_ref.5), channel_id=1, source_target_pairs={{0,31},{1,2},{2,1},{3,4},{4,3},{5,6},{6,5},{7,8},{8,7},{9,10},{10,... | collective-permute-start | bytes 1572872 | tf_op jit(solution)/shard_map/ppermute | solution.py:136
  13.9 13.5 %collective-permute-start = (bf16[32,64,128]{2,1,0:T(8,128)(2,1)}, bf16[32,64,128]{2,1,0:T(8,128)(2,1)S(1)}, u32[]{:S(2)}, u32[]{:S(2)}) collective-permute-start(bf16[32,64,128]{2,1,0:T(8,128)(2,1)} %cur_ref.5), channel_id=1, source_target_pairs={{0,1},{1,0},{2,3},{3,2},{4,5},{5,4},{6,7},{7,6},{8,9},{9,8},{10,11... | collective-permute-start | bytes 1572872 | tf_op jit(solution)/shard_map/ppermute | solution.py:136
  15.8 1.0 %copy-start = (bf16[32,64,128]{2,1,0:T(8,128)(2,1)S(1)}, bf16[32,64,128]{2,1,0:T(8,128)(2,1)}, u32[]{:S(2)}) copy-start(bf16[32,64,128]{2,1,0:T(8,128)(2,1)} %cur_ref.5) | copy-start | bytes 1572868
  16.9 0.8 %copy-start.6 = (bf16[128,128]{1,0:T(8,128)(2,1)S(1)}, bf16[128,128]{1,0:T(8,128)(2,1)}, u32[]{:S(2)}) copy-start(bf16[128,128]{1,0:T(8,128)(2,1)} %map_ref.1) | copy-start | bytes 98308
  17.6 12.7 %copy-start.9 = (bf16[30,128,128]{2,1,0:T(8,128)(2,1)S(1)}, bf16[30,128,128]{2,1,0:T(8,128)(2,1)}, u32[]{:S(2)}) copy-start(bf16[30,128,128]{2,1,0:T(8,128)(2,1)} %coup_ref.3) | copy-start | bytes 2949124
  19.8 26.4 %all-to-all-start = ((f32[16,32,128]{2,1,0:T(8,128)}), f32[16,32,128]{2,1,0:T(8,128)}, u32[]{:S(2)}, u32[]{:S(2)}) async-start(f32[16,32,128]{2,1,0:T(8,128)} %get-tuple-element.23), calls=%async_computation | async-start | bytes 524288 | tf_op jit(solution)/shard_map/all_to_all | solution.py:158
  27.4 1.0 %copy-start.1 = (bf16[32,64,128]{2,1,0:T(8,128)(2,1)S(1)}, bf16[32,64,128]{2,1,0:T(8,128)(2,1)}, u32[]{:S(2)}) copy-start(bf16[32,64,128]{2,1,0:T(8,128)(2,1)} %cur_ref.5) | copy-start | bytes 1572868
  28.4 0.7 %copy-start.7 = (s32[32,30]{1,0:T(8,128)S(1)}, s32[32,30]{1,0:T(8,128)}, u32[]{:S(2)}) copy-start(s32[32,30]{1,0:T(8,128)} %near_ref.1) | copy-start | bytes 11524
  29.1 0.7 %copy-start.8 = (bf16[30,64]{1,0:T(8,128)(2,1)S(1)}, bf16[30,64]{1,0:T(8,128)(2,1)}, u32[]{:S(2)}) copy-start(bf16[30,64]{1,0:T(8,128)(2,1)} %lag_ref.1) | copy-start | bytes 11524
  30.4 7.6 %copy-start.10 = (bf16[30,128,128]{2,1,0:T(8,128)(2,1)S(1)}, bf16[30,128,128]{2,1,0:T(8,128)(2,1)}, u32[]{:S(2)}) copy-start(bf16[30,128,128]{2,1,0:T(8,128)(2,1)} %coup_ref.3) | copy-start | bytes 2949124
  34.5 12.8 %copy-start.4 = (bf16[32,64,128]{2,1,0:T(8,128)(2,1)S(1)}, bf16[32,64,128]{2,1,0:T(8,128)(2,1)}, u32[]{:S(2)}) copy-start(bf16[32,64,128]{2,1,0:T(8,128)(2,1)} %exc_ref.1) | copy-start | bytes 1572868
  34.5 12.8 %copy-start.5 = (bf16[128,128]{1,0:T(8,128)(2,1)S(1)}, bf16[128,128]{1,0:T(8,128)(2,1)}, u32[]{:S(2)}) copy-start(bf16[128,128]{1,0:T(8,128)(2,1)} %pot_ref.1) | copy-start | bytes 98308
  34.5 13.1 %collective-permute-start.3 = (bf16[16,64,128]{2,1,0:T(8,128)(2,1)S(1)}, bf16[16,64,128]{2,1,0:T(8,128)(2,1)S(1)}, u32[]{:S(2)}, u32[]{:S(2)}) collective-permute-start(bf16[16,64,128]{2,1,0:T(8,128)(2,1)S(1)} %get-tuple-element.31), channel_id=1, source_target_pairs={{0,32},{1,33},{2,34},{3,35},{4,36},{5,37},{6,38},{7,39},{8,40},{9,... | collective-permute-start | bytes 786440 | tf_op jit(solution)/shard_map/ppermute | solution.py:136
  42.8 12.7 %collective-permute-start.2 = (bf16[16,64,128]{2,1,0:T(8,128)(2,1)}, bf16[16,64,128]{2,1,0:T(8,128)(2,1)S(1)}, u32[]{:S(2)}, u32[]{:S(2)}) collective-permute-start(bf16[16,64,128]{2,1,0:T(8,128)(2,1)} %get-tuple-element.30), channel_id=1, source_target_pairs={{0,32},{1,33},{2,34},{3,35},{4,36},{5,37},{6,38},{7,39},{8,40},{9,... | collective-permute-start | bytes 786440 | tf_op jit(solution)/shard_map/ppermute | solution.py:136
  47.2 1.0 %copy-start.2 = (bf16[32,64,128]{2,1,0:T(8,128)(2,1)S(1)}, bf16[32,64,128]{2,1,0:T(8,128)(2,1)}, u32[]{:S(2)}) copy-start(bf16[32,64,128]{2,1,0:T(8,128)(2,1)} %cur_ref.5) | copy-start | bytes 1572868
  47.3 1.4 %copy-start.3 = (bf16[32,128,128]{2,1,0:T(8,128)(2,1)S(1)}, bf16[32,128,128]{2,1,0:T(8,128)(2,1)}, u32[]{:S(2)}) copy-start(bf16[32,128,128]{2,1,0:T(8,128)(2,1)} %inv_ref.3) | copy-start | bytes 3145732
